TPU v7x, 32 devices: a whole 2x2x4 slice. The times are simulated.
32 devices in a mesh: groups: 1, dp: 32 (over z, y, x, core).
Axes of the slice: x: 2, y: 2, z: 4, core: 2. Of those that a mesh axis runs over, the one named last changes fastest.
Arguments:
- hidden_in: bfloat16 [256, 2, 1024], P(('groups', 'dp')), may hold values from -6 to 6
- query_in: bfloat16 [256, 2, 1024], P(('groups', 'dp')), may hold values from -6 to 6
- key_in: bfloat16 [256, 2, 1024], P(('groups', 'dp')), may hold values from -6 to 6
- value_in: bfloat16 [256, 2, 2048], P(('groups', 'dp')), may hold values from -6 to 6
- gate_in: bfloat16 [256, 2, 2048], P(('groups', 'dp')), may hold values from -6 to 6
- decay_in: bfloat16 [256, 2, 16], P(('groups', 'dp')), may hold values from -4 to 4
- beta_in: bfloat16 [256, 2, 16], P(('groups', 'dp')), may hold values from -5 to 5
- decay_log: float32 [16], replicated, may hold values from -3 to 2
- step_bias: float32 [16], replicated, may hold values from -1 to 1
- norm_gain: float32 [128], replicated, may hold values from 0.5 to 1.5
- state_in: bfloat16 [256, 16, 128, 128], P(('groups', 'dp')), may hold values from -3 to 3
- out_proj: bfloat16 [2048, 1024], replicated, may hold values from -0.125 to 0.125
- post_gain: float32 [1024], replicated, may hold values from 0.5 to 1.5
- router_weight: bfloat16 [1024, 32], replicated, may hold values from -0.1875 to 0.1875
- expert_gate_up: bfloat16 [32, 1024, 512], P('dp'), may hold values from -0.1875 to 0.1875
- expert_down: bfloat16 [32, 256, 1024], P('dp'), may hold values from -0.375 to 0.375
- expert_ids: int32 [256, 2, 10], P(('groups', 'dp')), may hold values from 0 to 31, all different within a row; in each aligned block of 16 rows (0 to 15, 16 to 31, ..., all dimensions but the last counted through in order) at most 8 rows name the same one
Outputs:
- layer_out: bfloat16 [256, 2, 1024], P(('groups', 'dp'))
Inputs may be any that keep to these rules, and one draw needn't show every extreme that they name: `expert_ids`: each row and position names 10 different experts. Taking rows and positions in order, in each aligned block of 16 of them no expert is named more than 8 times, a bound that some block reaches.
All inputs are finite; a program needn't handle non-finite values.
Results may differ from a plain program's by a relative error of at most 0.0095.
Values may be sent and summed in bfloat16 or wider, within the bound.
No kernel may reach another device: no remote copies, remote signals or barrier semaphores. Data moves between devices by JAX's collectives and lax.ppermute only.
A program may use at most 64 MiB of HBM per device.

v0:
```python
import jax
import jax.numpy as jnp
from jax import lax
from jax.sharding import PartitionSpec as P

eps_norm = 1e-06


def delta_block(
    query_in,
    key_in,
    value_in,
    gate_in,
    decay_in,
    beta_in,
    state_in,
    decay_log,
    step_bias,
    norm_gain,
):
    row_count = query_in.shape[0]
    value_heads = state_in.shape[1]
    key_size = state_in.shape[2]
    value_size = state_in.shape[3]
    key_heads = query_in.shape[2] // key_size
    repeat_count = value_heads // key_heads
    query_all = query_in.astype(jnp.float32).reshape(row_count, 2, key_heads, key_size)
    query_all = (
        query_all
        * lax.rsqrt(jnp.sum(query_all * query_all, axis=-1, keepdims=True) + eps_norm)
        * key_size ** (-0.5)
    )
    key_all = key_in.astype(jnp.float32).reshape(row_count, 2, key_heads, key_size)
    key_all = key_all * lax.rsqrt(jnp.sum(key_all * key_all, axis=-1, keepdims=True) + eps_norm)
    query_all = jnp.repeat(query_all, repeat_count, axis=2)
    key_all = jnp.repeat(key_all, repeat_count, axis=2)
    value_all = value_in.astype(jnp.float32).reshape(row_count, 2, value_heads, value_size)
    gate_all = gate_in.astype(jnp.float32).reshape(row_count, 2, value_heads, value_size)
    decay_rate = jnp.exp(
        -jnp.exp(decay_log) * jax.nn.softplus(decay_in.astype(jnp.float32) + step_bias)
    )
    beta_gate = jax.nn.sigmoid(beta_in.astype(jnp.float32))
    memory = state_in.astype(jnp.float32)
    outputs = []
    for position in range(2):
        keys_now = key_all[:, position]
        memory = memory * decay_rate[:, position, :, None, None]
        recalled = jnp.sum(memory * keys_now[..., None], axis=2)
        update = beta_gate[:, position, :, None] * (value_all[:, position] - recalled)
        memory = memory + keys_now[..., None] * update[:, :, None, :]
        outputs.append(jnp.sum(memory * query_all[:, position][..., None], axis=2))
    core_out = jnp.stack(outputs, axis=1)
    scaled = (
        core_out
        * lax.rsqrt(jnp.mean(core_out * core_out, axis=-1, keepdims=True) + eps_norm)
        * norm_gain
        * jax.nn.silu(gate_all)
    )
    return scaled.reshape(row_count, 2, value_heads * value_size).astype(jnp.bfloat16)


def gate_weights(logits_all, picked_ids):
    expert_index = jnp.arange(logits_all.shape[1], dtype=jnp.int32)
    chosen = jnp.sum(
        jnp.where(picked_ids[:, :, None] == expert_index, logits_all[:, None, :], 0.0), axis=-1
    )
    raised = jnp.exp(chosen)
    return raised / jnp.sum(raised, axis=-1, keepdims=True)


def slot_numbers(picked_flat):
    pick_total = picked_flat.shape[0]
    pick_order = jnp.arange(pick_total, dtype=jnp.int32)
    earlier_same = (picked_flat[:, None] == picked_flat[None, :]) & (
        pick_order[:, None] > pick_order[None, :]
    )
    return jnp.sum(earlier_same.astype(jnp.int32), axis=1)


def run_experts(blocks, expert_gate_up, expert_down):
    hidden_units = expert_down.shape[1]
    both_parts = jnp.einsum(
        "secd,edf->secf", blocks, expert_gate_up, preferred_element_type=jnp.float32
    )
    activated = (
        jax.nn.silu(both_parts[..., :hidden_units]) * both_parts[..., hidden_units:]
    ).astype(jnp.bfloat16)
    produced = jnp.einsum(
        "secf,efd->secd", activated, expert_down, preferred_element_type=jnp.float32
    ).astype(jnp.bfloat16)
    return lax.all_to_all(produced, "dp", split_axis=0, concat_axis=0, tiled=True)


def shards(
    hidden_in,
    query_in,
    key_in,
    value_in,
    gate_in,
    decay_in,
    beta_in,
    decay_log,
    step_bias,
    norm_gain,
    state_in,
    out_proj,
    post_gain,
    router_weight,
    expert_gate_up,
    expert_down,
    expert_ids,
):
    device_count = lax.axis_size("dp")
    local_experts = expert_gate_up.shape[0]
    expert_total = local_experts * device_count
    row_count = hidden_in.shape[0]
    model_width = hidden_in.shape[2]
    pick_count = expert_ids.shape[2]
    token_count = row_count * 2
    capacity = min(
        2 * row_count, max(2, (3 * row_count * pick_count + expert_total - 1) // expert_total)
    )
    mixer_out = delta_block(
        query_in,
        key_in,
        value_in,
        gate_in,
        decay_in,
        beta_in,
        state_in,
        decay_log,
        step_bias,
        norm_gain,
    )
    mixer_out = mixer_out.reshape(token_count, -1)
    residual = hidden_in.astype(jnp.float32).reshape(token_count, model_width)
    middle = (residual + jnp.dot(mixer_out, out_proj, preferred_element_type=jnp.float32)).astype(
        jnp.bfloat16
    )
    middle_wide = middle.astype(jnp.float32)
    routed = (
        middle_wide
        * lax.rsqrt(jnp.mean(middle_wide * middle_wide, axis=-1, keepdims=True) + eps_norm)
        * post_gain
    ).astype(jnp.bfloat16)
    logits_all = jnp.dot(routed, router_weight, preferred_element_type=jnp.float32)
    picked_ids = expert_ids.reshape(token_count, pick_count)
    gate_share = gate_weights(logits_all, picked_ids)
    slot_number = slot_numbers(picked_ids.reshape(-1)).reshape(token_count, pick_count)
    target = picked_ids * capacity + slot_number
    all_picks = lax.all_gather(picked_ids, "dp", axis=0, tiled=True)
    all_rows = lax.all_gather(routed, "dp", axis=0, tiled=True)
    source_picks = all_picks.reshape(device_count, token_count * pick_count)
    source_slots = jax.vmap(slot_numbers)(source_picks)
    local_pick = source_picks - lax.axis_index("dp") * local_experts
    owned_here = (local_pick >= 0) & (local_pick < local_experts)
    source_index = jnp.arange(device_count, dtype=jnp.int32)[:, None]
    slot_total = device_count * local_experts * capacity
    slot_place = jnp.where(
        owned_here,
        (source_index * local_experts + local_pick) * capacity + source_slots,
        slot_total,
    )
    row_number = (
        source_index * token_count
        + jnp.arange(token_count * pick_count, dtype=jnp.int32)[None, :] // pick_count
    )
    slot_source = jnp.full((slot_total,), device_count * token_count, jnp.int32)
    slot_source = slot_source.at[slot_place.reshape(-1)].set(row_number.reshape(-1), mode="drop")
    blocks = jnp.take(all_rows, slot_source, axis=0, mode="fill", fill_value=0)
    blocks = blocks.reshape(device_count, local_experts, capacity, model_width)
    returned = run_experts(blocks, expert_gate_up, expert_down)
    flat_results = returned.reshape(expert_total * capacity, model_width)
    picked = jnp.take(flat_results, target.reshape(-1), axis=0).reshape(
        token_count, pick_count, model_width
    )
    mixture = jnp.sum(gate_share[:, :, None] * picked.astype(jnp.float32), axis=1)
    return (middle_wide + mixture).astype(jnp.bfloat16).reshape(row_count, 2, model_width)


def solution(mesh):
    placed = (
        P(("groups", "dp"), None, None),
        P(("groups", "dp"), None, None),
        P(("groups", "dp"), None, None),
        P(("groups", "dp"), None, None),
        P(("groups", "dp"), None, None),
        P(("groups", "dp"), None, None),
        P(("groups", "dp"), None, None),
        P(),
        P(),
        P(),
        P(("groups", "dp"), None, None, None),
        P(),
        P(),
        P(),
        P("dp", None, None),
        P("dp", None, None),
        P(("groups", "dp"), None, None),
    )
    return jax.shard_map(
        shards,
        mesh=mesh,
        in_specs=placed,
        out_specs=P(("groups", "dp"), None, None),
        check_vma=False,
    )
```

profile of v0, /device:TPU:0, one launch (start us, length us, event | category | flops | bytes accessed | tf_op | source)
XLA Modules:
  0.0 138.5 jit_solution(1613642320734320544)
XLA Ops:
  6.5 0.7 exponential_negate_fusion
  7.3 0.7 fusion.24
  8.0 0.7 add_divide_fusion
  8.7 0.7 broadcast_bitcast_fusion
  9.4 0.8 reshape.358
  10.2 0.1 multiply_reduce_fusion.6
  10.3 0.1 multiply_multiply_fusion
  10.4 0.8 reshape.354
  11.2 0.1 multiply_reduce_fusion.7
  11.3 0.1 broadcast_multiply_fusion
  11.4 0.8 reshape.352
  12.2 0.9 reshape.356
  13.2 5.0 %multiply_reduce_fusion.3 = f32[8,16,128]{2,1,0:T(8,128)S(1)} fusion(bf16[8,16,128,128]{3,2,1,0:T(8,128)(2,1)} %param.27, f32[8,16,128]{2,1,0:T(8,128)S(1)} %get-tuple-element.17, f32[8,16]{1,0:T(8,128)S(1)} %get-tuple-element.14), kind=kLoop, calls=%fused_computation.7 | loop fusion | flops 8372224 | bytes 4325888 | tf_op jit(solution)/shard_map/reduce_sum | solution.py:48
  18.2 0.1 fusion.22
  18.3 5.8 %multiply_reduce_fusion.1 = f32[8,16,128]{2,1,0:T(8,128)S(1)} fusion(bf16[8,16,128,128]{3,2,1,0:T(8,128)(2,1)S(1)} %copy-done.1, f32[8,16,128]{2,1,0:T(8,128)S(1)} %get-tuple-element.18, f32[8,16]{1,0:T(8,128)S(1)} %get-tuple-element.13, f32[8,16,128]{2,1,0:T(8,128)S(1)} %fusion.22, f32[8,16,128]{2,1,0:T(8,128)S(1)} %get-tuple-element.17, ...), kind=kLoop, calls=%fused_computation.4 | loop fusion | flops 14663680 | bytes 4457472 | tf_op jit(solution)/shard_map/reduce_sum | solution.py:48
  24.1 0.1 fusion.20
  24.2 10.6 %multiply_reduce_fusion.2 = (f32[8,16,128]{2,1,0:T(8,128)S(1)}, f32[8,16,128]{2,1,0:T(8,128)S(1)}) fusion(bf16[8,16,128,128]{3,2,1,0:T(8,128)(2,1)S(1)} %copy-done.1, f32[8,16,128]{2,1,0:T(8,128)S(1)} %get-tuple-element.10, f32[8,16,128]{2,1,0:T(8,128)S(1)} %fusion.22, f32[8,16,128]{2,1,0:T(8,128)S(1)} %get-tuple-element.17, ...), kind=kLoop, calls=%fused_computation.5 | loop fusion | flops 23035904 | bytes 4719616 | tf_op jit(solution)/shard_map/reduce_sum | solution.py:51
  34.9 0.1 fusion.15
  35.0 0.1 mul.304
  35.2 0.3 fusion.18
  35.5 3.0 %multiply_reduce_fusion.5 = (f32[16]{0:T(128)S(1)}, f32[16,1024]{1,0:T(8,128)S(1)}) fusion(f32[16,1024]{1,0:T(8,128)S(1)} %reshape.352, bf16[16,2048]{1,0:T(8,128)(2,1)S(1)} %reshape.344, bf16[2048,1024]{1,0:T(8,128)(2,1)} %param.28), kind=kOutput, calls=%fused_computation.56 | convolution fusion | flops 67190768 | bytes 4390976 | tf_op jit(solution)/shard_map/dot_general | solution.py:137
  38.5 0.7 multiply_convert_fusion
  39.3 0.1 reshape.345
  39.4 0.1 broadcast_add_fusion
  39.5 0.1 reshape.379
  39.6 0.1 add.195
  39.7 44.0 %all_gather.6 = s32[512,10]{1,0:T(8,128)S(1)} all-gather(s32[16,10]{1,0:T(8,128)S(1)} %bitcast.87), channel_id=1, replica_groups=mesh['groups'=1,'dp'=32] {'dp'}, dimensions={0}, use_global_device_ids=true | all-gather | bytes 21120 | tf_op jit(solution)/shard_map/all_gather | solution.py:151
  83.6 0.1 eq.50
  83.8 2.3 %convert_reduce_fusion = s32[32,160]{1,0:T(8,128)S(1)} fusion(s32[32,160]{1,0:T(8,128)S(1)} %eq.50, pred[160,160]{1,0:T(8,128)(4,1)S(1)} %iota_compare_fusion), kind=kLoop, calls=%fused_computation.10 | loop fusion | flops 3271680 | bytes 66560 | tf_op jit(solution)/shard_map/vmap()/reduce_sum | solution.py:77
  86.1 0.1 reduce_sum.136
  86.2 0.2 sub.41
  86.5 19.2 %scatter_custom_fusion = s32[256]{0:T(256)S(1)} fusion(s32[5120]{0:T(1024)S(1)} %bitcast.90, s32[5120]{0:T(1024)S(1)} %reshape.379, s32[]{:T(128)} %constant.43.clone.1), kind=kCustom, calls=%fused_computation.89 | custom fusion | bytes 1028 | tf_op jit(solution)/shard_map/scatter | solution.py:169
  105.8 0.9 fusion.29
  106.7 2.9 %gather_fusion = bf16[256,1024]{1,0:T(8,128)(2,1)S(1)} fusion(bf16[512,1024]{1,0:T(8,128)(2,1)} %all-gather.2.cloned.1.call-done, s32[1024]{0:T(1024)S(1)} %pad_clamp_fusion.1), kind=kCustom, calls=%fused_computation | custom fusion | bytes 1049600 | tf_op jit(solution)/shard_map/jit(_take)/gather | solution.py:170
  109.6 0.5 convolution_bitcast_fusion
  110.1 1.1 fusion.1
  111.2 2.6 %all-to-all-start = ((bf16[32,1,8,1024]{3,2,1,0:T(8,128)(2,1)}), bf16[32,1,8,1024]{3,2,1,0:T(8,128)(2,1)S(1)}, u32[]{:S(2)}, u32[]{:S(2)}) async-start(bf16[32,1,8,1024]{3,2,1,0:T(8,128)(2,1)} %fusion.1), calls=%async_computation | async-start | bytes 1048576 | tf_op jit(solution)/shard_map/all_to_all | solution.py:91
  113.9 0.2 convert_reduce_fusion.1
  114.0 0.1 copy.45
  114.1 0.1 reduce_sum.134
  114.2 0.1 mul.329
  114.3 0.2 select_reduce_fusion
  114.5 0.1 copy.46
  114.6 14.7 %all-to-all-done = bf16[32,1,8,1024]{3,2,1,0:T(8,128)(2,1)S(1)} async-done(((bf16[32,1,8,1024]{3,2,1,0:T(8,128)(2,1)}), bf16[32,1,8,1024]{3,2,1,0:T(8,128)(2,1)S(1)}, u32[]{:S(2)}, u32[]{:S(2)}) %all-to-all-start) | async-done | bytes 524320 | tf_op jit(solution)/shard_map/all_to_all | solution.py:91
  129.4 0.9 gather_fusion.1
  130.3 0.1 gather.12
  130.5 0.5 multiply_reduce_fusion.4
  131.0 0.6 reshape.350
  (47 shorter events, 0.6 us)
Async XLA Ops:
  6.5 103.1 %copy-start = (bf16[1,1024,512]{2,1,0:T(8,128)(2,1)S(1)}, bf16[1,1024,512]{2,1,0:T(8,128)(2,1)}, u32[]{:S(2)}) copy-start(bf16[1,1024,512]{2,1,0:T(8,128)(2,1)} %param.31) | copy-start | bytes 3145732
  6.5 100.2 %all-gather.2.cloned.1.call-start = ((), (), s32[]{:S(2)}) async-start(), calls=%async_computation.1 | async-start | bytes 1081344 | tf_op jit(solution)/shard_map/all_gather | solution.py:152
  13.0 5.2 %copy-start.1 = (bf16[8,16,128,128]{3,2,1,0:T(8,128)(2,1)S(1)}, bf16[8,16,128,128]{3,2,1,0:T(8,128)(2,1)}, u32[]{:S(2)}) copy-start(bf16[8,16,128,128]{3,2,1,0:T(8,128)(2,1)} %param.27) | copy-start | bytes 12582916
  18.3 16.9 %copy-start.3 = (bf16[8,2,2048]{2,1,0:T(2,128)(2,1)S(1)}, bf16[8,2,2048]{2,1,0:T(2,128)(2,1)}, u32[]{:S(2)}) copy-start(bf16[8,2,2048]{2,1,0:T(2,128)(2,1)} %param.21) | copy-start | bytes 196612
  24.2 14.3 %copy-start.5 = (f32[1024]{0:T(1024)S(1)}, f32[1024]{0:T(1024)}, u32[]{:S(2)}) copy-start(f32[1024]{0:T(1024)} %param.29) | copy-start | bytes 12292
  24.2 15.1 %copy-start.2 = (s32[8,2,10]{2,1,0:T(2,128)S(1)}, s32[8,2,10]{2,1,0:T(2,128)}, u32[]{:S(2)}) copy-start(s32[8,2,10]{2,1,0:T(2,128)} %param.33) | copy-start | bytes 1924
  34.9 70.9 %copy-start.4 = (bf16[1024,32]{0,1:T(8,128)(2,1)S(1)}, bf16[1024,32]{0,1:T(8,128)(2,1)}, u32[]{:S(2)}) copy-start(bf16[1024,32]{0,1:T(8,128)(2,1)} %param.30) | copy-start | bytes 196612
  83.6 26.5 %copy-start.6 = (bf16[1,256,1024]{2,1,0:T(8,128)(2,1)S(1)}, bf16[1,256,1024]{2,1,0:T(8,128)(2,1)}, u32[]{:S(2)}) copy-start(bf16[1,256,1024]{2,1,0:T(8,128)(2,1)} %param.32) | copy-start | bytes 1572868
  111.2 18.2 %all-to-all-start = ((bf16[32,1,8,1024]{3,2,1,0:T(8,128)(2,1)}), bf16[32,1,8,1024]{3,2,1,0:T(8,128)(2,1)S(1)}, u32[]{:S(2)}, u32[]{:S(2)}) async-start(bf16[32,1,8,1024]{3,2,1,0:T(8,128)(2,1)} %fusion.1), calls=%async_computation | async-start | bytes 1048576 | tf_op jit(solution)/shard_map/all_to_all | solution.py:91
Sparse Core Ops, SparseCore 0:
  39.3 56.3 all-gather.1
where the time goes:
time: 139 us; the launch traced here: 138 us
  blocking collectives  44 us (32%)
  local copies, waits for them, and re-layouts  29.1 us (21%)
  other arithmetic  28.7 us (21%)
  waiting for transfers between devices  14.8 us (11%)
  between operations  13.9 us (10%)
  matrix products  5.43 us (4%)
  starting transfers between devices  2.61 us (2%)
    all_gather x1, blocking collectives, shards(): all_picks = lax.all_gather(picked_ids, 'dp', axis=0, tiled=True)  44 us
    scatter x1, local copies, waits for them, and re-layouts, shards(): slot_source.at[slot_place.reshape(-1)]  19.2 us
    all_to_all x1, waiting for transfers between devices, run_experts(): lax.all_to_all(produced, 'dp', split_axis=0, concat_axis=0, tiled=True)  14.7 us
    reduce_sum x2, other arithmetic, delta_block(): recalled = jnp.sum(memory * keys_now[..., None], axis=2)  10.8 us
    reduce_sum x1, other arithmetic, delta_block(): outputs.append(jnp.sum(memory * query_all[:, position][..., None], axis=2))  10.6 us
    dot_general x1, matrix products, shards(): jnp.dot(mixer_out, out_proj, preferred_element_type=jnp.float32)  2.95 us
    gather x1, local copies, waits for them, and re-layouts, shards(): blocks = jnp.take(all_rows, slot_source, axis=0, mode='fill', fill_value=0)  2.92 us
  transfers between devices with their start and end apart: 2, of which 1 were waited for; matrix products, arithmetic and copies ran while one was open for 17% of the time, Pallas kernels for 0%

commit v1 on v0

v1 whole, which is shorter than its diff:
```python
import functools

import jax
import jax.numpy as jnp
from jax import lax
from jax.experimental import pallas as pl
from jax.experimental.pallas import tpu as pltpu
from jax.sharding import PartitionSpec as P

eps_norm = 1e-06
f32 = jnp.float32
bf16 = jnp.bfloat16


def split_two(x):
    high = x.astype(bf16)
    low = (x - high.astype(f32)).astype(bf16)
    return high, low


def nt_dot(a, b):
    return lax.dot_general(a, b, (((1,), (1,)), ((), ())), preferred_element_type=f32)


def mixer_kernel(
    capacity,
    hidden_ref,
    query_ref,
    key_ref,
    value_ref,
    gate_ref,
    decay_in_ref,
    beta_in_ref,
    decay_log_ref,
    step_bias_ref,
    norm_gain_ref,
    post_gain_ref,
    router_ref,
    ids_ref,
    state_hbm,
    proj_hbm,
    blocks_ref,
    weights_ref,
    middle_ref,
    state_buf,
    proj_buf,
    left_buf,
    right_buf,
    state_sem,
    proj_sem,
):
    rows = query_ref.shape[0]
    value_heads, key_size, value_size = state_hbm.shape[1:]
    key_heads = query_ref.shape[2] // key_size
    share = value_heads // key_heads
    span = share * value_size
    chunks = proj_sem.shape[0]
    depth = proj_hbm.shape[0] // chunks

    def state_copy(h):
        return pltpu.make_async_copy(
            state_hbm.at[:, pl.ds(h * share, share)], state_buf.at[h], state_sem.at[h]
        )

    def proj_copy(c):
        part = pl.ds(c * depth, depth)
        return pltpu.make_async_copy(proj_hbm.at[part], proj_buf.at[part], proj_sem.at[c])

    for h in range(key_heads):
        state_copy(h).start()
    for c in range(chunks):
        proj_copy(c).start()

    query_all = query_ref[...].astype(f32)
    key_all = key_ref[...].astype(f32)
    value_all = value_ref[...].astype(f32)
    gate_all = gate_ref[...].astype(f32)
    decay_in = decay_in_ref[...].astype(f32)
    beta_in = beta_in_ref[...].astype(f32)
    rate = -jnp.exp(decay_log_ref[...].reshape(1, value_heads))
    bias = step_bias_ref[...].reshape(1, value_heads)
    decays, betas = [], []
    for p in range(2):
        decays.append(jnp.exp(rate * jax.nn.softplus(decay_in[:, p, :] + bias)))
        betas.append(1.0 / (1.0 + jnp.exp(-beta_in[:, p, :])))
    gain = norm_gain_ref[...].reshape(1, value_size)

    mixed = [[], []]
    for h in range(key_heads):
        lanes = slice(h * key_size, (h + 1) * key_size)
        keys, queries = [], []
        for p in range(2):
            k = key_all[:, p, lanes]
            q = query_all[:, p, lanes]
            keys.append(k * lax.rsqrt(jnp.sum(k * k, axis=-1, keepdims=True) + eps_norm))
            queries.append(
                q
                * lax.rsqrt(jnp.sum(q * q, axis=-1, keepdims=True) + eps_norm)
                * key_size ** (-0.5)
            )
        vectors = (keys[0], queries[0], keys[1], queries[1])
        for j, v in enumerate(vectors):
            high = v.astype(bf16).astype(f32)
            left_buf[h, pl.ds(2 * j, rows, stride=8), :] = high
            left_buf[h, pl.ds(2 * j + 1, rows, stride=8), :] = v - high
        key_key = jnp.sum(keys[0] * keys[1], axis=-1, keepdims=True)
        key_query00 = jnp.sum(keys[0] * queries[0], axis=-1, keepdims=True)
        key_query01 = jnp.sum(keys[0] * queries[1], axis=-1, keepdims=True)
        key_query11 = jnp.sum(keys[1] * queries[1], axis=-1, keepdims=True)

        state_copy(h).wait()
        for r in range(rows):
            left = left_buf[h, r * 8 : (r + 1) * 8, :].astype(bf16)
            right = jnp.concatenate([state_buf[h, r, i] for i in range(share)], axis=-1)
            out = jnp.dot(left, right, preferred_element_type=f32)
            for i in range(share):
                right_buf[h, i, r * 8 : (r + 1) * 8, :] = out[:, i * value_size : (i + 1) * value_size]

        for i in range(share):
            n = h * share + i
            heads = slice(n * value_size, (n + 1) * value_size)
            part = [
                right_buf[h, i, pl.ds(2 * j, rows, stride=8), :]
                + right_buf[h, i, pl.ds(2 * j + 1, rows, stride=8), :]
                for j in range(4)
            ]
            d0, d1 = decays[0][:, n : n + 1], decays[1][:, n : n + 1]
            b0, b1 = betas[0][:, n : n + 1], betas[1][:, n : n + 1]
            u0 = b0 * (value_all[:, 0, heads] - d0 * part[0])
            o0 = d0 * part[1] + key_query00 * u0
            u1 = b1 * (value_all[:, 1, heads] - d1 * (d0 * part[2] + key_key * u0))
            o1 = d1 * (d0 * part[3] + key_query01 * u0) + key_query11 * u1
            for p, o in enumerate((o0, o1)):
                g = gate_all[:, p, heads]
                mean = jnp.mean(o * o, axis=-1, keepdims=True)
                mixed[p].append(
                    o * lax.rsqrt(mean + eps_norm) * gain * (g / (1.0 + jnp.exp(-g)))
                )

    mixer_out = jnp.concatenate(
        [jnp.concatenate(mixed[p], axis=-1) for p in range(2)], axis=0
    ).astype(bf16)
    hidden = hidden_ref[...].astype(f32)
    total = jnp.concatenate([hidden[:, p, :] for p in range(2)], axis=0)
    for c in range(chunks):
        proj_copy(c).wait()
        part = slice(c * depth, (c + 1) * depth)
        total = total + jnp.dot(mixer_out[:, part], proj_buf[part, :], preferred_element_type=f32)
    middle = total.astype(bf16)
    middle_ref[...] = middle
    wide = middle.astype(f32)
    routed = (
        wide
        * lax.rsqrt(jnp.mean(wide * wide, axis=-1, keepdims=True) + eps_norm)
        * post_gain_ref[...].reshape(1, wide.shape[1])
    ).astype(bf16)
    logits = jnp.dot(routed, router_ref[...], preferred_element_type=f32)

    tokens = 2 * rows
    experts = logits.shape[1]
    slots = experts * capacity
    ids = jnp.concatenate([ids_ref[:, p, :] for p in range(2)], axis=0)
    expert = lax.broadcasted_iota(jnp.int32, (tokens, experts), 1)
    chosen = jnp.zeros((tokens, experts), f32)
    for k in range(ids.shape[1]):
        chosen = chosen + (ids[:, k : k + 1] == expert).astype(f32)
    raised = jnp.where(chosen > 0.0, jnp.exp(logits), 0.0)
    share_all = raised / jnp.sum(raised, axis=-1, keepdims=True)
    later = lax.broadcasted_iota(jnp.int32, (tokens, tokens), 0)
    earlier = lax.broadcasted_iota(jnp.int32, (tokens, tokens), 1)
    below = (later > earlier).astype(bf16)
    chosen16 = chosen.astype(bf16)
    slot = jnp.dot(below, chosen16, preferred_element_type=f32)
    place = jnp.where(chosen > 0.0, slot, -1.0).astype(bf16)
    slot_expert = lax.broadcasted_iota(jnp.int32, (slots, experts), 0) // capacity
    spread = (slot_expert == lax.broadcasted_iota(jnp.int32, (slots, experts), 1)).astype(bf16)
    number = lax.broadcasted_iota(jnp.int32, (slots, tokens), 0)
    take = (nt_dot(spread, place) == (number % capacity).astype(f32)).astype(bf16)
    blocks_ref[...] = jnp.dot(take, routed, preferred_element_type=f32).astype(bf16)
    lane = lax.broadcasted_iota(jnp.int32, (tokens, slots), 1)
    match = nt_dot(place, spread) == (lane % capacity).astype(f32)
    high, low = split_two(share_all)
    spread_share = nt_dot(high, spread) + nt_dot(low, spread)
    weights_ref[...] = jnp.where(match, spread_share, 0.0)


def expert_kernel(blocks_ref, up_ref, down_ref, out_ref):
    hidden_units = down_ref.shape[1]
    both = jnp.dot(blocks_ref[...], up_ref[0], preferred_element_type=f32)
    g = both[:, :hidden_units]
    activated = (g / (1.0 + jnp.exp(-g)) * both[:, hidden_units:]).astype(bf16)
    out_ref[...] = jnp.dot(activated, down_ref[0], preferred_element_type=f32).astype(bf16)


def combine_kernel(returned_ref, weights_ref, middle_ref, out_ref):
    rows = out_ref.shape[0]
    high, low = split_two(weights_ref[...])
    returned = returned_ref[...]
    total = (
        middle_ref[...].astype(f32)
        + jnp.dot(high, returned, preferred_element_type=f32)
        + jnp.dot(low, returned, preferred_element_type=f32)
    ).astype(bf16)
    for p in range(2):
        out_ref[:, p, :] = total[p * rows : (p + 1) * rows]


def vmem(count):
    return [pl.BlockSpec(memory_space=pltpu.VMEM)] * count


def shards(
    hidden_in,
    query_in,
    key_in,
    value_in,
    gate_in,
    decay_in,
    beta_in,
    decay_log,
    step_bias,
    norm_gain,
    state_in,
    out_proj,
    post_gain,
    router_weight,
    expert_gate_up,
    expert_down,
    expert_ids,
):
    device_count = lax.axis_size("dp")
    expert_total = expert_gate_up.shape[0] * device_count
    row_count, _, model_width = hidden_in.shape
    pick_count = expert_ids.shape[2]
    value_heads, key_size, value_size = state_in.shape[1:]
    key_heads = query_in.shape[2] // key_size
    share = value_heads // key_heads
    token_count = row_count * 2
    capacity = min(
        token_count, max(2, (3 * row_count * pick_count + expert_total - 1) // expert_total)
    )
    slots = expert_total * capacity
    chunks = 4
    params = pltpu.CompilerParams(vmem_limit_bytes=48 * 1024 * 1024)
    blocks, weights, middle = pl.pallas_call(
        functools.partial(mixer_kernel, capacity),
        out_shape=(
            jax.ShapeDtypeStruct((slots, model_width), bf16),
            jax.ShapeDtypeStruct((token_count, slots), f32),
            jax.ShapeDtypeStruct((token_count, model_width), bf16),
        ),
        in_specs=vmem(13) + [pl.BlockSpec(memory_space=pl.ANY)] * 2,
        out_specs=tuple(vmem(3)),
        scratch_shapes=[
            pltpu.VMEM((key_heads, row_count, share, key_size, value_size), bf16),
            pltpu.VMEM(out_proj.shape, bf16),
            pltpu.VMEM((key_heads, 8 * row_count, key_size), f32),
            pltpu.VMEM((key_heads, share, 8 * row_count, value_size), f32),
            pltpu.SemaphoreType.DMA((key_heads,)),
            pltpu.SemaphoreType.DMA((chunks,)),
        ],
        compiler_params=params,
        name="mixer",
    )(
        hidden_in,
        query_in,
        key_in,
        value_in,
        gate_in,
        decay_in,
        beta_in,
        decay_log,
        step_bias,
        norm_gain,
        post_gain,
        router_weight,
        expert_ids,
        state_in,
        out_proj,
    )
    received = lax.all_to_all(blocks, "dp", split_axis=0, concat_axis=0, tiled=True)
    produced = pl.pallas_call(
        expert_kernel,
        out_shape=jax.ShapeDtypeStruct((slots, model_width), bf16),
        in_specs=vmem(3),
        out_specs=vmem(1)[0],
        compiler_params=params,
        name="experts",
    )(received, expert_gate_up, expert_down)
    returned = lax.all_to_all(produced, "dp", split_axis=0, concat_axis=0, tiled=True)
    return pl.pallas_call(
        combine_kernel,
        out_shape=jax.ShapeDtypeStruct(hidden_in.shape, bf16),
        in_specs=vmem(3),
        out_specs=vmem(1)[0],
        compiler_params=params,
        name="combine",
    )(returned, weights, middle)


def solution(mesh):
    rows = P(("groups", "dp"))
    placed = (
        (rows,) * 7 + (P(),) * 3 + (rows,) + (P(),) * 3 + (P("dp"),) * 2 + (rows,)
    )
    return jax.shard_map(
        shards,
        mesh=mesh,
        in_specs=placed,
        out_specs=rows,
        check_vma=False,
    )
```

time: 139 us -> 59.6 us (0.43)
  other arithmetic: 28.7 us -> 0 us
  local copies, waits for them, and re-layouts: 29.1 us -> 11.9 us
  waiting for transfers between devices: 14.8 us -> 0 us
  between operations: 13.9 us -> 0.05 us
  Pallas kernels: 0 us -> 5.89 us
  matrix products: 5.43 us -> 0 us
  blocking collectives: 44 us -> 41.1 us
  starting transfers between devices: 2.61 us -> 0 us
    all_gather x1 -> x0, blocking collectives: 44 us -> none  [shards(): all_picks = lax.all_gather(picked_ids, 'dp', axis=0, tiled=True)]
    all_to_all x0 -> x2, blocking collectives: none -> 41.1 us  [the longest x1 22.6 us: shards(): lax.all_to_all(blocks, 'dp', split_axis=0, concat_axis=0, tiled=True)]
    reduce_sum x11 -> x0, other arithmetic: 24.9 us -> none  [the longest x2 10.8 us: delta_block(): recalled = jnp.sum(memory * keys_now[..., None], axis=2)]
    scatter x1 -> x0, local copies, waits for them, and re-layouts: 19.2 us -> none  [shards(): slot_source.at[slot_place.reshape(-1)]]
    all_to_all x1 -> x0, waiting for transfers between devices: 14.7 us -> none  [run_experts(): lax.all_to_all(produced, 'dp', split_axis=0, concat_axis=0, tiled=True)]
    unnamed x14 -> x31, local copies, waits for them, and re-layouts: 0.04 us -> 11.9 us
    pallas_call x0 -> x3, Pallas kernels: none -> 5.89 us  [the longest x1 4.34 us: shards(): pl.pallas_call(functools.partial(mixer_kernel, capacity), out_shape=(jax....]
    dot_general x4 -> x0, matrix products: 5.43 us -> none  [the longest x1 2.95 us: shards(): jnp.dot(mixer_out, out_proj, preferred_element_type=jnp.float32)]
  transfers between devices with their start and end apart: 2 -> 0, of which waited for: 1 -> 0; matrix products, arithmetic and copies ran while one was open for 17% -> 0% of each run, Pallas kernels for 0% -> 0%
where the time goes in v1:
time: 59.6 us; the launch traced here: 58.9 us
  blocking collectives  41.1 us (69%)
  local copies, waits for them, and re-layouts  11.9 us (20%)
  Pallas kernels  5.89 us (10%)
    all_to_all x1, blocking collectives, shards(): lax.all_to_all(blocks, 'dp', split_axis=0, concat_axis=0, tiled=True)  22.6 us
    all_to_all x1, blocking collectives, shards(): lax.all_to_all(produced, 'dp', split_axis=0, concat_axis=0, tiled=True)  18.4 us
    unnamed x31, local copies, waits for them, and re-layouts  11.9 us
    pallas_call x1, Pallas kernels, shards(): pl.pallas_call(functools.partial(mixer_kernel, capacity), out_shape=(jax....  4.34 us

profile of v1, /device:TPU:0, one launch (start us, length us, event | category | flops | bytes accessed | tf_op | source)
XLA Modules:
  0.0 58.9 jit_solution(18178892088970344349)
XLA Ops:
  0.0 1.0 %copy.18.router_ref = bf16[1024,32]{1,0:T(8,128)(2,1)S(1)} copy(bf16[1024,32]{0,1:T(8,128)(2,1)} %param.30) | data formatting | bytes 131072 | tf_op args[13]
  1.0 0.0 copy-start
  1.0 2.2 %copy-done = bf16[8,16,128,128]{3,2,1,0:T(8,128)(2,1)S(1)} copy-done((bf16[8,16,128,128]{3,2,1,0:T(8,128)(2,1)S(1)}, bf16[8,16,128,128]{3,2,1,0:T(8,128)(2,1)}, u32[]{:S(2)}) %copy-start) | copy-done | bytes 4194328
  3.2 0.0 copy-start.3
  3.2 0.8 %copy-done.3 = bf16[8,2,2048]{2,1,0:T(2,128)(2,1)S(1)} copy-done((bf16[8,2,2048]{2,1,0:T(2,128)(2,1)S(1)}, bf16[8,2,2048]{2,1,0:T(2,128)(2,1)}, u32[]{:S(2)}) %copy-start.3) | copy-done | bytes 65560
  4.0 0.0 copy-start.4
  4.0 0.8 %copy-done.4 = bf16[8,2,2048]{2,1,0:T(2,128)(2,1)S(1)} copy-done((bf16[8,2,2048]{2,1,0:T(2,128)(2,1)S(1)}, bf16[8,2,2048]{2,1,0:T(2,128)(2,1)}, u32[]{:S(2)}) %copy-start.4) | copy-done | bytes 65560
  4.9 0.0 copy-start.5
  4.9 0.8 %copy-done.5 = bf16[8,2,1024]{2,1,0:T(2,128)(2,1)S(1)} copy-done((bf16[8,2,1024]{2,1,0:T(2,128)(2,1)S(1)}, bf16[8,2,1024]{2,1,0:T(2,128)(2,1)}, u32[]{:S(2)}) %copy-start.5) | copy-done | bytes 32792
  5.6 0.0 copy-start.6
  5.6 0.8 %copy-done.6 = bf16[8,2,1024]{2,1,0:T(2,128)(2,1)S(1)} copy-done((bf16[8,2,1024]{2,1,0:T(2,128)(2,1)S(1)}, bf16[8,2,1024]{2,1,0:T(2,128)(2,1)}, u32[]{:S(2)}) %copy-start.6) | copy-done | bytes 32792
  6.4 0.0 copy-start.7
  6.4 0.8 %copy-done.7 = bf16[8,2,1024]{2,1,0:T(2,128)(2,1)S(1)} copy-done((bf16[8,2,1024]{2,1,0:T(2,128)(2,1)S(1)}, bf16[8,2,1024]{2,1,0:T(2,128)(2,1)}, u32[]{:S(2)}) %copy-start.7) | copy-done | bytes 32792
  7.2 0.0 copy-start.8
  7.2 0.7 %copy-done.8 = s32[8,2,10]{2,1,0:T(2,128)S(1)} copy-done((s32[8,2,10]{2,1,0:T(2,128)S(1)}, s32[8,2,10]{2,1,0:T(2,128)}, u32[]{:S(2)}) %copy-start.8) | copy-done | bytes 664
  7.9 0.0 copy-start.9
  7.9 0.7 %copy-done.9 = bf16[8,2,16]{2,1,0:T(2,128)(2,1)S(1)} copy-done((bf16[8,2,16]{2,1,0:T(2,128)(2,1)S(1)}, bf16[8,2,16]{2,1,0:T(2,128)(2,1)}, u32[]{:S(2)}) %copy-start.9) | copy-done | bytes 536
  8.5 0.0 copy-start.10
  8.5 0.7 %copy-done.10 = bf16[8,2,16]{2,1,0:T(2,128)(2,1)S(1)} copy-done((bf16[8,2,16]{2,1,0:T(2,128)(2,1)S(1)}, bf16[8,2,16]{2,1,0:T(2,128)(2,1)}, u32[]{:S(2)}) %copy-start.10) | copy-done | bytes 536
  9.2 0.0 copy-start.11
  9.2 0.7 %copy-done.11 = f32[1024]{0:T(1024)S(1)} copy-done((f32[1024]{0:T(1024)S(1)}, f32[1024]{0:T(1024)}, u32[]{:S(2)}) %copy-start.11) | copy-done | bytes 4120
  9.9 0.0 copy-start.12
  9.9 0.7 %copy-done.12 = f32[16]{0:T(128)S(1)} copy-done((f32[16]{0:T(128)S(1)}, f32[16]{0:T(128)}, u32[]{:S(2)}) %copy-start.12) | copy-done | bytes 88
  10.6 0.0 copy-start.13
  10.6 0.7 %copy-done.13 = f32[16]{0:T(128)S(1)} copy-done((f32[16]{0:T(128)S(1)}, f32[16]{0:T(128)}, u32[]{:S(2)}) %copy-start.13) | copy-done | bytes 88
  11.2 0.0 copy-start.14
  11.2 0.7 %copy-done.14 = f32[128]{0:T(128)S(1)} copy-done((f32[128]{0:T(128)S(1)}, f32[128]{0:T(128)}, u32[]{:S(2)}) %copy-start.14) | copy-done | bytes 536
  11.9 0.0 copy-start.1
  11.9 0.0 copy-start.2
  11.9 4.3 %mixer.1 = (bf16[256,1024]{1,0:T(8,128)(2,1)S(1)}, f32[16,256]{1,0:T(8,128)S(1)}, bf16[16,1024]{1,0:T(8,128)(2,1)S(1)}) custom-call(bf16[8,2,1024]{2,1,0:T(2,128)(2,1)S(1)} %copy-done.5, bf16[8,2,1024]{2,1,0:T(2,128)(2,1)S(1)} %copy-done.6, bf16[8,2,1024]{2,1,0:T(2,128)(2,1)S(1)} %copy-done.7, bf16[8,2,2048]{2,1,0:T(2,128)(2,1)S(1)} %copy-done.3, ...), custom_call_target="tpu_custom_call" | custom-call | tf_op jit(solution)/shard_map/mixer/pallas_call | solution.py:245
  16.2 22.6 %all_to_all.22 = bf16[32,8,1024]{2,1,0:T(8,128)(2,1)S(1)} all-to-all(bf16[32,8,1024]{2,1,0:T(8,128)(2,1)S(1)} %bitcast.7), channel_id=1, replica_groups=mesh['groups'=1,'dp'=32] {'dp'}, dimensions={0} | all-to-all | bytes 1048576 | tf_op jit(solution)/shard_map/all_to_all | solution.py:281
  38.9 0.0 copy-done.1
  38.9 0.0 copy-done.2
  38.9 0.7 %experts.1 = bf16[256,1024]{1,0:T(8,128)(2,1)S(1)} custom-call(bf16[256,1024]{1,0:T(8,128)(2,1)S(1)} %bitcast.4, bf16[1,1024,512]{2,1,0:T(8,128)(2,1)S(1)} %copy-done.1, bf16[1,256,1024]{2,1,0:T(8,128)(2,1)S(1)} %copy-done.2), custom_call_target="tpu_custom_call" | custom-call | tf_op jit(solution)/shard_map/experts/pallas_call | solution.py:282
  39.6 18.4 %all_to_all.23 = bf16[32,8,1024]{2,1,0:T(8,128)(2,1)S(1)} all-to-all(bf16[32,8,1024]{2,1,0:T(8,128)(2,1)S(1)} %bitcast.5), channel_id=1, replica_groups=mesh['groups'=1,'dp'=32] {'dp'}, dimensions={0} | all-to-all | bytes 1048576 | tf_op jit(solution)/shard_map/all_to_all | solution.py:290
  58.0 0.9 %combine.1 = bf16[8,2,1024]{2,1,0:T(2,128)(2,1)} custom-call(bf16[256,1024]{1,0:T(8,128)(2,1)S(1)} %bitcast.6, f32[16,256]{1,0:T(8,128)S(1)} %get-tuple-element.9.weights_ref, bf16[16,1024]{1,0:T(8,128)(2,1)S(1)} %get-tuple-element.10.middle_ref), custom_call_target="tpu_custom_call" | custom-call | tf_op jit(solution)/shard_map/combine/pallas_call | solution.py:291
Async XLA Ops:
  1.0 2.2 %copy-start = (bf16[8,16,128,128]{3,2,1,0:T(8,128)(2,1)S(1)}, bf16[8,16,128,128]{3,2,1,0:T(8,128)(2,1)}, u32[]{:S(2)}) copy-start(bf16[8,16,128,128]{3,2,1,0:T(8,128)(2,1)} %state_hbm.1) | copy-start | bytes 12582916
  3.2 0.8 %copy-start.3 = (bf16[8,2,2048]{2,1,0:T(2,128)(2,1)S(1)}, bf16[8,2,2048]{2,1,0:T(2,128)(2,1)}, u32[]{:S(2)}) copy-start(bf16[8,2,2048]{2,1,0:T(2,128)(2,1)} %value_ref.1) | copy-start | bytes 196612
  4.0 0.8 %copy-start.4 = (bf16[8,2,2048]{2,1,0:T(2,128)(2,1)S(1)}, bf16[8,2,2048]{2,1,0:T(2,128)(2,1)}, u32[]{:S(2)}) copy-start(bf16[8,2,2048]{2,1,0:T(2,128)(2,1)} %gate_ref.1) | copy-start | bytes 196612
  4.9 0.8 %copy-start.5 = (bf16[8,2,1024]{2,1,0:T(2,128)(2,1)S(1)}, bf16[8,2,1024]{2,1,0:T(2,128)(2,1)}, u32[]{:S(2)}) copy-start(bf16[8,2,1024]{2,1,0:T(2,128)(2,1)} %hidden_ref.1) | copy-start | bytes 98308
  5.6 0.8 %copy-start.6 = (bf16[8,2,1024]{2,1,0:T(2,128)(2,1)S(1)}, bf16[8,2,1024]{2,1,0:T(2,128)(2,1)}, u32[]{:S(2)}) copy-start(bf16[8,2,1024]{2,1,0:T(2,128)(2,1)} %query_ref.1) | copy-start | bytes 98308
  6.4 0.8 %copy-start.7 = (bf16[8,2,1024]{2,1,0:T(2,128)(2,1)S(1)}, bf16[8,2,1024]{2,1,0:T(2,128)(2,1)}, u32[]{:S(2)}) copy-start(bf16[8,2,1024]{2,1,0:T(2,128)(2,1)} %key_ref.1) | copy-start | bytes 98308
  7.2 0.7 %copy-start.8 = (s32[8,2,10]{2,1,0:T(2,128)S(1)}, s32[8,2,10]{2,1,0:T(2,128)}, u32[]{:S(2)}) copy-start(s32[8,2,10]{2,1,0:T(2,128)} %ids_ref.1) | copy-start | bytes 1924
  7.9 0.7 %copy-start.9 = (bf16[8,2,16]{2,1,0:T(2,128)(2,1)S(1)}, bf16[8,2,16]{2,1,0:T(2,128)(2,1)}, u32[]{:S(2)}) copy-start(bf16[8,2,16]{2,1,0:T(2,128)(2,1)} %decay_in_ref.1) | copy-start | bytes 1540
  8.5 0.7 %copy-start.10 = (bf16[8,2,16]{2,1,0:T(2,128)(2,1)S(1)}, bf16[8,2,16]{2,1,0:T(2,128)(2,1)}, u32[]{:S(2)}) copy-start(bf16[8,2,16]{2,1,0:T(2,128)(2,1)} %beta_in_ref.1) | copy-start | bytes 1540
  9.2 0.7 %copy-start.11 = (f32[1024]{0:T(1024)S(1)}, f32[1024]{0:T(1024)}, u32[]{:S(2)}) copy-start(f32[1024]{0:T(1024)} %post_gain_ref.1) | copy-start | bytes 12292
  9.9 0.7 %copy-start.12 = (f32[16]{0:T(128)S(1)}, f32[16]{0:T(128)}, u32[]{:S(2)}) copy-start(f32[16]{0:T(128)} %decay_log_ref.1) | copy-start | bytes 196
  10.6 0.7 %copy-start.13 = (f32[16]{0:T(128)S(1)}, f32[16]{0:T(128)}, u32[]{:S(2)}) copy-start(f32[16]{0:T(128)} %step_bias_ref.1) | copy-start | bytes 196
  11.2 0.7 %copy-start.14 = (f32[128]{0:T(128)S(1)}, f32[128]{0:T(128)}, u32[]{:S(2)}) copy-start(f32[128]{0:T(128)} %norm_gain_ref.1) | copy-start | bytes 1540
  11.9 27.0 %copy-start.1 = (bf16[1,1024,512]{2,1,0:T(8,128)(2,1)S(1)}, bf16[1,1024,512]{2,1,0:T(8,128)(2,1)}, u32[]{:S(2)}) copy-start(bf16[1,1024,512]{2,1,0:T(8,128)(2,1)} %up_ref.1) | copy-start | bytes 3145732
  11.9 27.0 %copy-start.2 = (bf16[1,256,1024]{2,1,0:T(8,128)(2,1)S(1)}, bf16[1,256,1024]{2,1,0:T(8,128)(2,1)}, u32[]{:S(2)}) copy-start(bf16[1,256,1024]{2,1,0:T(8,128)(2,1)} %down_ref.1) | copy-start | bytes 1572868

commit v2 on v1

--- a/solution.py
+++ b/solution.py
@@ -24,6 +24,24 @@
 
 def mixer_kernel(
     capacity,
+    hidden_hbm,
+    query_hbm,
+    key_hbm,
+    value_hbm,
+    gate_hbm,
+    decay_in_hbm,
+    beta_in_hbm,
+    decay_log_hbm,
+    step_bias_hbm,
+    norm_gain_hbm,
+    post_gain_hbm,
+    router_hbm,
+    ids_hbm,
+    state_hbm,
+    proj_hbm,
+    blocks_ref,
+    weights_ref,
+    middle_ref,
     hidden_ref,
     query_ref,
     key_ref,
@@ -37,15 +55,11 @@
     post_gain_ref,
     router_ref,
     ids_ref,
-    state_hbm,
-    proj_hbm,
-    blocks_ref,
-    weights_ref,
-    middle_ref,
     state_buf,
     proj_buf,
     left_buf,
     right_buf,
+    small_sem,
     state_sem,
     proj_sem,
 ):
@@ -66,10 +80,36 @@
         part = pl.ds(c * depth, depth)
         return pltpu.make_async_copy(proj_hbm.at[part], proj_buf.at[part], proj_sem.at[c])
 
-    for h in range(key_heads):
+    pairs = (
+        (key_hbm, key_ref),
+        (query_hbm, query_ref),
+        (decay_log_hbm, decay_log_ref),
+        (step_bias_hbm, step_bias_ref),
+        (decay_in_hbm, decay_in_ref),
+        (beta_in_hbm, beta_in_ref),
+        (norm_gain_hbm, norm_gain_ref),
+        (value_hbm, value_ref),
+        (gate_hbm, gate_ref),
+        (ids_hbm, ids_ref),
+        (hidden_hbm, hidden_ref),
+        (post_gain_hbm, post_gain_ref),
+        (router_hbm, router_ref),
+    )
+    small = [pltpu.make_async_copy(a, b, small_sem.at[i]) for i, (a, b) in enumerate(pairs)]
+    early, late = small[:9], small[9:]
+    for copy in early[:2]:
+        copy.start()
+    state_copy(0).start()
+    for copy in early[2:]:
+        copy.start()
+    for h in range(1, key_heads):
         state_copy(h).start()
     for c in range(chunks):
         proj_copy(c).start()
+    for copy in late:
+        copy.start()
+    for copy in early:
+        copy.wait()
 
     query_all = query_ref[...].astype(f32)
     key_all = key_ref[...].astype(f32)
@@ -140,6 +180,8 @@
     mixer_out = jnp.concatenate(
         [jnp.concatenate(mixed[p], axis=-1) for p in range(2)], axis=0
     ).astype(bf16)
+    for copy in late:
+        copy.wait()
     hidden = hidden_ref[...].astype(f32)
     total = jnp.concatenate([hidden[:, p, :] for p in range(2)], axis=0)
     for c in range(chunks):
@@ -154,7 +196,7 @@
         * lax.rsqrt(jnp.mean(wide * wide, axis=-1, keepdims=True) + eps_norm)
         * post_gain_ref[...].reshape(1, wide.shape[1])
     ).astype(bf16)
-    logits = jnp.dot(routed, router_ref[...], preferred_element_type=f32)
+    logits = nt_dot(routed, router_ref[...])
 
     tokens = 2 * rows
     experts = logits.shape[1]
@@ -242,26 +284,7 @@
     slots = expert_total * capacity
     chunks = 4
     params = pltpu.CompilerParams(vmem_limit_bytes=48 * 1024 * 1024)
-    blocks, weights, middle = pl.pallas_call(
-        functools.partial(mixer_kernel, capacity),
-        out_shape=(
-            jax.ShapeDtypeStruct((slots, model_width), bf16),
-            jax.ShapeDtypeStruct((token_count, slots), f32),
-            jax.ShapeDtypeStruct((token_count, model_width), bf16),
-        ),
-        in_specs=vmem(13) + [pl.BlockSpec(memory_space=pl.ANY)] * 2,
-        out_specs=tuple(vmem(3)),
-        scratch_shapes=[
-            pltpu.VMEM((key_heads, row_count, share, key_size, value_size), bf16),
-            pltpu.VMEM(out_proj.shape, bf16),
-            pltpu.VMEM((key_heads, 8 * row_count, key_size), f32),
-            pltpu.VMEM((key_heads, share, 8 * row_count, value_size), f32),
-            pltpu.SemaphoreType.DMA((key_heads,)),
-            pltpu.SemaphoreType.DMA((chunks,)),
-        ],
-        compiler_params=params,
-        name="mixer",
-    )(
+    operands = (
         hidden_in,
         query_in,
         key_in,
@@ -273,11 +296,34 @@
         step_bias,
         norm_gain,
         post_gain,
-        router_weight,
+        router_weight.T,
         expert_ids,
         state_in,
         out_proj,
     )
+    operands = [pltpu.with_memory_space_constraint(x, pltpu.HBM) for x in operands]
+    blocks, weights, middle = pl.pallas_call(
+        functools.partial(mixer_kernel, capacity),
+        out_shape=(
+            jax.ShapeDtypeStruct((slots, model_width), bf16),
+            jax.ShapeDtypeStruct((token_count, slots), f32),
+            jax.ShapeDtypeStruct((token_count, model_width), bf16),
+        ),
+        in_specs=[pl.BlockSpec(memory_space=pltpu.HBM)] * len(operands),
+        out_specs=tuple(vmem(3)),
+        scratch_shapes=[pltpu.VMEM(x.shape, x.dtype) for x in operands[:13]]
+        + [
+            pltpu.VMEM((key_heads, row_count, share, key_size, value_size), bf16),
+            pltpu.VMEM(out_proj.shape, bf16),
+            pltpu.VMEM((key_heads, 8 * row_count, key_size), f32),
+            pltpu.VMEM((key_heads, share, 8 * row_count, value_size), f32),
+            pltpu.SemaphoreType.DMA((13,)),
+            pltpu.SemaphoreType.DMA((key_heads,)),
+            pltpu.SemaphoreType.DMA((chunks,)),
+        ],
+        compiler_params=params,
+        name="mixer",
+    )(*operands)
     received = lax.all_to_all(blocks, "dp", split_axis=0, concat_axis=0, tiled=True)
     produced = pl.pallas_call(
         expert_kernel,

time: 59.6 us -> 48.3 us (0.81)
  local copies, waits for them, and re-layouts: 11.9 us -> 0.01 us
  Pallas kernels: 5.89 us -> 7.06 us
    unnamed x31 -> x4, local copies, waits for them, and re-layouts: 11.9 us -> 0.01 us
    pallas_call x1, Pallas kernels: 4.34 us -> 5.51 us  [shards(): pl.pallas_call(functools.partial(mixer_kernel, capacity), out_shape=(jax....]
where the time goes in v2:
time: 48.3 us; the launch traced here: 48.2 us
  blocking collectives  41.1 us (85%)
  Pallas kernels  7.06 us (15%)
    all_to_all x1, blocking collectives, shards(): lax.all_to_all(blocks, 'dp', split_axis=0, concat_axis=0, tiled=True)  22.7 us
    all_to_all x1, blocking collectives, shards(): lax.all_to_all(produced, 'dp', split_axis=0, concat_axis=0, tiled=True)  18.4 us
    pallas_call x1, Pallas kernels, shards(): pl.pallas_call(functools.partial(mixer_kernel, capacity), out_shape=(jax....  5.51 us

profile of v2, /device:TPU:0, one launch (start us, length us, event | category | flops | bytes accessed | tf_op | source)
XLA Modules:
  0.0 48.2 jit_solution(12716655193123424704)
XLA Ops:
  0.0 0.0 copy-start
  0.0 0.0 copy-start.1
  0.0 5.5 %mixer.1 = (bf16[256,1024]{1,0:T(8,128)(2,1)S(1)}, f32[16,256]{1,0:T(8,128)S(1)}, bf16[16,1024]{1,0:T(8,128)(2,1)S(1)}) custom-call(bf16[8,2,1024]{2,1,0:T(2,128)(2,1)} %hidden_hbm.1, bf16[8,2,1024]{2,1,0:T(2,128)(2,1)} %query_hbm.1, bf16[8,2,1024]{2,1,0:T(2,128)(2,1)} %key_hbm.1, bf16[8,2,2048]{2,1,0:T(2,128)(2,1)} %value_hbm.1, ...), custom_call_target="tpu_custom_call" | custom-call | tf_op jit(solution)/shard_map/mixer/pallas_call | solution.py:305
  5.5 22.7 %all_to_all.22 = bf16[32,8,1024]{2,1,0:T(8,128)(2,1)S(1)} all-to-all(bf16[32,8,1024]{2,1,0:T(8,128)(2,1)S(1)} %bitcast.8), channel_id=1, replica_groups=mesh['groups'=1,'dp'=32] {'dp'}, dimensions={0} | all-to-all | bytes 1048576 | tf_op jit(solution)/shard_map/all_to_all | solution.py:327
  28.2 0.0 copy-done
  28.2 0.0 copy-done.1
  28.2 0.7 %experts.1 = bf16[256,1024]{1,0:T(8,128)(2,1)S(1)} custom-call(bf16[256,1024]{1,0:T(8,128)(2,1)S(1)} %bitcast.5, bf16[1,1024,512]{2,1,0:T(8,128)(2,1)S(1)} %copy-done, bf16[1,256,1024]{2,1,0:T(8,128)(2,1)S(1)} %copy-done.1), custom_call_target="tpu_custom_call" | custom-call | tf_op jit(solution)/shard_map/experts/pallas_call | solution.py:328
  28.9 18.4 %all_to_all.23 = bf16[32,8,1024]{2,1,0:T(8,128)(2,1)S(1)} all-to-all(bf16[32,8,1024]{2,1,0:T(8,128)(2,1)S(1)} %bitcast.6), channel_id=1, replica_groups=mesh['groups'=1,'dp'=32] {'dp'}, dimensions={0} | all-to-all | bytes 1048576 | tf_op jit(solution)/shard_map/all_to_all | solution.py:336
  47.3 0.9 %combine.1 = bf16[8,2,1024]{2,1,0:T(2,128)(2,1)} custom-call(bf16[256,1024]{1,0:T(8,128)(2,1)S(1)} %bitcast.7, f32[16,256]{1,0:T(8,128)S(1)} %get-tuple-element.9.weights_ref, bf16[16,1024]{1,0:T(8,128)(2,1)S(1)} %get-tuple-element.10.middle_ref), custom_call_target="tpu_custom_call" | custom-call | tf_op jit(solution)/shard_map/combine/pallas_call | solution.py:337
Async XLA Ops:
  0.0 28.2 %copy-start = (bf16[1,1024,512]{2,1,0:T(8,128)(2,1)S(1)}, bf16[1,1024,512]{2,1,0:T(8,128)(2,1)}, u32[]{:S(2)}) copy-start(bf16[1,1024,512]{2,1,0:T(8,128)(2,1)} %up_ref.1) | copy-start | bytes 3145732
  0.0 28.2 %copy-start.1 = (bf16[1,256,1024]{2,1,0:T(8,128)(2,1)S(1)}, bf16[1,256,1024]{2,1,0:T(8,128)(2,1)}, u32[]{:S(2)}) copy-start(bf16[1,256,1024]{2,1,0:T(8,128)(2,1)} %down_ref.1) | copy-start | bytes 1572868

commit v3 on v2

--- a/solution.py
+++ b/solution.py
@@ -23,7 +23,6 @@
 
 
 def mixer_kernel(
-    capacity,
     hidden_hbm,
     query_hbm,
     key_hbm,
@@ -39,8 +38,7 @@
     ids_hbm,
     state_hbm,
     proj_hbm,
-    blocks_ref,
-    weights_ref,
+    routed_ref,
     middle_ref,
     hidden_ref,
     query_ref,
@@ -200,51 +198,96 @@
 
     tokens = 2 * rows
     experts = logits.shape[1]
-    slots = experts * capacity
     ids = jnp.concatenate([ids_ref[:, p, :] for p in range(2)], axis=0)
     expert = lax.broadcasted_iota(jnp.int32, (tokens, experts), 1)
     chosen = jnp.zeros((tokens, experts), f32)
     for k in range(ids.shape[1]):
         chosen = chosen + (ids[:, k : k + 1] == expert).astype(f32)
     raised = jnp.where(chosen > 0.0, jnp.exp(logits), 0.0)
-    share_all = raised / jnp.sum(raised, axis=-1, keepdims=True)
-    later = lax.broadcasted_iota(jnp.int32, (tokens, tokens), 0)
-    earlier = lax.broadcasted_iota(jnp.int32, (tokens, tokens), 1)
-    below = (later > earlier).astype(bf16)
-    chosen16 = chosen.astype(bf16)
-    slot = jnp.dot(below, chosen16, preferred_element_type=f32)
-    place = jnp.where(chosen > 0.0, slot, -1.0).astype(bf16)
-    slot_expert = lax.broadcasted_iota(jnp.int32, (slots, experts), 0) // capacity
-    spread = (slot_expert == lax.broadcasted_iota(jnp.int32, (slots, experts), 1)).astype(bf16)
-    number = lax.broadcasted_iota(jnp.int32, (slots, tokens), 0)
-    take = (nt_dot(spread, place) == (number % capacity).astype(f32)).astype(bf16)
-    blocks_ref[...] = jnp.dot(take, routed, preferred_element_type=f32).astype(bf16)
-    lane = lax.broadcasted_iota(jnp.int32, (tokens, slots), 1)
-    match = nt_dot(place, spread) == (lane % capacity).astype(f32)
-    high, low = split_two(share_all)
-    spread_share = nt_dot(high, spread) + nt_dot(low, spread)
-    weights_ref[...] = jnp.where(match, spread_share, 0.0)
-
-
-def expert_kernel(blocks_ref, up_ref, down_ref, out_ref):
-    hidden_units = down_ref.shape[1]
-    both = jnp.dot(blocks_ref[...], up_ref[0], preferred_element_type=f32)
-    g = both[:, :hidden_units]
-    activated = (g / (1.0 + jnp.exp(-g)) * both[:, hidden_units:]).astype(bf16)
-    out_ref[...] = jnp.dot(activated, down_ref[0], preferred_element_type=f32).astype(bf16)
-
-
-def combine_kernel(returned_ref, weights_ref, middle_ref, out_ref):
+    high, low = split_two(raised / jnp.sum(raised, axis=-1, keepdims=True))
+    width = routed.shape[1]
+    extra = routed_ref.shape[1] - width
+    lane = lax.broadcasted_iota(jnp.int32, (experts, extra), 1)
+    number = lax.broadcasted_iota(jnp.int32, (experts, extra), 0)
+    beside = jnp.dot(high, (lane == number).astype(bf16), preferred_element_type=f32)
+    beside += jnp.dot(low, (lane == number + experts).astype(bf16), preferred_element_type=f32)
+    routed_ref[:, :width] = routed
+    routed_ref[:, width:] = beside.astype(bf16)
+
+
+def column_kernel(*refs):
+    out_ref = refs[-1]
+    rows = refs[0].shape[0]
+    for i, ref in enumerate(refs[:-1]):
+        out_ref[i * rows : (i + 1) * rows, :] = ref[...]
+
+
+def expert_sum(rows, width, weights, first, experts):
+    hidden_units = weights[0][1].shape[1]
+    x = rows[:, :width]
+    beside = rows[:, width:].astype(f32)
+    lane = lax.broadcasted_iota(jnp.int32, beside.shape, 1)
+    total = None
+    for (up_ref, down_ref), e in zip(weights, first):
+        both = jnp.dot(x, up_ref[0], preferred_element_type=f32)
+        g = both[:, :hidden_units]
+        activated = (g / (1.0 + jnp.exp(-g)) * both[:, hidden_units:]).astype(bf16)
+        result = jnp.dot(activated, down_ref[0], preferred_element_type=f32).astype(bf16)
+        share = jnp.sum(jnp.where(lane == e, beside, 0.0), axis=-1, keepdims=True)
+        low_lane = lane == e + experts
+        share = share + jnp.sum(jnp.where(low_lane, beside, 0.0), axis=-1, keepdims=True)
+        part = share * result.astype(f32)
+        total = part if total is None else total + part
+    return total
+
+
+def expert_kernel(experts, count, *refs):
+    blocks = refs[:count]
+    up_own, down_own, up_other, down_other = refs[count : count + 4]
+    outs = refs[count + 4 :]
+    width = outs[0].shape[1]
+    me = lax.axis_index("dp")
+    weights = ((up_own, down_own), (up_other, down_other))
+    rows = blocks[0].shape[0]
+    x = blocks[0][...] if count == 1 else jnp.concatenate([b[...] for b in blocks], axis=0)
+    total = expert_sum(x, width, weights, (me, me ^ 1), experts)
+    for i, out in enumerate(outs):
+        out[...] = total[i * rows : (i + 1) * rows].astype(out.dtype)
+
+
+def column_sum_kernel(tokens, *refs):
+    own_ref = refs[0]
+    count = (own_ref.shape[0] // tokens)
+    outs = refs[-count:]
+    total = own_ref[...]
+    for ref in refs[1:-count]:
+        total = total + ref[...].astype(f32)
+    for i, out in enumerate(outs):
+        out[...] = total[i * tokens : (i + 1) * tokens].astype(out.dtype)
+
+
+def final_kernel(*refs):
+    out_ref = refs[-1]
     rows = out_ref.shape[0]
-    high, low = split_two(weights_ref[...])
-    returned = returned_ref[...]
-    total = (
-        middle_ref[...].astype(f32)
-        + jnp.dot(high, returned, preferred_element_type=f32)
-        + jnp.dot(low, returned, preferred_element_type=f32)
-    ).astype(bf16)
+    total = refs[0][...].astype(f32) + refs[1][...]
+    for ref in refs[2:-1]:
+        total = total + ref[...].astype(f32)
+    total = total.astype(bf16)
     for p in range(2):
         out_ref[:, p, :] = total[p * rows : (p + 1) * rows]
+
+
+def chip_masks(device_count):
+    bits = device_count.bit_length() - 2
+    low = bits // 2
+    near = [m << 1 for m in range(1, 1 << low)]
+    far = [m << (1 + low) for m in range(1, 1 << (bits - low))]
+    return near, far
+
+
+def hop(x, mask):
+    count = lax.axis_size("dp")
+    return lax.ppermute(x, "dp", [(i, i ^ mask) for i in range(count)])
 
 
 def vmem(count):
@@ -273,15 +316,12 @@
     device_count = lax.axis_size("dp")
     expert_total = expert_gate_up.shape[0] * device_count
     row_count, _, model_width = hidden_in.shape
-    pick_count = expert_ids.shape[2]
     value_heads, key_size, value_size = state_in.shape[1:]
     key_heads = query_in.shape[2] // key_size
     share = value_heads // key_heads
     token_count = row_count * 2
-    capacity = min(
-        token_count, max(2, (3 * row_count * pick_count + expert_total - 1) // expert_total)
-    )
-    slots = expert_total * capacity
+    sent_width = model_width + (2 * expert_total + 127) // 128 * 128
+    near, far = chip_masks(device_count)
     chunks = 4
     params = pltpu.CompilerParams(vmem_limit_bytes=48 * 1024 * 1024)
     operands = (
@@ -302,15 +342,15 @@
         out_proj,
     )
     operands = [pltpu.with_memory_space_constraint(x, pltpu.HBM) for x in operands]
-    blocks, weights, middle = pl.pallas_call(
-        functools.partial(mixer_kernel, capacity),
+    up_other, down_other = hop(expert_gate_up, 1), hop(expert_down, 1)
+    routed, middle = pl.pallas_call(
+        mixer_kernel,
         out_shape=(
-            jax.ShapeDtypeStruct((slots, model_width), bf16),
-            jax.ShapeDtypeStruct((token_count, slots), f32),
+            jax.ShapeDtypeStruct((token_count, sent_width), bf16),
             jax.ShapeDtypeStruct((token_count, model_width), bf16),
         ),
         in_specs=[pl.BlockSpec(memory_space=pltpu.HBM)] * len(operands),
-        out_specs=tuple(vmem(3)),
+        out_specs=tuple(vmem(2)),
         scratch_shapes=[pltpu.VMEM(x.shape, x.dtype) for x in operands[:13]]
         + [
             pltpu.VMEM((key_heads, row_count, share, key_size, value_size), bf16),
@@ -324,24 +364,49 @@
         compiler_params=params,
         name="mixer",
     )(*operands)
-    received = lax.all_to_all(blocks, "dp", split_axis=0, concat_axis=0, tiled=True)
-    produced = pl.pallas_call(
-        expert_kernel,
-        out_shape=jax.ShapeDtypeStruct((slots, model_width), bf16),
-        in_specs=vmem(3),
-        out_specs=vmem(1)[0],
-        compiler_params=params,
-        name="experts",
-    )(received, expert_gate_up, expert_down)
-    returned = lax.all_to_all(produced, "dp", split_axis=0, concat_axis=0, tiled=True)
-    return pl.pallas_call(
-        combine_kernel,
-        out_shape=jax.ShapeDtypeStruct(hidden_in.shape, bf16),
-        in_specs=vmem(3),
-        out_specs=vmem(1)[0],
-        compiler_params=params,
-        name="combine",
-    )(returned, weights, middle)
+
+    def local(body, name, outs, *args):
+        return pl.pallas_call(
+            body,
+            out_shape=tuple(jax.ShapeDtypeStruct(*o) for o in outs),
+            in_specs=vmem(len(args)),
+            out_specs=tuple(vmem(len(outs))),
+            compiler_params=params,
+            name=name,
+        )(*args)
+
+    weights = (expert_gate_up, expert_down, up_other, down_other)
+    column_rows = token_count * (len(far) + 1)
+    pieces = [hop(routed, m) for m in far]
+    (column,) = local(
+        column_kernel, "column", [((column_rows, sent_width), bf16)], routed, *pieces
+    )
+    columns = [hop(column, m) for m in near]
+    (own,) = local(
+        functools.partial(expert_kernel, expert_total, 1),
+        "own_experts",
+        [((column_rows, model_width), f32)],
+        column,
+        *weights,
+    )
+    results = local(
+        functools.partial(expert_kernel, expert_total, len(near)),
+        "experts",
+        [((column_rows, model_width), bf16)] * len(near),
+        *columns,
+        *weights,
+    )
+    back = [hop(r, m) for r, m in zip(results, near)]
+    mine, *others = local(
+        functools.partial(column_sum_kernel, token_count),
+        "column_sum",
+        [((token_count, model_width), f32)] + [((token_count, model_width), bf16)] * len(far),
+        own,
+        *back,
+    )
+    home = [hop(r, m) for r, m in zip(others, far)]
+    (out,) = local(final_kernel, "final", [(hidden_in.shape, bf16)], middle, mine, *home)
+    return out
 
 
 def solution(mesh):

time: 48.3 us -> 43.5 us (0.901)
  blocking collectives: 41.1 us -> 0 us
  starting transfers between devices: 0 us -> 17.8 us
  waiting for transfers between devices: 0 us -> 17.4 us
  Pallas kernels: 7.06 us -> 8.07 us
    all_to_all x2 -> x0, blocking collectives: 41.1 us -> none  [the longest x1 22.7 us: shards(): lax.all_to_all(blocks, 'dp', split_axis=0, concat_axis=0, tiled=True)]
    ppermute x0 -> x14, starting transfers between devices: none -> 17.8 us  [hop(): return lax.ppermute(x, 'dp', [(i, i ^ mask) for i in range(count)])]
    ppermute x0 -> x14, waiting for transfers between devices: none -> 17.4 us  [hop(): return lax.ppermute(x, 'dp', [(i, i ^ mask) for i in range(count)])]
    pallas_call x3 -> x6, Pallas kernels: 7.06 us -> 8.07 us  [the longest x1 5.47 us: shards(): pl.pallas_call(mixer_kernel, out_shape=(jax.ShapeDtypeStruct((token_count...]
  transfers between devices with their start and end apart: 0 -> 14, of which waited for: 0 -> 9; matrix products, arithmetic and copies ran while one was open for 0% -> 0% of each run, Pallas kernels for 0% -> 15%
where the time goes in v3:
time: 43.5 us; the launch traced here: 43.3 us
  starting transfers between devices  17.8 us (41%)
  waiting for transfers between devices  17.4 us (40%)
  Pallas kernels  8.07 us (19%)
    ppermute x14, starting transfers between devices, hop(): return lax.ppermute(x, 'dp', [(i, i ^ mask) for i in range(count)])  17.8 us
    ppermute x14, waiting for transfers between devices, hop(): return lax.ppermute(x, 'dp', [(i, i ^ mask) for i in range(count)])  17.4 us
    pallas_call x1, Pallas kernels, shards(): pl.pallas_call(mixer_kernel, out_shape=(jax.ShapeDtypeStruct((token_count...  5.47 us
    pallas_call x5, Pallas kernels, local(): pl.pallas_call(body, out_shape=tuple((jax.ShapeDtypeStruct(*o) for o in o...  2.6 us
  transfers between devices with their start and end apart: 14, of which 9 were waited for; matrix products, arithmetic and copies ran while one was open for 0% of the time, Pallas kernels for 15%

profile of v3, /device:TPU:0, one launch (start us, length us, event | category | flops | bytes accessed | tf_op | source)
XLA Modules:
  0.0 43.3 jit_solution(5424563042788107568)
XLA Ops:
  0.0 0.5 %collective-permute-start.3 = (bf16[1,1024,512]{2,1,0:T(8,128)(2,1)}, bf16[1,1024,512]{2,1,0:T(8,128)(2,1)S(1)}, u32[]{:S(2)}, u32[]{:S(2)}) collective-permute-start(bf16[1,1024,512]{2,1,0:T(8,128)(2,1)} %refs_3_.1), channel_id=1, source_target_pairs={{0,1},{1,0},{2,3},{3,2},{4,5},{5,4},{6,7},{7,6},{8,9},{9,8},{10,11... | collective-permute-start | bytes 3145736 | tf_op jit(solution)/shard_map/ppermute | solution.py:290
  0.5 0.1 collective-permute-start.4
  0.5 0.0 copy-start
  0.5 0.0 copy-start.1
  0.5 5.5 %mixer.1 = (bf16[16,1152]{1,0:T(8,128)(2,1)S(1)}, bf16[16,1024]{1,0:T(8,128)(2,1)S(1)}) custom-call(bf16[8,2,1024]{2,1,0:T(2,128)(2,1)} %hidden_hbm.1, bf16[8,2,1024]{2,1,0:T(2,128)(2,1)} %query_hbm.1, bf16[8,2,1024]{2,1,0:T(2,128)(2,1)} %key_hbm.1, bf16[8,2,2048]{2,1,0:T(2,128)(2,1)} %value_hbm.1, bf16[8,2,2048]{2,1,0:T(2,128)(2,1)} %gate_hbm.1, ...), custom_call_target="tpu_custom_call" | custom-call | tf_op jit(solution)/shard_map/mixer/pallas_call | solution.py:346
  6.0 5.1 %collective-permute-start.2 = (bf16[16,1152]{1,0:T(8,128)(2,1)S(1)}, bf16[16,1152]{1,0:T(8,128)(2,1)S(1)}, u32[]{:S(2)}, u32[]{:S(2)}) collective-permute-start(bf16[16,1152]{1,0:T(8,128)(2,1)S(1)} %get-tuple-element.15.refs_0_), channel_id=1, source_target_pairs={{0,24},{1,25},{2,26},{3,27},{4,28},{5,29},{6,30},{7,31},{8,16},{9,... | collective-permute-start | bytes 110600 | tf_op jit(solution)/shard_map/ppermute | solution.py:290
  11.1 0.0 collective-permute-start.1
  11.1 0.6 %collective-permute-start = (bf16[16,1152]{1,0:T(8,128)(2,1)S(1)}, bf16[16,1152]{1,0:T(8,128)(2,1)S(1)}, u32[]{:S(2)}, u32[]{:S(2)}) collective-permute-start(bf16[16,1152]{1,0:T(8,128)(2,1)S(1)} %get-tuple-element.15.refs_0_), channel_id=1, source_target_pairs={{0,8},{1,9},{2,10},{3,11},{4,12},{5,13},{6,14},{7,15},{8,0},{9,1},... | collective-permute-start | bytes 110600 | tf_op jit(solution)/shard_map/ppermute | solution.py:290
  11.7 1.3 %collective-permute-done.2.refs_3_ = bf16[16,1152]{1,0:T(8,128)(2,1)S(1)} collective-permute-done((bf16[16,1152]{1,0:T(8,128)(2,1)S(1)}, bf16[16,1152]{1,0:T(8,128)(2,1)S(1)}, u32[]{:S(2)}, u32[]{:S(2)}) %collective-permute-start.2) | collective-permute-done | bytes 36896 | tf_op jit(solution)/shard_map/ppermute | solution.py:290
  13.1 2.9 %collective-permute-done.1.refs_2_ = bf16[16,1152]{1,0:T(8,128)(2,1)S(1)} collective-permute-done((bf16[16,1152]{1,0:T(8,128)(2,1)S(1)}, bf16[16,1152]{1,0:T(8,128)(2,1)S(1)}, u32[]{:S(2)}, u32[]{:S(2)}) %collective-permute-start.1) | collective-permute-done | bytes 36896 | tf_op jit(solution)/shard_map/ppermute | solution.py:290
  16.0 0.0 collective-permute-done.refs_1_
  16.0 2.5 %collective-permute-start.7 = (bf16[64,1152]{1,0:T(8,128)(2,1)S(1)}, bf16[64,1152]{1,0:T(8,128)(2,1)S(1)}, u32[]{:S(2)}, u32[]{:S(2)}) collective-permute-start(bf16[64,1152]{1,0:T(8,128)(2,1)S(1)} %column.1.refs_0_), channel_id=1, source_target_pairs={{0,6},{1,7},{2,4},{3,5},{4,2},{5,3},{6,0},{7,1},{8,14},{9,15},{10,... | collective-permute-start | bytes 442376 | tf_op jit(solution)/shard_map/ppermute | solution.py:290
  18.5 0.5 %collective-permute-start.6 = (bf16[64,1152]{1,0:T(8,128)(2,1)S(1)}, bf16[64,1152]{1,0:T(8,128)(2,1)S(1)}, u32[]{:S(2)}, u32[]{:S(2)}) collective-permute-start(bf16[64,1152]{1,0:T(8,128)(2,1)S(1)} %column.1.refs_0_), channel_id=1, source_target_pairs={{0,4},{1,5},{2,6},{3,7},{4,0},{5,1},{6,2},{7,3},{8,12},{9,13},{10,... | collective-permute-start | bytes 442376 | tf_op jit(solution)/shard_map/ppermute | solution.py:290
  19.0 0.5 %collective-permute-start.5 = (bf16[64,1152]{1,0:T(8,128)(2,1)S(1)}, bf16[64,1152]{1,0:T(8,128)(2,1)S(1)}, u32[]{:S(2)}, u32[]{:S(2)}) collective-permute-start(bf16[64,1152]{1,0:T(8,128)(2,1)S(1)} %column.1.refs_0_), channel_id=1, source_target_pairs={{0,2},{1,3},{2,0},{3,1},{4,6},{5,7},{6,4},{7,5},{8,10},{9,11},{10,... | collective-permute-start | bytes 442376 | tf_op jit(solution)/shard_map/ppermute | solution.py:290
  19.5 3.7 %collective-permute-done.7.refs_2_ = bf16[64,1152]{1,0:T(8,128)(2,1)S(1)} collective-permute-done((bf16[64,1152]{1,0:T(8,128)(2,1)S(1)}, bf16[64,1152]{1,0:T(8,128)(2,1)S(1)}, u32[]{:S(2)}, u32[]{:S(2)}) %collective-permute-start.7) | collective-permute-done | bytes 147488 | tf_op jit(solution)/shard_map/ppermute | solution.py:290
  23.3 1.6 %collective-permute-done.6.refs_1_ = bf16[64,1152]{1,0:T(8,128)(2,1)S(1)} collective-permute-done((bf16[64,1152]{1,0:T(8,128)(2,1)S(1)}, bf16[64,1152]{1,0:T(8,128)(2,1)S(1)}, u32[]{:S(2)}, u32[]{:S(2)}) %collective-permute-start.6) | collective-permute-done | bytes 147488 | tf_op jit(solution)/shard_map/ppermute | solution.py:290
  24.8 0.1 collective-permute-done.5.refs_0_
  24.9 0.0 collective-permute-done.4.refs_4_.refs_6_
  24.9 0.0 collective-permute-done.3.refs_3_.refs_5_
  24.9 0.0 copy-done
  24.9 0.0 copy-done.1
  24.9 1.0 %experts.1 = (bf16[64,1024]{1,0:T(8,128)(2,1)S(1)}, bf16[64,1024]{1,0:T(8,128)(2,1)S(1)}, bf16[64,1024]{1,0:T(8,128)(2,1)S(1)}) custom-call(bf16[64,1152]{1,0:T(8,128)(2,1)S(1)} %collective-permute-done.5.refs_0_, bf16[64,1152]{1,0:T(8,128)(2,1)S(1)} %collective-permute-done.6.refs_1_, bf16[64,1152]{1,0:T(8,128)(2,1)S(1)} %collective-permute-done.7.refs_2_, ...), custom_call_target="tpu_custom_call" | custom-call | tf_op jit(solution)/shard_map/experts/pallas_call | solution.py:369
  26.0 1.6 %collective-permute-start.8 = (bf16[64,1024]{1,0:T(8,128)(2,1)S(1)}, bf16[64,1024]{1,0:T(8,128)(2,1)S(1)}, u32[]{:S(2)}, u32[]{:S(2)}) collective-permute-start(bf16[64,1024]{1,0:T(8,128)(2,1)S(1)} %get-tuple-element.16), channel_id=1, source_target_pairs={{0,2},{1,3},{2,0},{3,1},{4,6},{5,7},{6,4},{7,5},{8,10},{9,11},{10,... | collective-permute-start | bytes 393224 | tf_op jit(solution)/shard_map/ppermute | solution.py:290
  27.6 0.7 %collective-permute-start.9 = (bf16[64,1024]{1,0:T(8,128)(2,1)S(1)}, bf16[64,1024]{1,0:T(8,128)(2,1)S(1)}, u32[]{:S(2)}, u32[]{:S(2)}) collective-permute-start(bf16[64,1024]{1,0:T(8,128)(2,1)S(1)} %get-tuple-element.17), channel_id=1, source_target_pairs={{0,4},{1,5},{2,6},{3,7},{4,0},{5,1},{6,2},{7,3},{8,12},{9,13},{10,... | collective-permute-start | bytes 393224 | tf_op jit(solution)/shard_map/ppermute | solution.py:290
  28.3 1.2 %collective-permute-start.10 = (bf16[64,1024]{1,0:T(8,128)(2,1)S(1)}, bf16[64,1024]{1,0:T(8,128)(2,1)S(1)}, u32[]{:S(2)}, u32[]{:S(2)}) collective-permute-start(bf16[64,1024]{1,0:T(8,128)(2,1)S(1)} %get-tuple-element.18), channel_id=1, source_target_pairs={{0,6},{1,7},{2,4},{3,5},{4,2},{5,3},{6,0},{7,1},{8,14},{9,15},{10,... | collective-permute-start | bytes 393224 | tf_op jit(solution)/shard_map/ppermute | solution.py:290
  29.5 0.8 %own_experts.1.refs_0_ = f32[64,1024]{1,0:T(8,128)S(1)} custom-call(bf16[64,1152]{1,0:T(8,128)(2,1)S(1)} %column.1.refs_0_, bf16[1,1024,512]{2,1,0:T(8,128)(2,1)S(1)} %copy-done, bf16[1,256,1024]{2,1,0:T(8,128)(2,1)S(1)} %copy-done.1, bf16[1,1024,512]{2,1,0:T(8,128)(2,1)S(1)} %collective-permute-done.3.refs_3_.refs_5_, ...), custom_call_target="tpu_custom_call" | custom-call | tf_op jit(solution)/shard_map/own_experts/pallas_call | solution.py:369
  30.4 1.4 %collective-permute-done.8.refs_1_ = bf16[64,1024]{1,0:T(8,128)(2,1)S(1)} collective-permute-done((bf16[64,1024]{1,0:T(8,128)(2,1)S(1)}, bf16[64,1024]{1,0:T(8,128)(2,1)S(1)}, u32[]{:S(2)}, u32[]{:S(2)}) %collective-permute-start.8) | collective-permute-done | bytes 131104 | tf_op jit(solution)/shard_map/ppermute | solution.py:290
  31.8 3.0 %collective-permute-done.9.refs_2_ = bf16[64,1024]{1,0:T(8,128)(2,1)S(1)} collective-permute-done((bf16[64,1024]{1,0:T(8,128)(2,1)S(1)}, bf16[64,1024]{1,0:T(8,128)(2,1)S(1)}, u32[]{:S(2)}, u32[]{:S(2)}) %collective-permute-start.9) | collective-permute-done | bytes 131104 | tf_op jit(solution)/shard_map/ppermute | solution.py:290
  34.8 0.0 collective-permute-done.10.refs_3_
  34.8 0.1 column_sum.1
  34.8 0.5 %collective-permute-start.11 = (bf16[16,1024]{1,0:T(8,128)(2,1)S(1)}, bf16[16,1024]{1,0:T(8,128)(2,1)S(1)}, u32[]{:S(2)}, u32[]{:S(2)}) collective-permute-start(bf16[16,1024]{1,0:T(8,128)(2,1)S(1)} %get-tuple-element.20), channel_id=1, source_target_pairs={{0,8},{1,9},{2,10},{3,11},{4,12},{5,13},{6,14},{7,15},{8,0},{9,1},... | collective-permute-start | bytes 98312 | tf_op jit(solution)/shard_map/ppermute | solution.py:290
  35.4 1.6 %collective-permute-start.12 = (bf16[16,1024]{1,0:T(8,128)(2,1)S(1)}, bf16[16,1024]{1,0:T(8,128)(2,1)S(1)}, u32[]{:S(2)}, u32[]{:S(2)}) collective-permute-start(bf16[16,1024]{1,0:T(8,128)(2,1)S(1)} %get-tuple-element.21), channel_id=1, source_target_pairs={{0,16},{1,17},{2,18},{3,19},{4,20},{5,21},{6,22},{7,23},{8,24},{9,... | collective-permute-start | bytes 98312 | tf_op jit(solution)/shard_map/ppermute | solution.py:290
  37.0 2.3 %collective-permute-start.13 = (bf16[16,1024]{1,0:T(8,128)(2,1)S(1)}, bf16[16,1024]{1,0:T(8,128)(2,1)S(1)}, u32[]{:S(2)}, u32[]{:S(2)}) collective-permute-start(bf16[16,1024]{1,0:T(8,128)(2,1)S(1)} %get-tuple-element.22), channel_id=1, source_target_pairs={{0,24},{1,25},{2,26},{3,27},{4,28},{5,29},{6,30},{7,31},{8,16},{9,... | collective-permute-start | bytes 98312 | tf_op jit(solution)/shard_map/ppermute | solution.py:290
  39.3 0.0 collective-permute-done.11.refs_2_
  39.3 0.9 %collective-permute-done.12.refs_3_ = bf16[16,1024]{1,0:T(8,128)(2,1)S(1)} collective-permute-done((bf16[16,1024]{1,0:T(8,128)(2,1)S(1)}, bf16[16,1024]{1,0:T(8,128)(2,1)S(1)}, u32[]{:S(2)}, u32[]{:S(2)}) %collective-permute-start.12) | collective-permute-done | bytes 32800 | tf_op jit(solution)/shard_map/ppermute | solution.py:290
  40.2 2.5 %collective-permute-done.13.refs_4_ = bf16[16,1024]{1,0:T(8,128)(2,1)S(1)} collective-permute-done((bf16[16,1024]{1,0:T(8,128)(2,1)S(1)}, bf16[16,1024]{1,0:T(8,128)(2,1)S(1)}, u32[]{:S(2)}, u32[]{:S(2)}) %collective-permute-start.13) | collective-permute-done | bytes 32800 | tf_op jit(solution)/shard_map/ppermute | solution.py:290
  42.7 0.7 %final.1 = bf16[8,2,1024]{2,1,0:T(2,128)(2,1)} custom-call(bf16[16,1024]{1,0:T(8,128)(2,1)S(1)} %get-tuple-element.14.refs_0_, f32[16,1024]{1,0:T(8,128)S(1)} %get-tuple-element.19.refs_1_, bf16[16,1024]{1,0:T(8,128)(2,1)S(1)} %collective-permute-done.11.refs_2_, bf16[16,1024]{1,0:T(8,128)(2,1)S(1)} %collective-permute-done.12.refs_3_, ...), custom_call_target="tpu_custom_call" | custom-call | tf_op jit(solution)/shard_map/final/pallas_call | solution.py:369
  (1 shorter events, 0.0 us)
Async XLA Ops:
  0.0 24.9 %collective-permute-start.3 = (bf16[1,1024,512]{2,1,0:T(8,128)(2,1)}, bf16[1,1024,512]{2,1,0:T(8,128)(2,1)S(1)}, u32[]{:S(2)}, u32[]{:S(2)}) collective-permute-start(bf16[1,1024,512]{2,1,0:T(8,128)(2,1)} %refs_3_.1), channel_id=1, source_target_pairs={{0,1},{1,0},{2,3},{3,2},{4,5},{5,4},{6,7},{7,6},{8,9},{9,8},{10,11... | collective-permute-start | bytes 3145736 | tf_op jit(solution)/shard_map/ppermute | solution.py:290
  0.5 24.5 %collective-permute-start.4 = (bf16[1,256,1024]{2,1,0:T(8,128)(2,1)}, bf16[1,256,1024]{2,1,0:T(8,128)(2,1)S(1)}, u32[]{:S(2)}, u32[]{:S(2)}) collective-permute-start(bf16[1,256,1024]{2,1,0:T(8,128)(2,1)} %refs_4_.1), channel_id=1, source_target_pairs={{0,1},{1,0},{2,3},{3,2},{4,5},{5,4},{6,7},{7,6},{8,9},{9,8},{10,11... | collective-permute-start | bytes 1572872 | tf_op jit(solution)/shard_map/ppermute | solution.py:290
  0.5 24.4 %copy-start = (bf16[1,1024,512]{2,1,0:T(8,128)(2,1)S(1)}, bf16[1,1024,512]{2,1,0:T(8,128)(2,1)}, u32[]{:S(2)}) copy-start(bf16[1,1024,512]{2,1,0:T(8,128)(2,1)} %refs_3_.1) | copy-start | bytes 3145732
  0.5 24.4 %copy-start.1 = (bf16[1,256,1024]{2,1,0:T(8,128)(2,1)S(1)}, bf16[1,256,1024]{2,1,0:T(8,128)(2,1)}, u32[]{:S(2)}) copy-start(bf16[1,256,1024]{2,1,0:T(8,128)(2,1)} %refs_4_.1) | copy-start | bytes 1572868
  6.0 7.1 %collective-permute-start.2 = (bf16[16,1152]{1,0:T(8,128)(2,1)S(1)}, bf16[16,1152]{1,0:T(8,128)(2,1)S(1)}, u32[]{:S(2)}, u32[]{:S(2)}) collective-permute-start(bf16[16,1152]{1,0:T(8,128)(2,1)S(1)} %get-tuple-element.15.refs_0_), channel_id=1, source_target_pairs={{0,24},{1,25},{2,26},{3,27},{4,28},{5,29},{6,30},{7,31},{8,16},{9,... | collective-permute-start | bytes 110600 | tf_op jit(solution)/shard_map/ppermute | solution.py:290
  11.1 4.9 %collective-permute-start.1 = (bf16[16,1152]{1,0:T(8,128)(2,1)S(1)}, bf16[16,1152]{1,0:T(8,128)(2,1)S(1)}, u32[]{:S(2)}, u32[]{:S(2)}) collective-permute-start(bf16[16,1152]{1,0:T(8,128)(2,1)S(1)} %get-tuple-element.15.refs_0_), channel_id=1, source_target_pairs={{0,16},{1,17},{2,18},{3,19},{4,20},{5,21},{6,22},{7,23},{8,24},{9,... | collective-permute-start | bytes 110600 | tf_op jit(solution)/shard_map/ppermute | solution.py:290
  11.1 4.9 %collective-permute-start = (bf16[16,1152]{1,0:T(8,128)(2,1)S(1)}, bf16[16,1152]{1,0:T(8,128)(2,1)S(1)}, u32[]{:S(2)}, u32[]{:S(2)}) collective-permute-start(bf16[16,1152]{1,0:T(8,128)(2,1)S(1)} %get-tuple-element.15.refs_0_), channel_id=1, source_target_pairs={{0,8},{1,9},{2,10},{3,11},{4,12},{5,13},{6,14},{7,15},{8,0},{9,1},... | collective-permute-start | bytes 110600 | tf_op jit(solution)/shard_map/ppermute | solution.py:290
  16.0 7.3 %collective-permute-start.7 = (bf16[64,1152]{1,0:T(8,128)(2,1)S(1)}, bf16[64,1152]{1,0:T(8,128)(2,1)S(1)}, u32[]{:S(2)}, u32[]{:S(2)}) collective-permute-start(bf16[64,1152]{1,0:T(8,128)(2,1)S(1)} %column.1.refs_0_), channel_id=1, source_target_pairs={{0,6},{1,7},{2,4},{3,5},{4,2},{5,3},{6,0},{7,1},{8,14},{9,15},{10,... | collective-permute-start | bytes 442376 | tf_op jit(solution)/shard_map/ppermute | solution.py:290
  18.5 6.3 %collective-permute-start.6 = (bf16[64,1152]{1,0:T(8,128)(2,1)S(1)}, bf16[64,1152]{1,0:T(8,128)(2,1)S(1)}, u32[]{:S(2)}, u32[]{:S(2)}) collective-permute-start(bf16[64,1152]{1,0:T(8,128)(2,1)S(1)} %column.1.refs_0_), channel_id=1, source_target_pairs={{0,4},{1,5},{2,6},{3,7},{4,0},{5,1},{6,2},{7,3},{8,12},{9,13},{10,... | collective-permute-start | bytes 442376 | tf_op jit(solution)/shard_map/ppermute | solution.py:290
  19.0 5.9 %collective-permute-start.5 = (bf16[64,1152]{1,0:T(8,128)(2,1)S(1)}, bf16[64,1152]{1,0:T(8,128)(2,1)S(1)}, u32[]{:S(2)}, u32[]{:S(2)}) collective-permute-start(bf16[64,1152]{1,0:T(8,128)(2,1)S(1)} %column.1.refs_0_), channel_id=1, source_target_pairs={{0,2},{1,3},{2,0},{3,1},{4,6},{5,7},{6,4},{7,5},{8,10},{9,11},{10,... | collective-permute-start | bytes 442376 | tf_op jit(solution)/shard_map/ppermute | solution.py:290
  26.0 5.8 %collective-permute-start.8 = (bf16[64,1024]{1,0:T(8,128)(2,1)S(1)}, bf16[64,1024]{1,0:T(8,128)(2,1)S(1)}, u32[]{:S(2)}, u32[]{:S(2)}) collective-permute-start(bf16[64,1024]{1,0:T(8,128)(2,1)S(1)} %get-tuple-element.16), channel_id=1, source_target_pairs={{0,2},{1,3},{2,0},{3,1},{4,6},{5,7},{6,4},{7,5},{8,10},{9,11},{10,... | collective-permute-start | bytes 393224 | tf_op jit(solution)/shard_map/ppermute | solution.py:290
  27.6 7.2 %collective-permute-start.9 = (bf16[64,1024]{1,0:T(8,128)(2,1)S(1)}, bf16[64,1024]{1,0:T(8,128)(2,1)S(1)}, u32[]{:S(2)}, u32[]{:S(2)}) collective-permute-start(bf16[64,1024]{1,0:T(8,128)(2,1)S(1)} %get-tuple-element.17), channel_id=1, source_target_pairs={{0,4},{1,5},{2,6},{3,7},{4,0},{5,1},{6,2},{7,3},{8,12},{9,13},{10,... | collective-permute-start | bytes 393224 | tf_op jit(solution)/shard_map/ppermute | solution.py:290
  28.3 6.5 %collective-permute-start.10 = (bf16[64,1024]{1,0:T(8,128)(2,1)S(1)}, bf16[64,1024]{1,0:T(8,128)(2,1)S(1)}, u32[]{:S(2)}, u32[]{:S(2)}) collective-permute-start(bf16[64,1024]{1,0:T(8,128)(2,1)S(1)} %get-tuple-element.18), channel_id=1, source_target_pairs={{0,6},{1,7},{2,4},{3,5},{4,2},{5,3},{6,0},{7,1},{8,14},{9,15},{10,... | collective-permute-start | bytes 393224 | tf_op jit(solution)/shard_map/ppermute | solution.py:290
  34.8 4.5 %collective-permute-start.11 = (bf16[16,1024]{1,0:T(8,128)(2,1)S(1)}, bf16[16,1024]{1,0:T(8,128)(2,1)S(1)}, u32[]{:S(2)}, u32[]{:S(2)}) collective-permute-start(bf16[16,1024]{1,0:T(8,128)(2,1)S(1)} %get-tuple-element.20), channel_id=1, source_target_pairs={{0,8},{1,9},{2,10},{3,11},{4,12},{5,13},{6,14},{7,15},{8,0},{9,1},... | collective-permute-start | bytes 98312 | tf_op jit(solution)/shard_map/ppermute | solution.py:290
  35.4 4.8 %collective-permute-start.12 = (bf16[16,1024]{1,0:T(8,128)(2,1)S(1)}, bf16[16,1024]{1,0:T(8,128)(2,1)S(1)}, u32[]{:S(2)}, u32[]{:S(2)}) collective-permute-start(bf16[16,1024]{1,0:T(8,128)(2,1)S(1)} %get-tuple-element.21), channel_id=1, source_target_pairs={{0,16},{1,17},{2,18},{3,19},{4,20},{5,21},{6,22},{7,23},{8,24},{9,... | collective-permute-start | bytes 98312 | tf_op jit(solution)/shard_map/ppermute | solution.py:290
  37.0 5.7 %collective-permute-start.13 = (bf16[16,1024]{1,0:T(8,128)(2,1)S(1)}, bf16[16,1024]{1,0:T(8,128)(2,1)S(1)}, u32[]{:S(2)}, u32[]{:S(2)}) collective-permute-start(bf16[16,1024]{1,0:T(8,128)(2,1)S(1)} %get-tuple-element.22), channel_id=1, source_target_pairs={{0,24},{1,25},{2,26},{3,27},{4,28},{5,29},{6,30},{7,31},{8,16},{9,... | collective-permute-start | bytes 98312 | tf_op jit(solution)/shard_map/ppermute | solution.py:290

commit v4 on v3

--- a/solution.py
+++ b/solution.py
@@ -282,12 +282,14 @@
     low = bits // 2
     near = [m << 1 for m in range(1, 1 << low)]
     far = [m << (1 + low) for m in range(1, 1 << (bits - low))]
-    return near, far
-
-
-def hop(x, mask):
+    if len(near) != len(far):
+        return list(zip(far, far)), list(zip(near, near))
+    return list(zip(far, near)), list(zip(near, far))
+
+
+def hop(x, masks):
     count = lax.axis_size("dp")
-    return lax.ppermute(x, "dp", [(i, i ^ mask) for i in range(count)])
+    return lax.ppermute(x, "dp", [(i, i ^ masks[i % 2]) for i in range(count)])
 
 
 def vmem(count):
@@ -321,7 +323,7 @@
     share = value_heads // key_heads
     token_count = row_count * 2
     sent_width = model_width + (2 * expert_total + 127) // 128 * 128
-    near, far = chip_masks(device_count)
+    first, second = chip_masks(device_count)
     chunks = 4
     params = pltpu.CompilerParams(vmem_limit_bytes=48 * 1024 * 1024)
     operands = (
@@ -342,7 +344,7 @@
         out_proj,
     )
     operands = [pltpu.with_memory_space_constraint(x, pltpu.HBM) for x in operands]
-    up_other, down_other = hop(expert_gate_up, 1), hop(expert_down, 1)
+    up_other, down_other = hop(expert_gate_up, (1, 1)), hop(expert_down, (1, 1))
     routed, middle = pl.pallas_call(
         mixer_kernel,
         out_shape=(
@@ -376,12 +378,12 @@
         )(*args)
 
     weights = (expert_gate_up, expert_down, up_other, down_other)
-    column_rows = token_count * (len(far) + 1)
-    pieces = [hop(routed, m) for m in far]
+    column_rows = token_count * (len(first) + 1)
+    pieces = [hop(routed, m) for m in first]
     (column,) = local(
         column_kernel, "column", [((column_rows, sent_width), bf16)], routed, *pieces
     )
-    columns = [hop(column, m) for m in near]
+    columns = [hop(column, m) for m in second]
     (own,) = local(
         functools.partial(expert_kernel, expert_total, 1),
         "own_experts",
@@ -390,21 +392,21 @@
         *weights,
     )
     results = local(
-        functools.partial(expert_kernel, expert_total, len(near)),
+        functools.partial(expert_kernel, expert_total, len(second)),
         "experts",
-        [((column_rows, model_width), bf16)] * len(near),
+        [((column_rows, model_width), bf16)] * len(second),
         *columns,
         *weights,
     )
-    back = [hop(r, m) for r, m in zip(results, near)]
+    back = [hop(r, m) for r, m in zip(results[::-1], second[::-1])]
     mine, *others = local(
         functools.partial(column_sum_kernel, token_count),
         "column_sum",
-        [((token_count, model_width), f32)] + [((token_count, model_width), bf16)] * len(far),
+        [((token_count, model_width), f32)] + [((token_count, model_width), bf16)] * len(first),
         own,
         *back,
     )
-    home = [hop(r, m) for r, m in zip(others, far)]
+    home = [hop(r, m) for r, m in zip(others[::-1], first[::-1])]
     (out,) = local(final_kernel, "final", [(hidden_in.shape, bf16)], middle, mine, *home)
     return out
 

time: 43.5 us -> 40.6 us (0.933)
  waiting for transfers between devices: 17.4 us -> 14.5 us
    ppermute x14, waiting for transfers between devices: 17.4 us -> 14.5 us  [hop(): return lax.ppermute(x, 'dp', [(i, i ^ masks[i % 2]) for i in range(count)])]
  transfers between devices with their start and end apart: 14 -> 14, of which waited for: 9 -> 11; matrix products, arithmetic and copies ran while one was open for 0% -> 0% of each run, Pallas kernels for 15% -> 16%
where the time goes in v4:
time: 40.6 us; the launch traced here: 40.4 us
  starting transfers between devices  17.8 us (44%)
  waiting for transfers between devices  14.5 us (36%)
  Pallas kernels  8.06 us (20%)
    ppermute x14, starting transfers between devices, hop(): return lax.ppermute(x, 'dp', [(i, i ^ masks[i % 2]) for i in range(count)])  17.8 us
    ppermute x14, waiting for transfers between devices, hop(): return lax.ppermute(x, 'dp', [(i, i ^ masks[i % 2]) for i in range(count)])  14.5 us
    pallas_call x1, Pallas kernels, shards(): pl.pallas_call(mixer_kernel, out_shape=(jax.ShapeDtypeStruct((token_count...  5.47 us
    pallas_call x5, Pallas kernels, local(): pl.pallas_call(body, out_shape=tuple((jax.ShapeDtypeStruct(*o) for o in o...  2.6 us
  transfers between devices with their start and end apart: 14, of which 11 were waited for; matrix products, arithmetic and copies ran while one was open for 0% of the time, Pallas kernels for 16%

profile of v4, /device:TPU:0, one launch (start us, length us, event | category | flops | bytes accessed | tf_op | source)
XLA Modules:
  0.0 40.4 jit_solution(12073225373399565244)
XLA Ops:
  0.0 0.5 %collective-permute-start.3 = (bf16[1,1024,512]{2,1,0:T(8,128)(2,1)}, bf16[1,1024,512]{2,1,0:T(8,128)(2,1)S(1)}, u32[]{:S(2)}, u32[]{:S(2)}) collective-permute-start(bf16[1,1024,512]{2,1,0:T(8,128)(2,1)} %refs_3_.1), channel_id=1, source_target_pairs={{0,1},{1,0},{2,3},{3,2},{4,5},{5,4},{6,7},{7,6},{8,9},{9,8},{10,11... | collective-permute-start | bytes 3145736 | tf_op jit(solution)/shard_map/ppermute | solution.py:292
  0.5 0.1 collective-permute-start.4
  0.5 0.0 copy-start
  0.5 0.0 copy-start.1
  0.5 5.5 %mixer.1 = (bf16[16,1152]{1,0:T(8,128)(2,1)S(1)}, bf16[16,1024]{1,0:T(8,128)(2,1)S(1)}) custom-call(bf16[8,2,1024]{2,1,0:T(2,128)(2,1)} %hidden_hbm.1, bf16[8,2,1024]{2,1,0:T(2,128)(2,1)} %query_hbm.1, bf16[8,2,1024]{2,1,0:T(2,128)(2,1)} %key_hbm.1, bf16[8,2,2048]{2,1,0:T(2,128)(2,1)} %value_hbm.1, bf16[8,2,2048]{2,1,0:T(2,128)(2,1)} %gate_hbm.1, ...), custom_call_target="tpu_custom_call" | custom-call | tf_op jit(solution)/shard_map/mixer/pallas_call | solution.py:348
  6.0 5.1 %collective-permute-start.2 = (bf16[16,1152]{1,0:T(8,128)(2,1)S(1)}, bf16[16,1152]{1,0:T(8,128)(2,1)S(1)}, u32[]{:S(2)}, u32[]{:S(2)}) collective-permute-start(bf16[16,1152]{1,0:T(8,128)(2,1)S(1)} %get-tuple-element.15.refs_0_), channel_id=1, source_target_pairs={{0,24},{1,7},{2,26},{3,5},{4,28},{5,3},{6,30},{7,1},{8,16},{9,15},... | collective-permute-start | bytes 110600 | tf_op jit(solution)/shard_map/ppermute | solution.py:292
  11.1 0.0 collective-permute-start.1
  11.1 0.6 %collective-permute-start = (bf16[16,1152]{1,0:T(8,128)(2,1)S(1)}, bf16[16,1152]{1,0:T(8,128)(2,1)S(1)}, u32[]{:S(2)}, u32[]{:S(2)}) collective-permute-start(bf16[16,1152]{1,0:T(8,128)(2,1)S(1)} %get-tuple-element.15.refs_0_), channel_id=1, source_target_pairs={{0,8},{1,3},{2,10},{3,1},{4,12},{5,7},{6,14},{7,5},{8,0},{9,11},{1... | collective-permute-start | bytes 110600 | tf_op jit(solution)/shard_map/ppermute | solution.py:292
  11.7 1.3 %collective-permute-done.2.refs_3_ = bf16[16,1152]{1,0:T(8,128)(2,1)S(1)} collective-permute-done((bf16[16,1152]{1,0:T(8,128)(2,1)S(1)}, bf16[16,1152]{1,0:T(8,128)(2,1)S(1)}, u32[]{:S(2)}, u32[]{:S(2)}) %collective-permute-start.2) | collective-permute-done | bytes 36896 | tf_op jit(solution)/shard_map/ppermute | solution.py:292
  13.0 2.9 %collective-permute-done.1.refs_2_ = bf16[16,1152]{1,0:T(8,128)(2,1)S(1)} collective-permute-done((bf16[16,1152]{1,0:T(8,128)(2,1)S(1)}, bf16[16,1152]{1,0:T(8,128)(2,1)S(1)}, u32[]{:S(2)}, u32[]{:S(2)}) %collective-permute-start.1) | collective-permute-done | bytes 36896 | tf_op jit(solution)/shard_map/ppermute | solution.py:292
  16.0 0.0 collective-permute-done.refs_1_
  16.0 2.9 %collective-permute-start.7 = (bf16[64,1152]{1,0:T(8,128)(2,1)S(1)}, bf16[64,1152]{1,0:T(8,128)(2,1)S(1)}, u32[]{:S(2)}, u32[]{:S(2)}) collective-permute-start(bf16[64,1152]{1,0:T(8,128)(2,1)S(1)} %column.1.refs_0_), channel_id=1, source_target_pairs={{0,6},{1,25},{2,4},{3,27},{4,2},{5,29},{6,0},{7,31},{8,14},{9,17},... | collective-permute-start | bytes 442376 | tf_op jit(solution)/shard_map/ppermute | solution.py:292
  18.9 0.5 %collective-permute-start.6 = (bf16[64,1152]{1,0:T(8,128)(2,1)S(1)}, bf16[64,1152]{1,0:T(8,128)(2,1)S(1)}, u32[]{:S(2)}, u32[]{:S(2)}) collective-permute-start(bf16[64,1152]{1,0:T(8,128)(2,1)S(1)} %column.1.refs_0_), channel_id=1, source_target_pairs={{0,4},{1,17},{2,6},{3,19},{4,0},{5,21},{6,2},{7,23},{8,12},{9,25},... | collective-permute-start | bytes 442376 | tf_op jit(solution)/shard_map/ppermute | solution.py:292
  19.4 0.1 collective-permute-start.5
  19.5 2.5 %collective-permute-done.7.refs_2_ = bf16[64,1152]{1,0:T(8,128)(2,1)S(1)} collective-permute-done((bf16[64,1152]{1,0:T(8,128)(2,1)S(1)}, bf16[64,1152]{1,0:T(8,128)(2,1)S(1)}, u32[]{:S(2)}, u32[]{:S(2)}) %collective-permute-start.7) | collective-permute-done | bytes 147488 | tf_op jit(solution)/shard_map/ppermute | solution.py:292
  22.1 2.0 %collective-permute-done.6.refs_1_ = bf16[64,1152]{1,0:T(8,128)(2,1)S(1)} collective-permute-done((bf16[64,1152]{1,0:T(8,128)(2,1)S(1)}, bf16[64,1152]{1,0:T(8,128)(2,1)S(1)}, u32[]{:S(2)}, u32[]{:S(2)}) %collective-permute-start.6) | collective-permute-done | bytes 147488 | tf_op jit(solution)/shard_map/ppermute | solution.py:292
  24.0 0.5 %collective-permute-done.5.refs_0_ = bf16[64,1152]{1,0:T(8,128)(2,1)S(1)} collective-permute-done((bf16[64,1152]{1,0:T(8,128)(2,1)S(1)}, bf16[64,1152]{1,0:T(8,128)(2,1)S(1)}, u32[]{:S(2)}, u32[]{:S(2)}) %collective-permute-start.5) | collective-permute-done | bytes 147488 | tf_op jit(solution)/shard_map/ppermute | solution.py:292
  24.6 0.0 collective-permute-done.4.refs_4_.refs_6_
  24.6 0.0 collective-permute-done.3.refs_3_.refs_5_
  24.6 0.0 copy-done
  24.6 0.0 copy-done.1
  24.6 1.0 %experts.1 = (bf16[64,1024]{1,0:T(8,128)(2,1)S(1)}, bf16[64,1024]{1,0:T(8,128)(2,1)S(1)}, bf16[64,1024]{1,0:T(8,128)(2,1)S(1)}) custom-call(bf16[64,1152]{1,0:T(8,128)(2,1)S(1)} %collective-permute-done.5.refs_0_, bf16[64,1152]{1,0:T(8,128)(2,1)S(1)} %collective-permute-done.6.refs_1_, bf16[64,1152]{1,0:T(8,128)(2,1)S(1)} %collective-permute-done.7.refs_2_, ...), custom_call_target="tpu_custom_call" | custom-call | tf_op jit(solution)/shard_map/experts/pallas_call | solution.py:371
  25.6 1.2 %collective-permute-start.8 = (bf16[64,1024]{1,0:T(8,128)(2,1)S(1)}, bf16[64,1024]{1,0:T(8,128)(2,1)S(1)}, u32[]{:S(2)}, u32[]{:S(2)}) collective-permute-start(bf16[64,1024]{1,0:T(8,128)(2,1)S(1)} %get-tuple-element.16), channel_id=1, source_target_pairs={{0,6},{1,25},{2,4},{3,27},{4,2},{5,29},{6,0},{7,31},{8,14},{9,17},... | collective-permute-start | bytes 393224 | tf_op jit(solution)/shard_map/ppermute | solution.py:292
  26.9 1.4 %collective-permute-start.9 = (bf16[64,1024]{1,0:T(8,128)(2,1)S(1)}, bf16[64,1024]{1,0:T(8,128)(2,1)S(1)}, u32[]{:S(2)}, u32[]{:S(2)}) collective-permute-start(bf16[64,1024]{1,0:T(8,128)(2,1)S(1)} %get-tuple-element.17), channel_id=1, source_target_pairs={{0,4},{1,17},{2,6},{3,19},{4,0},{5,21},{6,2},{7,23},{8,12},{9,25},... | collective-permute-start | bytes 393224 | tf_op jit(solution)/shard_map/ppermute | solution.py:292
  28.3 0.9 %collective-permute-start.10 = (bf16[64,1024]{1,0:T(8,128)(2,1)S(1)}, bf16[64,1024]{1,0:T(8,128)(2,1)S(1)}, u32[]{:S(2)}, u32[]{:S(2)}) collective-permute-start(bf16[64,1024]{1,0:T(8,128)(2,1)S(1)} %get-tuple-element.18), channel_id=1, source_target_pairs={{0,2},{1,9},{2,0},{3,11},{4,6},{5,13},{6,4},{7,15},{8,10},{9,1},{1... | collective-permute-start | bytes 393224 | tf_op jit(solution)/shard_map/ppermute | solution.py:292
  29.2 0.8 %own_experts.1.refs_0_ = f32[64,1024]{1,0:T(8,128)S(1)} custom-call(bf16[64,1152]{1,0:T(8,128)(2,1)S(1)} %column.1.refs_0_, bf16[1,1024,512]{2,1,0:T(8,128)(2,1)S(1)} %copy-done, bf16[1,256,1024]{2,1,0:T(8,128)(2,1)S(1)} %copy-done.1, bf16[1,1024,512]{2,1,0:T(8,128)(2,1)S(1)} %collective-permute-done.3.refs_3_.refs_5_, ...), custom_call_target="tpu_custom_call" | custom-call | tf_op jit(solution)/shard_map/own_experts/pallas_call | solution.py:371
  30.0 1.6 %collective-permute-done.8.refs_1_ = bf16[64,1024]{1,0:T(8,128)(2,1)S(1)} collective-permute-done((bf16[64,1024]{1,0:T(8,128)(2,1)S(1)}, bf16[64,1024]{1,0:T(8,128)(2,1)S(1)}, u32[]{:S(2)}, u32[]{:S(2)}) %collective-permute-start.8) | collective-permute-done | bytes 131104 | tf_op jit(solution)/shard_map/ppermute | solution.py:292
  31.7 1.3 %collective-permute-done.9.refs_2_ = bf16[64,1024]{1,0:T(8,128)(2,1)S(1)} collective-permute-done((bf16[64,1024]{1,0:T(8,128)(2,1)S(1)}, bf16[64,1024]{1,0:T(8,128)(2,1)S(1)}, u32[]{:S(2)}, u32[]{:S(2)}) %collective-permute-start.9) | collective-permute-done | bytes 131104 | tf_op jit(solution)/shard_map/ppermute | solution.py:292
  33.0 0.3 collective-permute-done.10.refs_3_
  33.2 0.1 column_sum.1
  33.3 1.1 %collective-permute-start.11 = (bf16[16,1024]{1,0:T(8,128)(2,1)S(1)}, bf16[16,1024]{1,0:T(8,128)(2,1)S(1)}, u32[]{:S(2)}, u32[]{:S(2)}) collective-permute-start(bf16[16,1024]{1,0:T(8,128)(2,1)S(1)} %get-tuple-element.20), channel_id=1, source_target_pairs={{0,24},{1,7},{2,26},{3,5},{4,28},{5,3},{6,30},{7,1},{8,16},{9,15},... | collective-permute-start | bytes 98312 | tf_op jit(solution)/shard_map/ppermute | solution.py:292
  34.4 1.0 %collective-permute-start.12 = (bf16[16,1024]{1,0:T(8,128)(2,1)S(1)}, bf16[16,1024]{1,0:T(8,128)(2,1)S(1)}, u32[]{:S(2)}, u32[]{:S(2)}) collective-permute-start(bf16[16,1024]{1,0:T(8,128)(2,1)S(1)} %get-tuple-element.21), channel_id=1, source_target_pairs={{0,16},{1,5},{2,18},{3,7},{4,20},{5,1},{6,22},{7,3},{8,24},{9,13},... | collective-permute-start | bytes 98312 | tf_op jit(solution)/shard_map/ppermute | solution.py:292
  35.4 2.3 %collective-permute-start.13 = (bf16[16,1024]{1,0:T(8,128)(2,1)S(1)}, bf16[16,1024]{1,0:T(8,128)(2,1)S(1)}, u32[]{:S(2)}, u32[]{:S(2)}) collective-permute-start(bf16[16,1024]{1,0:T(8,128)(2,1)S(1)} %get-tuple-element.22), channel_id=1, source_target_pairs={{0,8},{1,3},{2,10},{3,1},{4,12},{5,7},{6,14},{7,5},{8,0},{9,11},{1... | collective-permute-start | bytes 98312 | tf_op jit(solution)/shard_map/ppermute | solution.py:292
  37.8 1.3 %collective-permute-done.11.refs_2_ = bf16[16,1024]{1,0:T(8,128)(2,1)S(1)} collective-permute-done((bf16[16,1024]{1,0:T(8,128)(2,1)S(1)}, bf16[16,1024]{1,0:T(8,128)(2,1)S(1)}, u32[]{:S(2)}, u32[]{:S(2)}) %collective-permute-start.11) | collective-permute-done | bytes 32800 | tf_op jit(solution)/shard_map/ppermute | solution.py:292
  39.1 0.3 collective-permute-done.12.refs_3_
  39.4 0.3 collective-permute-done.13.refs_4_
  39.8 0.7 %final.1 = bf16[8,2,1024]{2,1,0:T(2,128)(2,1)} custom-call(bf16[16,1024]{1,0:T(8,128)(2,1)S(1)} %get-tuple-element.14.refs_0_, f32[16,1024]{1,0:T(8,128)S(1)} %get-tuple-element.19.refs_1_, bf16[16,1024]{1,0:T(8,128)(2,1)S(1)} %collective-permute-done.11.refs_2_, bf16[16,1024]{1,0:T(8,128)(2,1)S(1)} %collective-permute-done.12.refs_3_, ...), custom_call_target="tpu_custom_call" | custom-call | tf_op jit(solution)/shard_map/final/pallas_call | solution.py:371
  (1 shorter events, 0.0 us)
Async XLA Ops:
  0.0 24.6 %collective-permute-start.3 = (bf16[1,1024,512]{2,1,0:T(8,128)(2,1)}, bf16[1,1024,512]{2,1,0:T(8,128)(2,1)S(1)}, u32[]{:S(2)}, u32[]{:S(2)}) collective-permute-start(bf16[1,1024,512]{2,1,0:T(8,128)(2,1)} %refs_3_.1), channel_id=1, source_target_pairs={{0,1},{1,0},{2,3},{3,2},{4,5},{5,4},{6,7},{7,6},{8,9},{9,8},{10,11... | collective-permute-start | bytes 3145736 | tf_op jit(solution)/shard_map/ppermute | solution.py:292
  0.5 24.1 %collective-permute-start.4 = (bf16[1,256,1024]{2,1,0:T(8,128)(2,1)}, bf16[1,256,1024]{2,1,0:T(8,128)(2,1)S(1)}, u32[]{:S(2)}, u32[]{:S(2)}) collective-permute-start(bf16[1,256,1024]{2,1,0:T(8,128)(2,1)} %refs_4_.1), channel_id=1, source_target_pairs={{0,1},{1,0},{2,3},{3,2},{4,5},{5,4},{6,7},{7,6},{8,9},{9,8},{10,11... | collective-permute-start | bytes 1572872 | tf_op jit(solution)/shard_map/ppermute | solution.py:292
  0.5 24.0 %copy-start = (bf16[1,1024,512]{2,1,0:T(8,128)(2,1)S(1)}, bf16[1,1024,512]{2,1,0:T(8,128)(2,1)}, u32[]{:S(2)}) copy-start(bf16[1,1024,512]{2,1,0:T(8,128)(2,1)} %refs_3_.1) | copy-start | bytes 3145732
  0.5 24.1 %copy-start.1 = (bf16[1,256,1024]{2,1,0:T(8,128)(2,1)S(1)}, bf16[1,256,1024]{2,1,0:T(8,128)(2,1)}, u32[]{:S(2)}) copy-start(bf16[1,256,1024]{2,1,0:T(8,128)(2,1)} %refs_4_.1) | copy-start | bytes 1572868
  6.0 7.1 %collective-permute-start.2 = (bf16[16,1152]{1,0:T(8,128)(2,1)S(1)}, bf16[16,1152]{1,0:T(8,128)(2,1)S(1)}, u32[]{:S(2)}, u32[]{:S(2)}) collective-permute-start(bf16[16,1152]{1,0:T(8,128)(2,1)S(1)} %get-tuple-element.15.refs_0_), channel_id=1, source_target_pairs={{0,24},{1,7},{2,26},{3,5},{4,28},{5,3},{6,30},{7,1},{8,16},{9,15},... | collective-permute-start | bytes 110600 | tf_op jit(solution)/shard_map/ppermute | solution.py:292
  11.1 4.9 %collective-permute-start.1 = (bf16[16,1152]{1,0:T(8,128)(2,1)S(1)}, bf16[16,1152]{1,0:T(8,128)(2,1)S(1)}, u32[]{:S(2)}, u32[]{:S(2)}) collective-permute-start(bf16[16,1152]{1,0:T(8,128)(2,1)S(1)} %get-tuple-element.15.refs_0_), channel_id=1, source_target_pairs={{0,16},{1,5},{2,18},{3,7},{4,20},{5,1},{6,22},{7,3},{8,24},{9,13},... | collective-permute-start | bytes 110600 | tf_op jit(solution)/shard_map/ppermute | solution.py:292
  11.1 4.9 %collective-permute-start = (bf16[16,1152]{1,0:T(8,128)(2,1)S(1)}, bf16[16,1152]{1,0:T(8,128)(2,1)S(1)}, u32[]{:S(2)}, u32[]{:S(2)}) collective-permute-start(bf16[16,1152]{1,0:T(8,128)(2,1)S(1)} %get-tuple-element.15.refs_0_), channel_id=1, source_target_pairs={{0,8},{1,3},{2,10},{3,1},{4,12},{5,7},{6,14},{7,5},{8,0},{9,11},{1... | collective-permute-start | bytes 110600 | tf_op jit(solution)/shard_map/ppermute | solution.py:292
  16.0 6.1 %collective-permute-start.7 = (bf16[64,1152]{1,0:T(8,128)(2,1)S(1)}, bf16[64,1152]{1,0:T(8,128)(2,1)S(1)}, u32[]{:S(2)}, u32[]{:S(2)}) collective-permute-start(bf16[64,1152]{1,0:T(8,128)(2,1)S(1)} %column.1.refs_0_), channel_id=1, source_target_pairs={{0,6},{1,25},{2,4},{3,27},{4,2},{5,29},{6,0},{7,31},{8,14},{9,17},... | collective-permute-start | bytes 442376 | tf_op jit(solution)/shard_map/ppermute | solution.py:292
  18.9 5.1 %collective-permute-start.6 = (bf16[64,1152]{1,0:T(8,128)(2,1)S(1)}, bf16[64,1152]{1,0:T(8,128)(2,1)S(1)}, u32[]{:S(2)}, u32[]{:S(2)}) collective-permute-start(bf16[64,1152]{1,0:T(8,128)(2,1)S(1)} %column.1.refs_0_), channel_id=1, source_target_pairs={{0,4},{1,17},{2,6},{3,19},{4,0},{5,21},{6,2},{7,23},{8,12},{9,25},... | collective-permute-start | bytes 442376 | tf_op jit(solution)/shard_map/ppermute | solution.py:292
  19.4 5.1 %collective-permute-start.5 = (bf16[64,1152]{1,0:T(8,128)(2,1)S(1)}, bf16[64,1152]{1,0:T(8,128)(2,1)S(1)}, u32[]{:S(2)}, u32[]{:S(2)}) collective-permute-start(bf16[64,1152]{1,0:T(8,128)(2,1)S(1)} %column.1.refs_0_), channel_id=1, source_target_pairs={{0,2},{1,9},{2,0},{3,11},{4,6},{5,13},{6,4},{7,15},{8,10},{9,1},{1... | collective-permute-start | bytes 442376 | tf_op jit(solution)/shard_map/ppermute | solution.py:292
  25.6 6.0 %collective-permute-start.8 = (bf16[64,1024]{1,0:T(8,128)(2,1)S(1)}, bf16[64,1024]{1,0:T(8,128)(2,1)S(1)}, u32[]{:S(2)}, u32[]{:S(2)}) collective-permute-start(bf16[64,1024]{1,0:T(8,128)(2,1)S(1)} %get-tuple-element.16), channel_id=1, source_target_pairs={{0,6},{1,25},{2,4},{3,27},{4,2},{5,29},{6,0},{7,31},{8,14},{9,17},... | collective-permute-start | bytes 393224 | tf_op jit(solution)/shard_map/ppermute | solution.py:292
  26.9 6.1 %collective-permute-start.9 = (bf16[64,1024]{1,0:T(8,128)(2,1)S(1)}, bf16[64,1024]{1,0:T(8,128)(2,1)S(1)}, u32[]{:S(2)}, u32[]{:S(2)}) collective-permute-start(bf16[64,1024]{1,0:T(8,128)(2,1)S(1)} %get-tuple-element.17), channel_id=1, source_target_pairs={{0,4},{1,17},{2,6},{3,19},{4,0},{5,21},{6,2},{7,23},{8,12},{9,25},... | collective-permute-start | bytes 393224 | tf_op jit(solution)/shard_map/ppermute | solution.py:292
  28.3 5.0 %collective-permute-start.10 = (bf16[64,1024]{1,0:T(8,128)(2,1)S(1)}, bf16[64,1024]{1,0:T(8,128)(2,1)S(1)}, u32[]{:S(2)}, u32[]{:S(2)}) collective-permute-start(bf16[64,1024]{1,0:T(8,128)(2,1)S(1)} %get-tuple-element.18), channel_id=1, source_target_pairs={{0,2},{1,9},{2,0},{3,11},{4,6},{5,13},{6,4},{7,15},{8,10},{9,1},{1... | collective-permute-start | bytes 393224 | tf_op jit(solution)/shard_map/ppermute | solution.py:292
  33.3 5.8 %collective-permute-start.11 = (bf16[16,1024]{1,0:T(8,128)(2,1)S(1)}, bf16[16,1024]{1,0:T(8,128)(2,1)S(1)}, u32[]{:S(2)}, u32[]{:S(2)}) collective-permute-start(bf16[16,1024]{1,0:T(8,128)(2,1)S(1)} %get-tuple-element.20), channel_id=1, source_target_pairs={{0,24},{1,7},{2,26},{3,5},{4,28},{5,3},{6,30},{7,1},{8,16},{9,15},... | collective-permute-start | bytes 98312 | tf_op jit(solution)/shard_map/ppermute | solution.py:292
  34.4 5.0 %collective-permute-start.12 = (bf16[16,1024]{1,0:T(8,128)(2,1)S(1)}, bf16[16,1024]{1,0:T(8,128)(2,1)S(1)}, u32[]{:S(2)}, u32[]{:S(2)}) collective-permute-start(bf16[16,1024]{1,0:T(8,128)(2,1)S(1)} %get-tuple-element.21), channel_id=1, source_target_pairs={{0,16},{1,5},{2,18},{3,7},{4,20},{5,1},{6,22},{7,3},{8,24},{9,13},... | collective-permute-start | bytes 98312 | tf_op jit(solution)/shard_map/ppermute | solution.py:292
  35.4 4.4 %collective-permute-start.13 = (bf16[16,1024]{1,0:T(8,128)(2,1)S(1)}, bf16[16,1024]{1,0:T(8,128)(2,1)S(1)}, u32[]{:S(2)}, u32[]{:S(2)}) collective-permute-start(bf16[16,1024]{1,0:T(8,128)(2,1)S(1)} %get-tuple-element.22), channel_id=1, source_target_pairs={{0,8},{1,3},{2,10},{3,1},{4,12},{5,7},{6,14},{7,5},{8,0},{9,11},{1... | collective-permute-start | bytes 98312 | tf_op jit(solution)/shard_map/ppermute | solution.py:292

commit v5 on v4

--- a/solution.py
+++ b/solution.py
@@ -69,9 +69,13 @@
     chunks = proj_sem.shape[0]
     depth = proj_hbm.shape[0] // chunks
 
-    def state_copy(h):
+    groups = state_sem.shape[0]
+    group = key_heads // groups
+
+    def state_copy(c):
+        part = pl.ds(c * group * share, group * share)
         return pltpu.make_async_copy(
-            state_hbm.at[:, pl.ds(h * share, share)], state_buf.at[h], state_sem.at[h]
+            state_hbm.at[:, part], state_buf.at[:, part], state_sem.at[c]
         )
 
     def proj_copy(c):
@@ -100,8 +104,8 @@
     state_copy(0).start()
     for copy in early[2:]:
         copy.start()
-    for h in range(1, key_heads):
-        state_copy(h).start()
+    for c in range(1, groups):
+        state_copy(c).start()
     for c in range(chunks):
         proj_copy(c).start()
     for copy in late:
@@ -146,10 +150,11 @@
         key_query01 = jnp.sum(keys[0] * queries[1], axis=-1, keepdims=True)
         key_query11 = jnp.sum(keys[1] * queries[1], axis=-1, keepdims=True)
 
-        state_copy(h).wait()
+        if h % group == 0:
+            state_copy(h // group).wait()
         for r in range(rows):
             left = left_buf[h, r * 8 : (r + 1) * 8, :].astype(bf16)
-            right = jnp.concatenate([state_buf[h, r, i] for i in range(share)], axis=-1)
+            right = jnp.concatenate([state_buf[r, h * share + i] for i in range(share)], axis=-1)
             out = jnp.dot(left, right, preferred_element_type=f32)
             for i in range(share):
                 right_buf[h, i, r * 8 : (r + 1) * 8, :] = out[:, i * value_size : (i + 1) * value_size]
@@ -324,7 +329,7 @@
     token_count = row_count * 2
     sent_width = model_width + (2 * expert_total + 127) // 128 * 128
     first, second = chip_masks(device_count)
-    chunks = 4
+    chunks = 2
     params = pltpu.CompilerParams(vmem_limit_bytes=48 * 1024 * 1024)
     operands = (
         hidden_in,
@@ -355,12 +360,12 @@
         out_specs=tuple(vmem(2)),
         scratch_shapes=[pltpu.VMEM(x.shape, x.dtype) for x in operands[:13]]
         + [
-            pltpu.VMEM((key_heads, row_count, share, key_size, value_size), bf16),
+            pltpu.VMEM(state_in.shape, bf16),
             pltpu.VMEM(out_proj.shape, bf16),
             pltpu.VMEM((key_heads, 8 * row_count, key_size), f32),
             pltpu.VMEM((key_heads, share, 8 * row_count, value_size), f32),
             pltpu.SemaphoreType.DMA((13,)),
-            pltpu.SemaphoreType.DMA((key_heads,)),
+            pltpu.SemaphoreType.DMA((key_heads // 2,)),
             pltpu.SemaphoreType.DMA((chunks,)),
         ],
         compiler_params=params,

time: 40.6 us -> 40 us (0.985)
  Pallas kernels: 8.06 us -> 7.49 us
    pallas_call x1, Pallas kernels: 5.47 us -> 4.89 us  [shards(): pl.pallas_call(mixer_kernel, out_shape=(jax.ShapeDtypeStruct((token_count...]
  transfers between devices with their start and end apart: 14 -> 14, of which waited for: 11 -> 11; matrix products, arithmetic and copies ran while one was open for 0% -> 0% of each run, Pallas kernels for 16% -> 14%
where the time goes in v5:
time: 40 us; the launch traced here: 39.9 us
  starting transfers between devices  17.8 us (44%)
  waiting for transfers between devices  14.5 us (36%)
  Pallas kernels  7.49 us (19%)
    ppermute x14, starting transfers between devices, hop(): return lax.ppermute(x, 'dp', [(i, i ^ masks[i % 2]) for i in range(count)])  17.8 us
    ppermute x14, waiting for transfers between devices, hop(): return lax.ppermute(x, 'dp', [(i, i ^ masks[i % 2]) for i in range(count)])  14.5 us
    pallas_call x1, Pallas kernels, shards(): pl.pallas_call(mixer_kernel, out_shape=(jax.ShapeDtypeStruct((token_count...  4.89 us
    pallas_call x5, Pallas kernels, local(): pl.pallas_call(body, out_shape=tuple((jax.ShapeDtypeStruct(*o) for o in o...  2.6 us
  transfers between devices with their start and end apart: 14, of which 11 were waited for; matrix products, arithmetic and copies ran while one was open for 0% of the time, Pallas kernels for 14%

profile of v5, /device:TPU:0, one launch (start us, length us, event | category | flops | bytes accessed | tf_op | source)
XLA Modules:
  0.0 39.9 jit_solution(16654865526337370293)
XLA Ops:
  0.0 0.5 %collective-permute-start.3 = (bf16[1,1024,512]{2,1,0:T(8,128)(2,1)}, bf16[1,1024,512]{2,1,0:T(8,128)(2,1)S(1)}, u32[]{:S(2)}, u32[]{:S(2)}) collective-permute-start(bf16[1,1024,512]{2,1,0:T(8,128)(2,1)} %refs_3_.1), channel_id=1, source_target_pairs={{0,1},{1,0},{2,3},{3,2},{4,5},{5,4},{6,7},{7,6},{8,9},{9,8},{10,11... | collective-permute-start | bytes 3145736 | tf_op jit(solution)/shard_map/ppermute | solution.py:297
  0.5 0.1 collective-permute-start.4
  0.5 0.0 copy-start
  0.5 0.0 copy-start.1
  0.5 4.9 %mixer.1 = (bf16[16,1152]{1,0:T(8,128)(2,1)S(1)}, bf16[16,1024]{1,0:T(8,128)(2,1)S(1)}) custom-call(bf16[8,2,1024]{2,1,0:T(2,128)(2,1)} %hidden_hbm.1, bf16[8,2,1024]{2,1,0:T(2,128)(2,1)} %query_hbm.1, bf16[8,2,1024]{2,1,0:T(2,128)(2,1)} %key_hbm.1, bf16[8,2,2048]{2,1,0:T(2,128)(2,1)} %value_hbm.1, bf16[8,2,2048]{2,1,0:T(2,128)(2,1)} %gate_hbm.1, ...), custom_call_target="tpu_custom_call" | custom-call | tf_op jit(solution)/shard_map/mixer/pallas_call | solution.py:353
  5.4 5.1 %collective-permute-start.2 = (bf16[16,1152]{1,0:T(8,128)(2,1)S(1)}, bf16[16,1152]{1,0:T(8,128)(2,1)S(1)}, u32[]{:S(2)}, u32[]{:S(2)}) collective-permute-start(bf16[16,1152]{1,0:T(8,128)(2,1)S(1)} %get-tuple-element.15.refs_0_), channel_id=1, source_target_pairs={{0,24},{1,7},{2,26},{3,5},{4,28},{5,3},{6,30},{7,1},{8,16},{9,15},... | collective-permute-start | bytes 110600 | tf_op jit(solution)/shard_map/ppermute | solution.py:297
  10.5 0.0 collective-permute-start.1
  10.5 0.6 %collective-permute-start = (bf16[16,1152]{1,0:T(8,128)(2,1)S(1)}, bf16[16,1152]{1,0:T(8,128)(2,1)S(1)}, u32[]{:S(2)}, u32[]{:S(2)}) collective-permute-start(bf16[16,1152]{1,0:T(8,128)(2,1)S(1)} %get-tuple-element.15.refs_0_), channel_id=1, source_target_pairs={{0,8},{1,3},{2,10},{3,1},{4,12},{5,7},{6,14},{7,5},{8,0},{9,11},{1... | collective-permute-start | bytes 110600 | tf_op jit(solution)/shard_map/ppermute | solution.py:297
  11.2 1.3 %collective-permute-done.2.refs_3_ = bf16[16,1152]{1,0:T(8,128)(2,1)S(1)} collective-permute-done((bf16[16,1152]{1,0:T(8,128)(2,1)S(1)}, bf16[16,1152]{1,0:T(8,128)(2,1)S(1)}, u32[]{:S(2)}, u32[]{:S(2)}) %collective-permute-start.2) | collective-permute-done | bytes 36896 | tf_op jit(solution)/shard_map/ppermute | solution.py:297
  12.5 2.9 %collective-permute-done.1.refs_2_ = bf16[16,1152]{1,0:T(8,128)(2,1)S(1)} collective-permute-done((bf16[16,1152]{1,0:T(8,128)(2,1)S(1)}, bf16[16,1152]{1,0:T(8,128)(2,1)S(1)}, u32[]{:S(2)}, u32[]{:S(2)}) %collective-permute-start.1) | collective-permute-done | bytes 36896 | tf_op jit(solution)/shard_map/ppermute | solution.py:297
  15.4 0.0 collective-permute-done.refs_1_
  15.4 2.9 %collective-permute-start.7 = (bf16[64,1152]{1,0:T(8,128)(2,1)S(1)}, bf16[64,1152]{1,0:T(8,128)(2,1)S(1)}, u32[]{:S(2)}, u32[]{:S(2)}) collective-permute-start(bf16[64,1152]{1,0:T(8,128)(2,1)S(1)} %column.1.refs_0_), channel_id=1, source_target_pairs={{0,6},{1,25},{2,4},{3,27},{4,2},{5,29},{6,0},{7,31},{8,14},{9,17},... | collective-permute-start | bytes 442376 | tf_op jit(solution)/shard_map/ppermute | solution.py:297
  18.3 0.5 %collective-permute-start.6 = (bf16[64,1152]{1,0:T(8,128)(2,1)S(1)}, bf16[64,1152]{1,0:T(8,128)(2,1)S(1)}, u32[]{:S(2)}, u32[]{:S(2)}) collective-permute-start(bf16[64,1152]{1,0:T(8,128)(2,1)S(1)} %column.1.refs_0_), channel_id=1, source_target_pairs={{0,4},{1,17},{2,6},{3,19},{4,0},{5,21},{6,2},{7,23},{8,12},{9,25},... | collective-permute-start | bytes 442376 | tf_op jit(solution)/shard_map/ppermute | solution.py:297
  18.8 0.1 collective-permute-start.5
  19.0 2.5 %collective-permute-done.7.refs_2_ = bf16[64,1152]{1,0:T(8,128)(2,1)S(1)} collective-permute-done((bf16[64,1152]{1,0:T(8,128)(2,1)S(1)}, bf16[64,1152]{1,0:T(8,128)(2,1)S(1)}, u32[]{:S(2)}, u32[]{:S(2)}) %collective-permute-start.7) | collective-permute-done | bytes 147488 | tf_op jit(solution)/shard_map/ppermute | solution.py:297
  21.5 2.0 %collective-permute-done.6.refs_1_ = bf16[64,1152]{1,0:T(8,128)(2,1)S(1)} collective-permute-done((bf16[64,1152]{1,0:T(8,128)(2,1)S(1)}, bf16[64,1152]{1,0:T(8,128)(2,1)S(1)}, u32[]{:S(2)}, u32[]{:S(2)}) %collective-permute-start.6) | collective-permute-done | bytes 147488 | tf_op jit(solution)/shard_map/ppermute | solution.py:297
  23.5 0.5 %collective-permute-done.5.refs_0_ = bf16[64,1152]{1,0:T(8,128)(2,1)S(1)} collective-permute-done((bf16[64,1152]{1,0:T(8,128)(2,1)S(1)}, bf16[64,1152]{1,0:T(8,128)(2,1)S(1)}, u32[]{:S(2)}, u32[]{:S(2)}) %collective-permute-start.5) | collective-permute-done | bytes 147488 | tf_op jit(solution)/shard_map/ppermute | solution.py:297
  24.0 0.0 collective-permute-done.4.refs_4_.refs_6_
  24.0 0.0 collective-permute-done.3.refs_3_.refs_5_
  24.0 0.0 copy-done
  24.0 0.0 copy-done.1
  24.0 1.0 %experts.1 = (bf16[64,1024]{1,0:T(8,128)(2,1)S(1)}, bf16[64,1024]{1,0:T(8,128)(2,1)S(1)}, bf16[64,1024]{1,0:T(8,128)(2,1)S(1)}) custom-call(bf16[64,1152]{1,0:T(8,128)(2,1)S(1)} %collective-permute-done.5.refs_0_, bf16[64,1152]{1,0:T(8,128)(2,1)S(1)} %collective-permute-done.6.refs_1_, bf16[64,1152]{1,0:T(8,128)(2,1)S(1)} %collective-permute-done.7.refs_2_, ...), custom_call_target="tpu_custom_call" | custom-call | tf_op jit(solution)/shard_map/experts/pallas_call | solution.py:376
  25.0 1.2 %collective-permute-start.8 = (bf16[64,1024]{1,0:T(8,128)(2,1)S(1)}, bf16[64,1024]{1,0:T(8,128)(2,1)S(1)}, u32[]{:S(2)}, u32[]{:S(2)}) collective-permute-start(bf16[64,1024]{1,0:T(8,128)(2,1)S(1)} %get-tuple-element.16), channel_id=1, source_target_pairs={{0,6},{1,25},{2,4},{3,27},{4,2},{5,29},{6,0},{7,31},{8,14},{9,17},... | collective-permute-start | bytes 393224 | tf_op jit(solution)/shard_map/ppermute | solution.py:297
  26.3 1.4 %collective-permute-start.9 = (bf16[64,1024]{1,0:T(8,128)(2,1)S(1)}, bf16[64,1024]{1,0:T(8,128)(2,1)S(1)}, u32[]{:S(2)}, u32[]{:S(2)}) collective-permute-start(bf16[64,1024]{1,0:T(8,128)(2,1)S(1)} %get-tuple-element.17), channel_id=1, source_target_pairs={{0,4},{1,17},{2,6},{3,19},{4,0},{5,21},{6,2},{7,23},{8,12},{9,25},... | collective-permute-start | bytes 393224 | tf_op jit(solution)/shard_map/ppermute | solution.py:297
  27.7 0.9 %collective-permute-start.10 = (bf16[64,1024]{1,0:T(8,128)(2,1)S(1)}, bf16[64,1024]{1,0:T(8,128)(2,1)S(1)}, u32[]{:S(2)}, u32[]{:S(2)}) collective-permute-start(bf16[64,1024]{1,0:T(8,128)(2,1)S(1)} %get-tuple-element.18), channel_id=1, source_target_pairs={{0,2},{1,9},{2,0},{3,11},{4,6},{5,13},{6,4},{7,15},{8,10},{9,1},{1... | collective-permute-start | bytes 393224 | tf_op jit(solution)/shard_map/ppermute | solution.py:297
  28.6 0.8 %own_experts.1.refs_0_ = f32[64,1024]{1,0:T(8,128)S(1)} custom-call(bf16[64,1152]{1,0:T(8,128)(2,1)S(1)} %column.1.refs_0_, bf16[1,1024,512]{2,1,0:T(8,128)(2,1)S(1)} %copy-done, bf16[1,256,1024]{2,1,0:T(8,128)(2,1)S(1)} %copy-done.1, bf16[1,1024,512]{2,1,0:T(8,128)(2,1)S(1)} %collective-permute-done.3.refs_3_.refs_5_, ...), custom_call_target="tpu_custom_call" | custom-call | tf_op jit(solution)/shard_map/own_experts/pallas_call | solution.py:376
  29.4 1.6 %collective-permute-done.8.refs_1_ = bf16[64,1024]{1,0:T(8,128)(2,1)S(1)} collective-permute-done((bf16[64,1024]{1,0:T(8,128)(2,1)S(1)}, bf16[64,1024]{1,0:T(8,128)(2,1)S(1)}, u32[]{:S(2)}, u32[]{:S(2)}) %collective-permute-start.8) | collective-permute-done | bytes 131104 | tf_op jit(solution)/shard_map/ppermute | solution.py:297
  31.1 1.3 %collective-permute-done.9.refs_2_ = bf16[64,1024]{1,0:T(8,128)(2,1)S(1)} collective-permute-done((bf16[64,1024]{1,0:T(8,128)(2,1)S(1)}, bf16[64,1024]{1,0:T(8,128)(2,1)S(1)}, u32[]{:S(2)}, u32[]{:S(2)}) %collective-permute-start.9) | collective-permute-done | bytes 131104 | tf_op jit(solution)/shard_map/ppermute | solution.py:297
  32.4 0.3 collective-permute-done.10.refs_3_
  32.7 0.1 column_sum.1
  32.7 1.1 %collective-permute-start.11 = (bf16[16,1024]{1,0:T(8,128)(2,1)S(1)}, bf16[16,1024]{1,0:T(8,128)(2,1)S(1)}, u32[]{:S(2)}, u32[]{:S(2)}) collective-permute-start(bf16[16,1024]{1,0:T(8,128)(2,1)S(1)} %get-tuple-element.20), channel_id=1, source_target_pairs={{0,24},{1,7},{2,26},{3,5},{4,28},{5,3},{6,30},{7,1},{8,16},{9,15},... | collective-permute-start | bytes 98312 | tf_op jit(solution)/shard_map/ppermute | solution.py:297
  33.8 1.0 %collective-permute-start.12 = (bf16[16,1024]{1,0:T(8,128)(2,1)S(1)}, bf16[16,1024]{1,0:T(8,128)(2,1)S(1)}, u32[]{:S(2)}, u32[]{:S(2)}) collective-permute-start(bf16[16,1024]{1,0:T(8,128)(2,1)S(1)} %get-tuple-element.21), channel_id=1, source_target_pairs={{0,16},{1,5},{2,18},{3,7},{4,20},{5,1},{6,22},{7,3},{8,24},{9,13},... | collective-permute-start | bytes 98312 | tf_op jit(solution)/shard_map/ppermute | solution.py:297
  34.8 2.3 %collective-permute-start.13 = (bf16[16,1024]{1,0:T(8,128)(2,1)S(1)}, bf16[16,1024]{1,0:T(8,128)(2,1)S(1)}, u32[]{:S(2)}, u32[]{:S(2)}) collective-permute-start(bf16[16,1024]{1,0:T(8,128)(2,1)S(1)} %get-tuple-element.22), channel_id=1, source_target_pairs={{0,8},{1,3},{2,10},{3,1},{4,12},{5,7},{6,14},{7,5},{8,0},{9,11},{1... | collective-permute-start | bytes 98312 | tf_op jit(solution)/shard_map/ppermute | solution.py:297
  37.2 1.3 %collective-permute-done.11.refs_2_ = bf16[16,1024]{1,0:T(8,128)(2,1)S(1)} collective-permute-done((bf16[16,1024]{1,0:T(8,128)(2,1)S(1)}, bf16[16,1024]{1,0:T(8,128)(2,1)S(1)}, u32[]{:S(2)}, u32[]{:S(2)}) %collective-permute-start.11) | collective-permute-done | bytes 32800 | tf_op jit(solution)/shard_map/ppermute | solution.py:297
  38.5 0.3 collective-permute-done.12.refs_3_
  38.9 0.3 collective-permute-done.13.refs_4_
  39.2 0.7 %final.1 = bf16[8,2,1024]{2,1,0:T(2,128)(2,1)} custom-call(bf16[16,1024]{1,0:T(8,128)(2,1)S(1)} %get-tuple-element.14.refs_0_, f32[16,1024]{1,0:T(8,128)S(1)} %get-tuple-element.19.refs_1_, bf16[16,1024]{1,0:T(8,128)(2,1)S(1)} %collective-permute-done.11.refs_2_, bf16[16,1024]{1,0:T(8,128)(2,1)S(1)} %collective-permute-done.12.refs_3_, ...), custom_call_target="tpu_custom_call" | custom-call | tf_op jit(solution)/shard_map/final/pallas_call | solution.py:376
  (1 shorter events, 0.0 us)
Async XLA Ops:
  0.0 24.0 %collective-permute-start.3 = (bf16[1,1024,512]{2,1,0:T(8,128)(2,1)}, bf16[1,1024,512]{2,1,0:T(8,128)(2,1)S(1)}, u32[]{:S(2)}, u32[]{:S(2)}) collective-permute-start(bf16[1,1024,512]{2,1,0:T(8,128)(2,1)} %refs_3_.1), channel_id=1, source_target_pairs={{0,1},{1,0},{2,3},{3,2},{4,5},{5,4},{6,7},{7,6},{8,9},{9,8},{10,11... | collective-permute-start | bytes 3145736 | tf_op jit(solution)/shard_map/ppermute | solution.py:297
  0.5 23.5 %collective-permute-start.4 = (bf16[1,256,1024]{2,1,0:T(8,128)(2,1)}, bf16[1,256,1024]{2,1,0:T(8,128)(2,1)S(1)}, u32[]{:S(2)}, u32[]{:S(2)}) collective-permute-start(bf16[1,256,1024]{2,1,0:T(8,128)(2,1)} %refs_4_.1), channel_id=1, source_target_pairs={{0,1},{1,0},{2,3},{3,2},{4,5},{5,4},{6,7},{7,6},{8,9},{9,8},{10,11... | collective-permute-start | bytes 1572872 | tf_op jit(solution)/shard_map/ppermute | solution.py:297
  0.5 23.5 %copy-start = (bf16[1,1024,512]{2,1,0:T(8,128)(2,1)S(1)}, bf16[1,1024,512]{2,1,0:T(8,128)(2,1)}, u32[]{:S(2)}) copy-start(bf16[1,1024,512]{2,1,0:T(8,128)(2,1)} %refs_3_.1) | copy-start | bytes 3145732
  0.5 23.5 %copy-start.1 = (bf16[1,256,1024]{2,1,0:T(8,128)(2,1)S(1)}, bf16[1,256,1024]{2,1,0:T(8,128)(2,1)}, u32[]{:S(2)}) copy-start(bf16[1,256,1024]{2,1,0:T(8,128)(2,1)} %refs_4_.1) | copy-start | bytes 1572868
  5.4 7.1 %collective-permute-start.2 = (bf16[16,1152]{1,0:T(8,128)(2,1)S(1)}, bf16[16,1152]{1,0:T(8,128)(2,1)S(1)}, u32[]{:S(2)}, u32[]{:S(2)}) collective-permute-start(bf16[16,1152]{1,0:T(8,128)(2,1)S(1)} %get-tuple-element.15.refs_0_), channel_id=1, source_target_pairs={{0,24},{1,7},{2,26},{3,5},{4,28},{5,3},{6,30},{7,1},{8,16},{9,15},... | collective-permute-start | bytes 110600 | tf_op jit(solution)/shard_map/ppermute | solution.py:297
  10.5 4.9 %collective-permute-start.1 = (bf16[16,1152]{1,0:T(8,128)(2,1)S(1)}, bf16[16,1152]{1,0:T(8,128)(2,1)S(1)}, u32[]{:S(2)}, u32[]{:S(2)}) collective-permute-start(bf16[16,1152]{1,0:T(8,128)(2,1)S(1)} %get-tuple-element.15.refs_0_), channel_id=1, source_target_pairs={{0,16},{1,5},{2,18},{3,7},{4,20},{5,1},{6,22},{7,3},{8,24},{9,13},... | collective-permute-start | bytes 110600 | tf_op jit(solution)/shard_map/ppermute | solution.py:297
  10.5 4.9 %collective-permute-start = (bf16[16,1152]{1,0:T(8,128)(2,1)S(1)}, bf16[16,1152]{1,0:T(8,128)(2,1)S(1)}, u32[]{:S(2)}, u32[]{:S(2)}) collective-permute-start(bf16[16,1152]{1,0:T(8,128)(2,1)S(1)} %get-tuple-element.15.refs_0_), channel_id=1, source_target_pairs={{0,8},{1,3},{2,10},{3,1},{4,12},{5,7},{6,14},{7,5},{8,0},{9,11},{1... | collective-permute-start | bytes 110600 | tf_op jit(solution)/shard_map/ppermute | solution.py:297
  15.4 6.1 %collective-permute-start.7 = (bf16[64,1152]{1,0:T(8,128)(2,1)S(1)}, bf16[64,1152]{1,0:T(8,128)(2,1)S(1)}, u32[]{:S(2)}, u32[]{:S(2)}) collective-permute-start(bf16[64,1152]{1,0:T(8,128)(2,1)S(1)} %column.1.refs_0_), channel_id=1, source_target_pairs={{0,6},{1,25},{2,4},{3,27},{4,2},{5,29},{6,0},{7,31},{8,14},{9,17},... | collective-permute-start | bytes 442376 | tf_op jit(solution)/shard_map/ppermute | solution.py:297
  18.3 5.1 %collective-permute-start.6 = (bf16[64,1152]{1,0:T(8,128)(2,1)S(1)}, bf16[64,1152]{1,0:T(8,128)(2,1)S(1)}, u32[]{:S(2)}, u32[]{:S(2)}) collective-permute-start(bf16[64,1152]{1,0:T(8,128)(2,1)S(1)} %column.1.refs_0_), channel_id=1, source_target_pairs={{0,4},{1,17},{2,6},{3,19},{4,0},{5,21},{6,2},{7,23},{8,12},{9,25},... | collective-permute-start | bytes 442376 | tf_op jit(solution)/shard_map/ppermute | solution.py:297
  18.8 5.1 %collective-permute-start.5 = (bf16[64,1152]{1,0:T(8,128)(2,1)S(1)}, bf16[64,1152]{1,0:T(8,128)(2,1)S(1)}, u32[]{:S(2)}, u32[]{:S(2)}) collective-permute-start(bf16[64,1152]{1,0:T(8,128)(2,1)S(1)} %column.1.refs_0_), channel_id=1, source_target_pairs={{0,2},{1,9},{2,0},{3,11},{4,6},{5,13},{6,4},{7,15},{8,10},{9,1},{1... | collective-permute-start | bytes 442376 | tf_op jit(solution)/shard_map/ppermute | solution.py:297
  25.0 6.0 %collective-permute-start.8 = (bf16[64,1024]{1,0:T(8,128)(2,1)S(1)}, bf16[64,1024]{1,0:T(8,128)(2,1)S(1)}, u32[]{:S(2)}, u32[]{:S(2)}) collective-permute-start(bf16[64,1024]{1,0:T(8,128)(2,1)S(1)} %get-tuple-element.16), channel_id=1, source_target_pairs={{0,6},{1,25},{2,4},{3,27},{4,2},{5,29},{6,0},{7,31},{8,14},{9,17},... | collective-permute-start | bytes 393224 | tf_op jit(solution)/shard_map/ppermute | solution.py:297
  26.3 6.1 %collective-permute-start.9 = (bf16[64,1024]{1,0:T(8,128)(2,1)S(1)}, bf16[64,1024]{1,0:T(8,128)(2,1)S(1)}, u32[]{:S(2)}, u32[]{:S(2)}) collective-permute-start(bf16[64,1024]{1,0:T(8,128)(2,1)S(1)} %get-tuple-element.17), channel_id=1, source_target_pairs={{0,4},{1,17},{2,6},{3,19},{4,0},{5,21},{6,2},{7,23},{8,12},{9,25},... | collective-permute-start | bytes 393224 | tf_op jit(solution)/shard_map/ppermute | solution.py:297
  27.7 5.0 %collective-permute-start.10 = (bf16[64,1024]{1,0:T(8,128)(2,1)S(1)}, bf16[64,1024]{1,0:T(8,128)(2,1)S(1)}, u32[]{:S(2)}, u32[]{:S(2)}) collective-permute-start(bf16[64,1024]{1,0:T(8,128)(2,1)S(1)} %get-tuple-element.18), channel_id=1, source_target_pairs={{0,2},{1,9},{2,0},{3,11},{4,6},{5,13},{6,4},{7,15},{8,10},{9,1},{1... | collective-permute-start | bytes 393224 | tf_op jit(solution)/shard_map/ppermute | solution.py:297
  32.7 5.8 %collective-permute-start.11 = (bf16[16,1024]{1,0:T(8,128)(2,1)S(1)}, bf16[16,1024]{1,0:T(8,128)(2,1)S(1)}, u32[]{:S(2)}, u32[]{:S(2)}) collective-permute-start(bf16[16,1024]{1,0:T(8,128)(2,1)S(1)} %get-tuple-element.20), channel_id=1, source_target_pairs={{0,24},{1,7},{2,26},{3,5},{4,28},{5,3},{6,30},{7,1},{8,16},{9,15},... | collective-permute-start | bytes 98312 | tf_op jit(solution)/shard_map/ppermute | solution.py:297
  33.8 5.0 %collective-permute-start.12 = (bf16[16,1024]{1,0:T(8,128)(2,1)S(1)}, bf16[16,1024]{1,0:T(8,128)(2,1)S(1)}, u32[]{:S(2)}, u32[]{:S(2)}) collective-permute-start(bf16[16,1024]{1,0:T(8,128)(2,1)S(1)} %get-tuple-element.21), channel_id=1, source_target_pairs={{0,16},{1,5},{2,18},{3,7},{4,20},{5,1},{6,22},{7,3},{8,24},{9,13},... | collective-permute-start | bytes 98312 | tf_op jit(solution)/shard_map/ppermute | solution.py:297
  34.8 4.4 %collective-permute-start.13 = (bf16[16,1024]{1,0:T(8,128)(2,1)S(1)}, bf16[16,1024]{1,0:T(8,128)(2,1)S(1)}, u32[]{:S(2)}, u32[]{:S(2)}) collective-permute-start(bf16[16,1024]{1,0:T(8,128)(2,1)S(1)} %get-tuple-element.22), channel_id=1, source_target_pairs={{0,8},{1,3},{2,10},{3,1},{4,12},{5,7},{6,14},{7,5},{8,0},{9,11},{1... | collective-permute-start | bytes 98312 | tf_op jit(solution)/shard_map/ppermute | solution.py:297

commit v6 on v5

--- a/solution.py
+++ b/solution.py
@@ -10,12 +10,6 @@
 eps_norm = 1e-06
 f32 = jnp.float32
 bf16 = jnp.bfloat16
-
-
-def split_two(x):
-    high = x.astype(bf16)
-    low = (x - high.astype(f32)).astype(bf16)
-    return high, low
 
 
 def nt_dot(a, b):
@@ -34,7 +28,6 @@
     step_bias_hbm,
     norm_gain_hbm,
     post_gain_hbm,
-    router_hbm,
     ids_hbm,
     state_hbm,
     proj_hbm,
@@ -51,7 +44,6 @@
     step_bias_ref,
     norm_gain_ref,
     post_gain_ref,
-    router_ref,
     ids_ref,
     state_buf,
     proj_buf,
@@ -95,7 +87,6 @@
         (ids_hbm, ids_ref),
         (hidden_hbm, hidden_ref),
         (post_gain_hbm, post_gain_ref),
-        (router_hbm, router_ref),
     )
     small = [pltpu.make_async_copy(a, b, small_sem.at[i]) for i, (a, b) in enumerate(pairs)]
     early, late = small[:9], small[9:]
@@ -185,6 +176,13 @@
     ).astype(bf16)
     for copy in late:
         copy.wait()
+    tokens, extra = 2 * rows, routed_ref.shape[1] - proj_hbm.shape[1]
+    ids = jnp.concatenate([ids_ref[:, p, :] for p in range(2)], axis=0)
+    lane = lax.broadcasted_iota(jnp.int32, (tokens, extra), 1)
+    chosen = jnp.zeros((tokens, extra), f32)
+    for k in range(ids.shape[1]):
+        chosen = chosen + (ids[:, k : k + 1] == lane).astype(f32)
+    routed_ref[:, -extra:] = chosen.astype(bf16)
     hidden = hidden_ref[...].astype(f32)
     total = jnp.concatenate([hidden[:, p, :] for p in range(2)], axis=0)
     for c in range(chunks):
@@ -199,25 +197,7 @@
         * lax.rsqrt(jnp.mean(wide * wide, axis=-1, keepdims=True) + eps_norm)
         * post_gain_ref[...].reshape(1, wide.shape[1])
     ).astype(bf16)
-    logits = nt_dot(routed, router_ref[...])
-
-    tokens = 2 * rows
-    experts = logits.shape[1]
-    ids = jnp.concatenate([ids_ref[:, p, :] for p in range(2)], axis=0)
-    expert = lax.broadcasted_iota(jnp.int32, (tokens, experts), 1)
-    chosen = jnp.zeros((tokens, experts), f32)
-    for k in range(ids.shape[1]):
-        chosen = chosen + (ids[:, k : k + 1] == expert).astype(f32)
-    raised = jnp.where(chosen > 0.0, jnp.exp(logits), 0.0)
-    high, low = split_two(raised / jnp.sum(raised, axis=-1, keepdims=True))
-    width = routed.shape[1]
-    extra = routed_ref.shape[1] - width
-    lane = lax.broadcasted_iota(jnp.int32, (experts, extra), 1)
-    number = lax.broadcasted_iota(jnp.int32, (experts, extra), 0)
-    beside = jnp.dot(high, (lane == number).astype(bf16), preferred_element_type=f32)
-    beside += jnp.dot(low, (lane == number + experts).astype(bf16), preferred_element_type=f32)
-    routed_ref[:, :width] = routed
-    routed_ref[:, width:] = beside.astype(bf16)
+    routed_ref[:, : routed.shape[1]] = routed
 
 
 def column_kernel(*refs):
@@ -227,35 +207,28 @@
         out_ref[i * rows : (i + 1) * rows, :] = ref[...]
 
 
-def expert_sum(rows, width, weights, first, experts):
-    hidden_units = weights[0][1].shape[1]
-    x = rows[:, :width]
-    beside = rows[:, width:].astype(f32)
-    lane = lax.broadcasted_iota(jnp.int32, beside.shape, 1)
+def expert_kernel(count, *refs):
+    blocks = refs[:count]
+    router, up_own, down_own, up_other, down_other = refs[count : count + 5]
+    outs = refs[count + 5 :]
+    rows, width = outs[0].shape
+    hidden_units = down_own.shape[1]
+    me = lax.axis_index("dp")
+    both_parts = blocks[0][...] if count == 1 else jnp.concatenate([b[...] for b in blocks], axis=0)
+    x = both_parts[:, :width]
+    chosen = both_parts[:, width:].astype(f32)[:, : router.shape[0]] > 0.0
+    raised = jnp.where(chosen, jnp.exp(nt_dot(x, router[...])), 0.0)
+    whole = jnp.sum(raised, axis=-1, keepdims=True)
+    lane = lax.broadcasted_iota(jnp.int32, raised.shape, 1)
     total = None
-    for (up_ref, down_ref), e in zip(weights, first):
+    for up_ref, down_ref, e in ((up_own, down_own, me), (up_other, down_other, me ^ 1)):
         both = jnp.dot(x, up_ref[0], preferred_element_type=f32)
         g = both[:, :hidden_units]
         activated = (g / (1.0 + jnp.exp(-g)) * both[:, hidden_units:]).astype(bf16)
         result = jnp.dot(activated, down_ref[0], preferred_element_type=f32).astype(bf16)
-        share = jnp.sum(jnp.where(lane == e, beside, 0.0), axis=-1, keepdims=True)
-        low_lane = lane == e + experts
-        share = share + jnp.sum(jnp.where(low_lane, beside, 0.0), axis=-1, keepdims=True)
+        share = jnp.sum(jnp.where(lane == e, raised, 0.0), axis=-1, keepdims=True) / whole
         part = share * result.astype(f32)
         total = part if total is None else total + part
-    return total
-
-
-def expert_kernel(experts, count, *refs):
-    blocks = refs[:count]
-    up_own, down_own, up_other, down_other = refs[count : count + 4]
-    outs = refs[count + 4 :]
-    width = outs[0].shape[1]
-    me = lax.axis_index("dp")
-    weights = ((up_own, down_own), (up_other, down_other))
-    rows = blocks[0].shape[0]
-    x = blocks[0][...] if count == 1 else jnp.concatenate([b[...] for b in blocks], axis=0)
-    total = expert_sum(x, width, weights, (me, me ^ 1), experts)
     for i, out in enumerate(outs):
         out[...] = total[i * rows : (i + 1) * rows].astype(out.dtype)
 
@@ -327,7 +300,7 @@
     key_heads = query_in.shape[2] // key_size
     share = value_heads // key_heads
     token_count = row_count * 2
-    sent_width = model_width + (2 * expert_total + 127) // 128 * 128
+    sent_width = model_width + (expert_total + 127) // 128 * 128
     first, second = chip_masks(device_count)
     chunks = 2
     params = pltpu.CompilerParams(vmem_limit_bytes=48 * 1024 * 1024)
@@ -343,7 +316,6 @@
         step_bias,
         norm_gain,
         post_gain,
-        router_weight.T,
         expert_ids,
         state_in,
         out_proj,
@@ -358,13 +330,13 @@
         ),
         in_specs=[pl.BlockSpec(memory_space=pltpu.HBM)] * len(operands),
         out_specs=tuple(vmem(2)),
-        scratch_shapes=[pltpu.VMEM(x.shape, x.dtype) for x in operands[:13]]
+        scratch_shapes=[pltpu.VMEM(x.shape, x.dtype) for x in operands[:12]]
         + [
             pltpu.VMEM(state_in.shape, bf16),
             pltpu.VMEM(out_proj.shape, bf16),
             pltpu.VMEM((key_heads, 8 * row_count, key_size), f32),
             pltpu.VMEM((key_heads, share, 8 * row_count, value_size), f32),
-            pltpu.SemaphoreType.DMA((13,)),
+            pltpu.SemaphoreType.DMA((12,)),
             pltpu.SemaphoreType.DMA((key_heads // 2,)),
             pltpu.SemaphoreType.DMA((chunks,)),
         ],
@@ -382,7 +354,7 @@
             name=name,
         )(*args)
 
-    weights = (expert_gate_up, expert_down, up_other, down_other)
+    weights = (router_weight.T, expert_gate_up, expert_down, up_other, down_other)
     column_rows = token_count * (len(first) + 1)
     pieces = [hop(routed, m) for m in first]
     (column,) = local(
@@ -390,14 +362,14 @@
     )
     columns = [hop(column, m) for m in second]
     (own,) = local(
-        functools.partial(expert_kernel, expert_total, 1),
+        functools.partial(expert_kernel, 1),
         "own_experts",
         [((column_rows, model_width), f32)],
         column,
         *weights,
     )
     results = local(
-        functools.partial(expert_kernel, expert_total, len(second)),
+        functools.partial(expert_kernel, len(second)),
         "experts",
         [((column_rows, model_width), bf16)] * len(second),
         *columns,

time: 40 us -> 39.8 us (level)
    pallas_call x1, Pallas kernels: 4.89 us -> 4.43 us  [shards(): pl.pallas_call(mixer_kernel, out_shape=(jax.ShapeDtypeStruct((token_count...]
  transfers between devices with their start and end apart: 14 -> 14, of which waited for: 11 -> 11; matrix products, arithmetic and copies ran while one was open for 0% -> 0% of each run, Pallas kernels for 14% -> 13%
where the time goes in v6:
time: 39.8 us; the launch traced here: 39.7 us
  starting transfers between devices  17.9 us (45%)
  waiting for transfers between devices  14.4 us (36%)
  Pallas kernels  7.3 us (18%)
    ppermute x14, starting transfers between devices, hop(): return lax.ppermute(x, 'dp', [(i, i ^ masks[i % 2]) for i in range(count)])  17.9 us
    ppermute x14, waiting for transfers between devices, hop(): return lax.ppermute(x, 'dp', [(i, i ^ masks[i % 2]) for i in range(count)])  14.4 us
    pallas_call x1, Pallas kernels, shards(): pl.pallas_call(mixer_kernel, out_shape=(jax.ShapeDtypeStruct((token_count...  4.43 us
    pallas_call x5, Pallas kernels, local(): pl.pallas_call(body, out_shape=tuple((jax.ShapeDtypeStruct(*o) for o in o...  2.86 us
  transfers between devices with their start and end apart: 14, of which 11 were waited for; matrix products, arithmetic and copies ran while one was open for 0% of the time, Pallas kernels for 13%

profile of v6, /device:TPU:0, one launch (start us, length us, event | category | flops | bytes accessed | tf_op | source)
XLA Modules:
  0.0 39.7 jit_solution(17561091726136404132)
XLA Ops:
  0.0 0.0 copy-start
  0.0 0.0 copy-start.1
  0.0 0.0 copy-start.2
  0.0 0.5 %collective-permute-start.3 = (bf16[1,1024,512]{2,1,0:T(8,128)(2,1)}, bf16[1,1024,512]{2,1,0:T(8,128)(2,1)S(1)}, u32[]{:S(2)}, u32[]{:S(2)}) collective-permute-start(bf16[1,1024,512]{2,1,0:T(8,128)(2,1)} %refs_4_.1), channel_id=1, source_target_pairs={{0,1},{1,0},{2,3},{3,2},{4,5},{5,4},{6,7},{7,6},{8,9},{9,8},{10,11... | collective-permute-start | bytes 3145736 | tf_op jit(solution)/shard_map/ppermute | solution.py:270
  0.5 0.1 collective-permute-start.4
  0.6 4.4 %mixer.1 = (bf16[16,1152]{1,0:T(8,128)(2,1)S(1)}, bf16[16,1024]{1,0:T(8,128)(2,1)S(1)}) custom-call(bf16[8,2,1024]{2,1,0:T(2,128)(2,1)} %hidden_hbm.1, bf16[8,2,1024]{2,1,0:T(2,128)(2,1)} %query_hbm.1, bf16[8,2,1024]{2,1,0:T(2,128)(2,1)} %key_hbm.1, bf16[8,2,2048]{2,1,0:T(2,128)(2,1)} %value_hbm.1, bf16[8,2,2048]{2,1,0:T(2,128)(2,1)} %gate_hbm.1, ...), custom_call_target="tpu_custom_call" | custom-call | tf_op jit(solution)/shard_map/mixer/pallas_call | solution.py:325
  5.0 5.1 %collective-permute-start.2 = (bf16[16,1152]{1,0:T(8,128)(2,1)S(1)}, bf16[16,1152]{1,0:T(8,128)(2,1)S(1)}, u32[]{:S(2)}, u32[]{:S(2)}) collective-permute-start(bf16[16,1152]{1,0:T(8,128)(2,1)S(1)} %get-tuple-element.15.refs_0_), channel_id=1, source_target_pairs={{0,24},{1,7},{2,26},{3,5},{4,28},{5,3},{6,30},{7,1},{8,16},{9,15},... | collective-permute-start | bytes 110600 | tf_op jit(solution)/shard_map/ppermute | solution.py:270
  10.1 0.0 collective-permute-start.1
  10.1 0.6 %collective-permute-start = (bf16[16,1152]{1,0:T(8,128)(2,1)S(1)}, bf16[16,1152]{1,0:T(8,128)(2,1)S(1)}, u32[]{:S(2)}, u32[]{:S(2)}) collective-permute-start(bf16[16,1152]{1,0:T(8,128)(2,1)S(1)} %get-tuple-element.15.refs_0_), channel_id=1, source_target_pairs={{0,8},{1,3},{2,10},{3,1},{4,12},{5,7},{6,14},{7,5},{8,0},{9,11},{1... | collective-permute-start | bytes 110600 | tf_op jit(solution)/shard_map/ppermute | solution.py:270
  10.8 1.3 %collective-permute-done.2.refs_3_ = bf16[16,1152]{1,0:T(8,128)(2,1)S(1)} collective-permute-done((bf16[16,1152]{1,0:T(8,128)(2,1)S(1)}, bf16[16,1152]{1,0:T(8,128)(2,1)S(1)}, u32[]{:S(2)}, u32[]{:S(2)}) %collective-permute-start.2) | collective-permute-done | bytes 36896 | tf_op jit(solution)/shard_map/ppermute | solution.py:270
  12.1 2.9 %collective-permute-done.1.refs_2_ = bf16[16,1152]{1,0:T(8,128)(2,1)S(1)} collective-permute-done((bf16[16,1152]{1,0:T(8,128)(2,1)S(1)}, bf16[16,1152]{1,0:T(8,128)(2,1)S(1)}, u32[]{:S(2)}, u32[]{:S(2)}) %collective-permute-start.1) | collective-permute-done | bytes 36896 | tf_op jit(solution)/shard_map/ppermute | solution.py:270
  15.0 0.0 collective-permute-done.refs_1_
  15.0 2.9 %collective-permute-start.7 = (bf16[64,1152]{1,0:T(8,128)(2,1)S(1)}, bf16[64,1152]{1,0:T(8,128)(2,1)S(1)}, u32[]{:S(2)}, u32[]{:S(2)}) collective-permute-start(bf16[64,1152]{1,0:T(8,128)(2,1)S(1)} %column.1.refs_0_), channel_id=1, source_target_pairs={{0,6},{1,25},{2,4},{3,27},{4,2},{5,29},{6,0},{7,31},{8,14},{9,17},... | collective-permute-start | bytes 442376 | tf_op jit(solution)/shard_map/ppermute | solution.py:270
  17.9 0.5 %collective-permute-start.6 = (bf16[64,1152]{1,0:T(8,128)(2,1)S(1)}, bf16[64,1152]{1,0:T(8,128)(2,1)S(1)}, u32[]{:S(2)}, u32[]{:S(2)}) collective-permute-start(bf16[64,1152]{1,0:T(8,128)(2,1)S(1)} %column.1.refs_0_), channel_id=1, source_target_pairs={{0,4},{1,17},{2,6},{3,19},{4,0},{5,21},{6,2},{7,23},{8,12},{9,25},... | collective-permute-start | bytes 442376 | tf_op jit(solution)/shard_map/ppermute | solution.py:270
  18.4 0.1 collective-permute-start.5
  18.6 2.6 %collective-permute-done.7.refs_2_ = bf16[64,1152]{1,0:T(8,128)(2,1)S(1)} collective-permute-done((bf16[64,1152]{1,0:T(8,128)(2,1)S(1)}, bf16[64,1152]{1,0:T(8,128)(2,1)S(1)}, u32[]{:S(2)}, u32[]{:S(2)}) %collective-permute-start.7) | collective-permute-done | bytes 147488 | tf_op jit(solution)/shard_map/ppermute | solution.py:270
  21.1 1.9 %collective-permute-done.6.refs_1_ = bf16[64,1152]{1,0:T(8,128)(2,1)S(1)} collective-permute-done((bf16[64,1152]{1,0:T(8,128)(2,1)S(1)}, bf16[64,1152]{1,0:T(8,128)(2,1)S(1)}, u32[]{:S(2)}, u32[]{:S(2)}) %collective-permute-start.6) | collective-permute-done | bytes 147488 | tf_op jit(solution)/shard_map/ppermute | solution.py:270
  23.1 0.5 %collective-permute-done.5.refs_0_ = bf16[64,1152]{1,0:T(8,128)(2,1)S(1)} collective-permute-done((bf16[64,1152]{1,0:T(8,128)(2,1)S(1)}, bf16[64,1152]{1,0:T(8,128)(2,1)S(1)}, u32[]{:S(2)}, u32[]{:S(2)}) %collective-permute-start.5) | collective-permute-done | bytes 147488 | tf_op jit(solution)/shard_map/ppermute | solution.py:270
  23.6 0.0 collective-permute-done.4.refs_5_.refs_7_
  23.6 0.0 collective-permute-done.3.refs_4_.refs_6_
  23.6 0.0 copy-done
  23.6 0.0 copy-done.1
  23.6 0.0 copy-done.2
  23.6 1.2 %experts.1 = (bf16[64,1024]{1,0:T(8,128)(2,1)S(1)}, bf16[64,1024]{1,0:T(8,128)(2,1)S(1)}, bf16[64,1024]{1,0:T(8,128)(2,1)S(1)}) custom-call(bf16[64,1152]{1,0:T(8,128)(2,1)S(1)} %collective-permute-done.5.refs_0_, bf16[64,1152]{1,0:T(8,128)(2,1)S(1)} %collective-permute-done.6.refs_1_, bf16[64,1152]{1,0:T(8,128)(2,1)S(1)} %collective-permute-done.7.refs_2_, ...), custom_call_target="tpu_custom_call" | custom-call | tf_op jit(solution)/shard_map/experts/pallas_call | solution.py:348
  24.9 1.2 %collective-permute-start.8 = (bf16[64,1024]{1,0:T(8,128)(2,1)S(1)}, bf16[64,1024]{1,0:T(8,128)(2,1)S(1)}, u32[]{:S(2)}, u32[]{:S(2)}) collective-permute-start(bf16[64,1024]{1,0:T(8,128)(2,1)S(1)} %get-tuple-element.16), channel_id=1, source_target_pairs={{0,6},{1,25},{2,4},{3,27},{4,2},{5,29},{6,0},{7,31},{8,14},{9,17},... | collective-permute-start | bytes 393224 | tf_op jit(solution)/shard_map/ppermute | solution.py:270
  26.1 1.4 %collective-permute-start.9 = (bf16[64,1024]{1,0:T(8,128)(2,1)S(1)}, bf16[64,1024]{1,0:T(8,128)(2,1)S(1)}, u32[]{:S(2)}, u32[]{:S(2)}) collective-permute-start(bf16[64,1024]{1,0:T(8,128)(2,1)S(1)} %get-tuple-element.17), channel_id=1, source_target_pairs={{0,4},{1,17},{2,6},{3,19},{4,0},{5,21},{6,2},{7,23},{8,12},{9,25},... | collective-permute-start | bytes 393224 | tf_op jit(solution)/shard_map/ppermute | solution.py:270
  27.5 0.9 %collective-permute-start.10 = (bf16[64,1024]{1,0:T(8,128)(2,1)S(1)}, bf16[64,1024]{1,0:T(8,128)(2,1)S(1)}, u32[]{:S(2)}, u32[]{:S(2)}) collective-permute-start(bf16[64,1024]{1,0:T(8,128)(2,1)S(1)} %get-tuple-element.18), channel_id=1, source_target_pairs={{0,2},{1,9},{2,0},{3,11},{4,6},{5,13},{6,4},{7,15},{8,10},{9,1},{1... | collective-permute-start | bytes 393224 | tf_op jit(solution)/shard_map/ppermute | solution.py:270
  28.4 0.9 %own_experts.1.refs_0_ = f32[64,1024]{1,0:T(8,128)S(1)} custom-call(bf16[64,1152]{1,0:T(8,128)(2,1)S(1)} %column.1.refs_0_, bf16[32,1024]{1,0:T(8,128)(2,1)S(1)} %bitcast.2, bf16[1,1024,512]{2,1,0:T(8,128)(2,1)S(1)} %copy-done, bf16[1,256,1024]{2,1,0:T(8,128)(2,1)S(1)} %copy-done.1, bf16[1,1024,512]{2,1,0:T(8,128)(2,1)S(1)} %collective-permute-done.3.refs_4_.refs_6_, ...), custom_call_target="tpu_custom_call" | custom-call | tf_op jit(solution)/shard_map/own_experts/pallas_call | solution.py:348
  29.3 1.6 %collective-permute-done.8.refs_1_ = bf16[64,1024]{1,0:T(8,128)(2,1)S(1)} collective-permute-done((bf16[64,1024]{1,0:T(8,128)(2,1)S(1)}, bf16[64,1024]{1,0:T(8,128)(2,1)S(1)}, u32[]{:S(2)}, u32[]{:S(2)}) %collective-permute-start.8) | collective-permute-done | bytes 131104 | tf_op jit(solution)/shard_map/ppermute | solution.py:270
  30.9 1.3 %collective-permute-done.9.refs_2_ = bf16[64,1024]{1,0:T(8,128)(2,1)S(1)} collective-permute-done((bf16[64,1024]{1,0:T(8,128)(2,1)S(1)}, bf16[64,1024]{1,0:T(8,128)(2,1)S(1)}, u32[]{:S(2)}, u32[]{:S(2)}) %collective-permute-start.9) | collective-permute-done | bytes 131104 | tf_op jit(solution)/shard_map/ppermute | solution.py:270
  32.2 0.3 collective-permute-done.10.refs_3_
  32.5 0.1 column_sum.1
  32.5 1.1 %collective-permute-start.11 = (bf16[16,1024]{1,0:T(8,128)(2,1)S(1)}, bf16[16,1024]{1,0:T(8,128)(2,1)S(1)}, u32[]{:S(2)}, u32[]{:S(2)}) collective-permute-start(bf16[16,1024]{1,0:T(8,128)(2,1)S(1)} %get-tuple-element.20), channel_id=1, source_target_pairs={{0,24},{1,7},{2,26},{3,5},{4,28},{5,3},{6,30},{7,1},{8,16},{9,15},... | collective-permute-start | bytes 98312 | tf_op jit(solution)/shard_map/ppermute | solution.py:270
  33.7 1.0 %collective-permute-start.12 = (bf16[16,1024]{1,0:T(8,128)(2,1)S(1)}, bf16[16,1024]{1,0:T(8,128)(2,1)S(1)}, u32[]{:S(2)}, u32[]{:S(2)}) collective-permute-start(bf16[16,1024]{1,0:T(8,128)(2,1)S(1)} %get-tuple-element.21), channel_id=1, source_target_pairs={{0,16},{1,5},{2,18},{3,7},{4,20},{5,1},{6,22},{7,3},{8,24},{9,13},... | collective-permute-start | bytes 98312 | tf_op jit(solution)/shard_map/ppermute | solution.py:270
  34.7 2.3 %collective-permute-start.13 = (bf16[16,1024]{1,0:T(8,128)(2,1)S(1)}, bf16[16,1024]{1,0:T(8,128)(2,1)S(1)}, u32[]{:S(2)}, u32[]{:S(2)}) collective-permute-start(bf16[16,1024]{1,0:T(8,128)(2,1)S(1)} %get-tuple-element.22), channel_id=1, source_target_pairs={{0,8},{1,3},{2,10},{3,1},{4,12},{5,7},{6,14},{7,5},{8,0},{9,11},{1... | collective-permute-start | bytes 98312 | tf_op jit(solution)/shard_map/ppermute | solution.py:270
  37.0 1.3 %collective-permute-done.11.refs_2_ = bf16[16,1024]{1,0:T(8,128)(2,1)S(1)} collective-permute-done((bf16[16,1024]{1,0:T(8,128)(2,1)S(1)}, bf16[16,1024]{1,0:T(8,128)(2,1)S(1)}, u32[]{:S(2)}, u32[]{:S(2)}) %collective-permute-start.11) | collective-permute-done | bytes 32800 | tf_op jit(solution)/shard_map/ppermute | solution.py:270
  38.3 0.3 collective-permute-done.12.refs_3_
  38.7 0.3 collective-permute-done.13.refs_4_
  39.0 0.7 %final.1 = bf16[8,2,1024]{2,1,0:T(2,128)(2,1)} custom-call(bf16[16,1024]{1,0:T(8,128)(2,1)S(1)} %get-tuple-element.14.refs_0_, f32[16,1024]{1,0:T(8,128)S(1)} %get-tuple-element.19.refs_1_, bf16[16,1024]{1,0:T(8,128)(2,1)S(1)} %collective-permute-done.11.refs_2_, bf16[16,1024]{1,0:T(8,128)(2,1)S(1)} %collective-permute-done.12.refs_3_, ...), custom_call_target="tpu_custom_call" | custom-call | tf_op jit(solution)/shard_map/final/pallas_call | solution.py:348
  (1 shorter events, 0.0 us)
Async XLA Ops:
  0.0 23.6 %copy-start = (bf16[1,1024,512]{2,1,0:T(8,128)(2,1)S(1)}, bf16[1,1024,512]{2,1,0:T(8,128)(2,1)}, u32[]{:S(2)}) copy-start(bf16[1,1024,512]{2,1,0:T(8,128)(2,1)} %refs_4_.1) | copy-start | bytes 3145732
  0.0 23.6 %copy-start.1 = (bf16[1,256,1024]{2,1,0:T(8,128)(2,1)S(1)}, bf16[1,256,1024]{2,1,0:T(8,128)(2,1)}, u32[]{:S(2)}) copy-start(bf16[1,256,1024]{2,1,0:T(8,128)(2,1)} %refs_5_.1) | copy-start | bytes 1572868
  0.0 23.6 %copy-start.2 = (bf16[1024,32]{0,1:T(8,128)(2,1)S(1)}, bf16[1024,32]{0,1:T(8,128)(2,1)}, u32[]{:S(2)}) copy-start(bf16[1024,32]{0,1:T(8,128)(2,1)} %param.30) | copy-start | bytes 196612
  0.0 23.6 %collective-permute-start.3 = (bf16[1,1024,512]{2,1,0:T(8,128)(2,1)}, bf16[1,1024,512]{2,1,0:T(8,128)(2,1)S(1)}, u32[]{:S(2)}, u32[]{:S(2)}) collective-permute-start(bf16[1,1024,512]{2,1,0:T(8,128)(2,1)} %refs_4_.1), channel_id=1, source_target_pairs={{0,1},{1,0},{2,3},{3,2},{4,5},{5,4},{6,7},{7,6},{8,9},{9,8},{10,11... | collective-permute-start | bytes 3145736 | tf_op jit(solution)/shard_map/ppermute | solution.py:270
  0.5 23.0 %collective-permute-start.4 = (bf16[1,256,1024]{2,1,0:T(8,128)(2,1)}, bf16[1,256,1024]{2,1,0:T(8,128)(2,1)S(1)}, u32[]{:S(2)}, u32[]{:S(2)}) collective-permute-start(bf16[1,256,1024]{2,1,0:T(8,128)(2,1)} %refs_5_.1), channel_id=1, source_target_pairs={{0,1},{1,0},{2,3},{3,2},{4,5},{5,4},{6,7},{7,6},{8,9},{9,8},{10,11... | collective-permute-start | bytes 1572872 | tf_op jit(solution)/shard_map/ppermute | solution.py:270
  5.0 7.0 %collective-permute-start.2 = (bf16[16,1152]{1,0:T(8,128)(2,1)S(1)}, bf16[16,1152]{1,0:T(8,128)(2,1)S(1)}, u32[]{:S(2)}, u32[]{:S(2)}) collective-permute-start(bf16[16,1152]{1,0:T(8,128)(2,1)S(1)} %get-tuple-element.15.refs_0_), channel_id=1, source_target_pairs={{0,24},{1,7},{2,26},{3,5},{4,28},{5,3},{6,30},{7,1},{8,16},{9,15},... | collective-permute-start | bytes 110600 | tf_op jit(solution)/shard_map/ppermute | solution.py:270
  10.1 4.9 %collective-permute-start.1 = (bf16[16,1152]{1,0:T(8,128)(2,1)S(1)}, bf16[16,1152]{1,0:T(8,128)(2,1)S(1)}, u32[]{:S(2)}, u32[]{:S(2)}) collective-permute-start(bf16[16,1152]{1,0:T(8,128)(2,1)S(1)} %get-tuple-element.15.refs_0_), channel_id=1, source_target_pairs={{0,16},{1,5},{2,18},{3,7},{4,20},{5,1},{6,22},{7,3},{8,24},{9,13},... | collective-permute-start | bytes 110600 | tf_op jit(solution)/shard_map/ppermute | solution.py:270
  10.1 4.9 %collective-permute-start = (bf16[16,1152]{1,0:T(8,128)(2,1)S(1)}, bf16[16,1152]{1,0:T(8,128)(2,1)S(1)}, u32[]{:S(2)}, u32[]{:S(2)}) collective-permute-start(bf16[16,1152]{1,0:T(8,128)(2,1)S(1)} %get-tuple-element.15.refs_0_), channel_id=1, source_target_pairs={{0,8},{1,3},{2,10},{3,1},{4,12},{5,7},{6,14},{7,5},{8,0},{9,11},{1... | collective-permute-start | bytes 110600 | tf_op jit(solution)/shard_map/ppermute | solution.py:270
  15.0 6.1 %collective-permute-start.7 = (bf16[64,1152]{1,0:T(8,128)(2,1)S(1)}, bf16[64,1152]{1,0:T(8,128)(2,1)S(1)}, u32[]{:S(2)}, u32[]{:S(2)}) collective-permute-start(bf16[64,1152]{1,0:T(8,128)(2,1)S(1)} %column.1.refs_0_), channel_id=1, source_target_pairs={{0,6},{1,25},{2,4},{3,27},{4,2},{5,29},{6,0},{7,31},{8,14},{9,17},... | collective-permute-start | bytes 442376 | tf_op jit(solution)/shard_map/ppermute | solution.py:270
  17.9 5.1 %collective-permute-start.6 = (bf16[64,1152]{1,0:T(8,128)(2,1)S(1)}, bf16[64,1152]{1,0:T(8,128)(2,1)S(1)}, u32[]{:S(2)}, u32[]{:S(2)}) collective-permute-start(bf16[64,1152]{1,0:T(8,128)(2,1)S(1)} %column.1.refs_0_), channel_id=1, source_target_pairs={{0,4},{1,17},{2,6},{3,19},{4,0},{5,21},{6,2},{7,23},{8,12},{9,25},... | collective-permute-start | bytes 442376 | tf_op jit(solution)/shard_map/ppermute | solution.py:270
  18.4 5.1 %collective-permute-start.5 = (bf16[64,1152]{1,0:T(8,128)(2,1)S(1)}, bf16[64,1152]{1,0:T(8,128)(2,1)S(1)}, u32[]{:S(2)}, u32[]{:S(2)}) collective-permute-start(bf16[64,1152]{1,0:T(8,128)(2,1)S(1)} %column.1.refs_0_), channel_id=1, source_target_pairs={{0,2},{1,9},{2,0},{3,11},{4,6},{5,13},{6,4},{7,15},{8,10},{9,1},{1... | collective-permute-start | bytes 442376 | tf_op jit(solution)/shard_map/ppermute | solution.py:270
  24.9 6.0 %collective-permute-start.8 = (bf16[64,1024]{1,0:T(8,128)(2,1)S(1)}, bf16[64,1024]{1,0:T(8,128)(2,1)S(1)}, u32[]{:S(2)}, u32[]{:S(2)}) collective-permute-start(bf16[64,1024]{1,0:T(8,128)(2,1)S(1)} %get-tuple-element.16), channel_id=1, source_target_pairs={{0,6},{1,25},{2,4},{3,27},{4,2},{5,29},{6,0},{7,31},{8,14},{9,17},... | collective-permute-start | bytes 393224 | tf_op jit(solution)/shard_map/ppermute | solution.py:270
  26.1 6.1 %collective-permute-start.9 = (bf16[64,1024]{1,0:T(8,128)(2,1)S(1)}, bf16[64,1024]{1,0:T(8,128)(2,1)S(1)}, u32[]{:S(2)}, u32[]{:S(2)}) collective-permute-start(bf16[64,1024]{1,0:T(8,128)(2,1)S(1)} %get-tuple-element.17), channel_id=1, source_target_pairs={{0,4},{1,17},{2,6},{3,19},{4,0},{5,21},{6,2},{7,23},{8,12},{9,25},... | collective-permute-start | bytes 393224 | tf_op jit(solution)/shard_map/ppermute | solution.py:270
  27.5 5.0 %collective-permute-start.10 = (bf16[64,1024]{1,0:T(8,128)(2,1)S(1)}, bf16[64,1024]{1,0:T(8,128)(2,1)S(1)}, u32[]{:S(2)}, u32[]{:S(2)}) collective-permute-start(bf16[64,1024]{1,0:T(8,128)(2,1)S(1)} %get-tuple-element.18), channel_id=1, source_target_pairs={{0,2},{1,9},{2,0},{3,11},{4,6},{5,13},{6,4},{7,15},{8,10},{9,1},{1... | collective-permute-start | bytes 393224 | tf_op jit(solution)/shard_map/ppermute | solution.py:270
  32.5 5.8 %collective-permute-start.11 = (bf16[16,1024]{1,0:T(8,128)(2,1)S(1)}, bf16[16,1024]{1,0:T(8,128)(2,1)S(1)}, u32[]{:S(2)}, u32[]{:S(2)}) collective-permute-start(bf16[16,1024]{1,0:T(8,128)(2,1)S(1)} %get-tuple-element.20), channel_id=1, source_target_pairs={{0,24},{1,7},{2,26},{3,5},{4,28},{5,3},{6,30},{7,1},{8,16},{9,15},... | collective-permute-start | bytes 98312 | tf_op jit(solution)/shard_map/ppermute | solution.py:270
  33.7 5.0 %collective-permute-start.12 = (bf16[16,1024]{1,0:T(8,128)(2,1)S(1)}, bf16[16,1024]{1,0:T(8,128)(2,1)S(1)}, u32[]{:S(2)}, u32[]{:S(2)}) collective-permute-start(bf16[16,1024]{1,0:T(8,128)(2,1)S(1)} %get-tuple-element.21), channel_id=1, source_target_pairs={{0,16},{1,5},{2,18},{3,7},{4,20},{5,1},{6,22},{7,3},{8,24},{9,13},... | collective-permute-start | bytes 98312 | tf_op jit(solution)/shard_map/ppermute | solution.py:270
  34.7 4.4 %collective-permute-start.13 = (bf16[16,1024]{1,0:T(8,128)(2,1)S(1)}, bf16[16,1024]{1,0:T(8,128)(2,1)S(1)}, u32[]{:S(2)}, u32[]{:S(2)}) collective-permute-start(bf16[16,1024]{1,0:T(8,128)(2,1)S(1)} %get-tuple-element.22), channel_id=1, source_target_pairs={{0,8},{1,3},{2,10},{3,1},{4,12},{5,7},{6,14},{7,5},{8,0},{9,11},{1... | collective-permute-start | bytes 98312 | tf_op jit(solution)/shard_map/ppermute | solution.py:270

commit v7 on v6

--- a/solution.py
+++ b/solution.py
@@ -200,23 +200,54 @@
     routed_ref[:, : routed.shape[1]] = routed
 
 
-def column_kernel(*refs):
+def choice_place(experts, piece):
+    per = max(1, 128 // experts)
+    return piece // per, piece % per * experts
+
+
+def column_kernel(experts, *refs):
     out_ref = refs[-1]
-    rows = refs[0].shape[0]
-    for i, ref in enumerate(refs[:-1]):
-        out_ref[i * rows : (i + 1) * rows, :] = ref[...]
-
-
-def expert_kernel(count, *refs):
+    pieces = refs[:-1]
+    tokens = pieces[0].shape[0]
+    width = pieces[0].shape[1] - 128
+    column = tokens * len(pieces)
+    for i, ref in enumerate(pieces):
+        for j in range(width // 128):
+            first = j * column + i * tokens
+            out_ref[first : first + tokens, :] = ref[:, j * 128 : (j + 1) * 128]
+    groups = {}
+    for i, ref in enumerate(pieces):
+        group, start = choice_place(experts, i)
+        choices = ref[:, width:].astype(f32)
+        if start:
+            choices = pltpu.roll(choices, start, 1)
+        groups[group] = choices + groups.get(group, 0.0)
+    first = column * (width // 128)
+    for group, choices in groups.items():
+        out_ref[first + group * tokens : first + (group + 1) * tokens, :] = choices.astype(bf16)
+
+
+def expert_kernel(tokens, count, *refs):
     blocks = refs[:count]
     router, up_own, down_own, up_other, down_other = refs[count : count + 5]
     outs = refs[count + 5 :]
     rows, width = outs[0].shape
     hidden_units = down_own.shape[1]
     me = lax.axis_index("dp")
-    both_parts = blocks[0][...] if count == 1 else jnp.concatenate([b[...] for b in blocks], axis=0)
-    x = both_parts[:, :width]
-    chosen = both_parts[:, width:].astype(f32)[:, : router.shape[0]] > 0.0
+    experts = router.shape[0]
+    blocks_rows, blocks_chosen = [], []
+    for block in blocks:
+        parts = [block[j * rows : (j + 1) * rows, :] for j in range(width // 128)]
+        blocks_rows.append(jnp.concatenate(parts, axis=-1))
+        for i in range(rows // tokens):
+            group, start = choice_place(experts, i)
+            first = rows * (width // 128) + group * tokens
+            choices = block[first : first + tokens, :].astype(f32)
+            if start:
+                choices = pltpu.roll(choices, 128 - start, 1)
+            blocks_chosen.append(choices[:, :experts])
+    x = jnp.concatenate(blocks_rows, axis=0)
+    chosen = jnp.concatenate(blocks_chosen, axis=0) > 0.0
     raised = jnp.where(chosen, jnp.exp(nt_dot(x, router[...])), 0.0)
     whole = jnp.sum(raised, axis=-1, keepdims=True)
     lane = lax.broadcasted_iota(jnp.int32, raised.shape, 1)
@@ -300,7 +331,7 @@
     key_heads = query_in.shape[2] // key_size
     share = value_heads // key_heads
     token_count = row_count * 2
-    sent_width = model_width + (expert_total + 127) // 128 * 128
+    sent_width = model_width + 128
     first, second = chip_masks(device_count)
     chunks = 2
     params = pltpu.CompilerParams(vmem_limit_bytes=48 * 1024 * 1024)
@@ -356,20 +387,26 @@
 
     weights = (router_weight.T, expert_gate_up, expert_down, up_other, down_other)
     column_rows = token_count * (len(first) + 1)
+    groups = choice_place(expert_total, len(first))[0] + 1
+    column_size = column_rows * (model_width // 128) + groups * token_count
     pieces = [hop(routed, m) for m in first]
     (column,) = local(
-        column_kernel, "column", [((column_rows, sent_width), bf16)], routed, *pieces
+        functools.partial(column_kernel, expert_total),
+        "column",
+        [((column_size, 128), bf16)],
+        routed,
+        *pieces,
     )
     columns = [hop(column, m) for m in second]
     (own,) = local(
-        functools.partial(expert_kernel, 1),
+        functools.partial(expert_kernel, token_count, 1),
         "own_experts",
         [((column_rows, model_width), f32)],
         column,
         *weights,
     )
     results = local(
-        functools.partial(expert_kernel, len(second)),
+        functools.partial(expert_kernel, token_count, len(second)),
         "experts",
         [((column_rows, model_width), bf16)] * len(second),
         *columns,

time: 39.8 us -> 39.6 us (level)
  transfers between devices with their start and end apart: 14 -> 14, of which waited for: 11 -> 11; matrix products, arithmetic and copies ran while one was open for 0% -> 0% of each run, Pallas kernels for 13% -> 14%
where the time goes in v7:
time: 39.6 us; the launch traced here: 39.4 us
  starting transfers between devices  17.8 us (45%)
  waiting for transfers between devices  14.1 us (36%)
  Pallas kernels  7.41 us (19%)
    ppermute x14, starting transfers between devices, hop(): return lax.ppermute(x, 'dp', [(i, i ^ masks[i % 2]) for i in range(count)])  17.8 us
    ppermute x14, waiting for transfers between devices, hop(): return lax.ppermute(x, 'dp', [(i, i ^ masks[i % 2]) for i in range(count)])  14.1 us
    pallas_call x1, Pallas kernels, shards(): pl.pallas_call(mixer_kernel, out_shape=(jax.ShapeDtypeStruct((token_count...  4.43 us
    pallas_call x5, Pallas kernels, local(): pl.pallas_call(body, out_shape=tuple((jax.ShapeDtypeStruct(*o) for o in o...  2.98 us
  transfers between devices with their start and end apart: 14, of which 11 were waited for; matrix products, arithmetic and copies ran while one was open for 0% of the time, Pallas kernels for 14%

profile of v7, /device:TPU:0, one launch (start us, length us, event | category | flops | bytes accessed | tf_op | source)
XLA Modules:
  0.0 39.4 jit_solution(1963635807326562976)
XLA Ops:
  0.0 0.0 copy-start
  0.0 0.0 copy-start.1
  0.0 0.0 copy-start.2
  0.0 0.5 %collective-permute-start.3 = (bf16[1,1024,512]{2,1,0:T(8,128)(2,1)}, bf16[1,1024,512]{2,1,0:T(8,128)(2,1)S(1)}, u32[]{:S(2)}, u32[]{:S(2)}) collective-permute-start(bf16[1,1024,512]{2,1,0:T(8,128)(2,1)} %refs_4_.1), channel_id=1, source_target_pairs={{0,1},{1,0},{2,3},{3,2},{4,5},{5,4},{6,7},{7,6},{8,9},{9,8},{10,11... | collective-permute-start | bytes 3145736 | tf_op jit(solution)/shard_map/ppermute | solution.py:301
  0.5 0.1 collective-permute-start.4
  0.6 4.4 %mixer.1 = (bf16[16,1152]{1,0:T(8,128)(2,1)S(1)}, bf16[16,1024]{1,0:T(8,128)(2,1)S(1)}) custom-call(bf16[8,2,1024]{2,1,0:T(2,128)(2,1)} %hidden_hbm.1, bf16[8,2,1024]{2,1,0:T(2,128)(2,1)} %query_hbm.1, bf16[8,2,1024]{2,1,0:T(2,128)(2,1)} %key_hbm.1, bf16[8,2,2048]{2,1,0:T(2,128)(2,1)} %value_hbm.1, bf16[8,2,2048]{2,1,0:T(2,128)(2,1)} %gate_hbm.1, ...), custom_call_target="tpu_custom_call" | custom-call | tf_op jit(solution)/shard_map/mixer/pallas_call | solution.py:356
  5.0 5.1 %collective-permute-start.2 = (bf16[16,1152]{1,0:T(8,128)(2,1)S(1)}, bf16[16,1152]{1,0:T(8,128)(2,1)S(1)}, u32[]{:S(2)}, u32[]{:S(2)}) collective-permute-start(bf16[16,1152]{1,0:T(8,128)(2,1)S(1)} %get-tuple-element.15.refs_0_), channel_id=1, source_target_pairs={{0,24},{1,7},{2,26},{3,5},{4,28},{5,3},{6,30},{7,1},{8,16},{9,15},... | collective-permute-start | bytes 110600 | tf_op jit(solution)/shard_map/ppermute | solution.py:301
  10.1 0.0 collective-permute-start.1
  10.1 0.6 %collective-permute-start = (bf16[16,1152]{1,0:T(8,128)(2,1)S(1)}, bf16[16,1152]{1,0:T(8,128)(2,1)S(1)}, u32[]{:S(2)}, u32[]{:S(2)}) collective-permute-start(bf16[16,1152]{1,0:T(8,128)(2,1)S(1)} %get-tuple-element.15.refs_0_), channel_id=1, source_target_pairs={{0,8},{1,3},{2,10},{3,1},{4,12},{5,7},{6,14},{7,5},{8,0},{9,11},{1... | collective-permute-start | bytes 110600 | tf_op jit(solution)/shard_map/ppermute | solution.py:301
  10.8 1.3 %collective-permute-done.2.refs_3_ = bf16[16,1152]{1,0:T(8,128)(2,1)S(1)} collective-permute-done((bf16[16,1152]{1,0:T(8,128)(2,1)S(1)}, bf16[16,1152]{1,0:T(8,128)(2,1)S(1)}, u32[]{:S(2)}, u32[]{:S(2)}) %collective-permute-start.2) | collective-permute-done | bytes 36896 | tf_op jit(solution)/shard_map/ppermute | solution.py:301
  12.1 2.9 %collective-permute-done.1.refs_2_ = bf16[16,1152]{1,0:T(8,128)(2,1)S(1)} collective-permute-done((bf16[16,1152]{1,0:T(8,128)(2,1)S(1)}, bf16[16,1152]{1,0:T(8,128)(2,1)S(1)}, u32[]{:S(2)}, u32[]{:S(2)}) %collective-permute-start.1) | collective-permute-done | bytes 36896 | tf_op jit(solution)/shard_map/ppermute | solution.py:301
  15.0 0.0 collective-permute-done.refs_1_
  15.0 0.1 column.1.refs_0_
  15.1 2.9 %collective-permute-start.7 = (bf16[528,128]{1,0:T(8,128)(2,1)S(1)}, bf16[528,128]{1,0:T(8,128)(2,1)S(1)}, u32[]{:S(2)}, u32[]{:S(2)}) collective-permute-start(bf16[528,128]{1,0:T(8,128)(2,1)S(1)} %column.1.refs_0_), channel_id=1, source_target_pairs={{0,6},{1,25},{2,4},{3,27},{4,2},{5,29},{6,0},{7,31},{8,14},{9,17},... | collective-permute-start | bytes 405512 | tf_op jit(solution)/shard_map/ppermute | solution.py:301
  17.9 0.5 %collective-permute-start.6 = (bf16[528,128]{1,0:T(8,128)(2,1)S(1)}, bf16[528,128]{1,0:T(8,128)(2,1)S(1)}, u32[]{:S(2)}, u32[]{:S(2)}) collective-permute-start(bf16[528,128]{1,0:T(8,128)(2,1)S(1)} %column.1.refs_0_), channel_id=1, source_target_pairs={{0,4},{1,17},{2,6},{3,19},{4,0},{5,21},{6,2},{7,23},{8,12},{9,25},... | collective-permute-start | bytes 405512 | tf_op jit(solution)/shard_map/ppermute | solution.py:301
  18.4 0.1 collective-permute-start.5
  18.6 2.4 %collective-permute-done.7.refs_2_ = bf16[528,128]{1,0:T(8,128)(2,1)S(1)} collective-permute-done((bf16[528,128]{1,0:T(8,128)(2,1)S(1)}, bf16[528,128]{1,0:T(8,128)(2,1)S(1)}, u32[]{:S(2)}, u32[]{:S(2)}) %collective-permute-start.7) | collective-permute-done | bytes 135200 | tf_op jit(solution)/shard_map/ppermute | solution.py:301
  21.0 1.9 %collective-permute-done.6.refs_1_ = bf16[528,128]{1,0:T(8,128)(2,1)S(1)} collective-permute-done((bf16[528,128]{1,0:T(8,128)(2,1)S(1)}, bf16[528,128]{1,0:T(8,128)(2,1)S(1)}, u32[]{:S(2)}, u32[]{:S(2)}) %collective-permute-start.6) | collective-permute-done | bytes 135200 | tf_op jit(solution)/shard_map/ppermute | solution.py:301
  23.0 0.5 %collective-permute-done.5.refs_0_ = bf16[528,128]{1,0:T(8,128)(2,1)S(1)} collective-permute-done((bf16[528,128]{1,0:T(8,128)(2,1)S(1)}, bf16[528,128]{1,0:T(8,128)(2,1)S(1)}, u32[]{:S(2)}, u32[]{:S(2)}) %collective-permute-start.5) | collective-permute-done | bytes 135200 | tf_op jit(solution)/shard_map/ppermute | solution.py:301
  23.5 0.0 collective-permute-done.4.refs_5_.refs_7_
  23.5 0.0 collective-permute-done.3.refs_4_.refs_6_
  23.5 0.0 copy-done
  23.5 0.0 copy-done.1
  23.5 0.0 copy-done.2
  23.5 1.3 %experts.1 = (bf16[64,1024]{1,0:T(8,128)(2,1)S(1)}, bf16[64,1024]{1,0:T(8,128)(2,1)S(1)}, bf16[64,1024]{1,0:T(8,128)(2,1)S(1)}) custom-call(bf16[528,128]{1,0:T(8,128)(2,1)S(1)} %collective-permute-done.5.refs_0_, bf16[528,128]{1,0:T(8,128)(2,1)S(1)} %collective-permute-done.6.refs_1_, bf16[528,128]{1,0:T(8,128)(2,1)S(1)} %collective-permute-done.7.refs_2_, ...), custom_call_target="tpu_custom_call" | custom-call | tf_op jit(solution)/shard_map/experts/pallas_call | solution.py:379
  24.8 1.2 %collective-permute-start.8 = (bf16[64,1024]{1,0:T(8,128)(2,1)S(1)}, bf16[64,1024]{1,0:T(8,128)(2,1)S(1)}, u32[]{:S(2)}, u32[]{:S(2)}) collective-permute-start(bf16[64,1024]{1,0:T(8,128)(2,1)S(1)} %get-tuple-element.16), channel_id=1, source_target_pairs={{0,6},{1,25},{2,4},{3,27},{4,2},{5,29},{6,0},{7,31},{8,14},{9,17},... | collective-permute-start | bytes 393224 | tf_op jit(solution)/shard_map/ppermute | solution.py:301
  25.9 1.4 %collective-permute-start.9 = (bf16[64,1024]{1,0:T(8,128)(2,1)S(1)}, bf16[64,1024]{1,0:T(8,128)(2,1)S(1)}, u32[]{:S(2)}, u32[]{:S(2)}) collective-permute-start(bf16[64,1024]{1,0:T(8,128)(2,1)S(1)} %get-tuple-element.17), channel_id=1, source_target_pairs={{0,4},{1,17},{2,6},{3,19},{4,0},{5,21},{6,2},{7,23},{8,12},{9,25},... | collective-permute-start | bytes 393224 | tf_op jit(solution)/shard_map/ppermute | solution.py:301
  27.3 1.0 %collective-permute-start.10 = (bf16[64,1024]{1,0:T(8,128)(2,1)S(1)}, bf16[64,1024]{1,0:T(8,128)(2,1)S(1)}, u32[]{:S(2)}, u32[]{:S(2)}) collective-permute-start(bf16[64,1024]{1,0:T(8,128)(2,1)S(1)} %get-tuple-element.18), channel_id=1, source_target_pairs={{0,2},{1,9},{2,0},{3,11},{4,6},{5,13},{6,4},{7,15},{8,10},{9,1},{1... | collective-permute-start | bytes 393224 | tf_op jit(solution)/shard_map/ppermute | solution.py:301
  28.3 0.9 %own_experts.1.refs_0_ = f32[64,1024]{1,0:T(8,128)S(1)} custom-call(bf16[528,128]{1,0:T(8,128)(2,1)S(1)} %column.1.refs_0_, bf16[32,1024]{1,0:T(8,128)(2,1)S(1)} %bitcast.2, bf16[1,1024,512]{2,1,0:T(8,128)(2,1)S(1)} %copy-done, bf16[1,256,1024]{2,1,0:T(8,128)(2,1)S(1)} %copy-done.1, bf16[1,1024,512]{2,1,0:T(8,128)(2,1)S(1)} %collective-permute-done.3.refs_4_.refs_6_, ...), custom_call_target="tpu_custom_call" | custom-call | tf_op jit(solution)/shard_map/own_experts/pallas_call | solution.py:379
  29.2 1.6 %collective-permute-done.8.refs_1_ = bf16[64,1024]{1,0:T(8,128)(2,1)S(1)} collective-permute-done((bf16[64,1024]{1,0:T(8,128)(2,1)S(1)}, bf16[64,1024]{1,0:T(8,128)(2,1)S(1)}, u32[]{:S(2)}, u32[]{:S(2)}) %collective-permute-start.8) | collective-permute-done | bytes 131104 | tf_op jit(solution)/shard_map/ppermute | solution.py:301
  30.8 1.3 %collective-permute-done.9.refs_2_ = bf16[64,1024]{1,0:T(8,128)(2,1)S(1)} collective-permute-done((bf16[64,1024]{1,0:T(8,128)(2,1)S(1)}, bf16[64,1024]{1,0:T(8,128)(2,1)S(1)}, u32[]{:S(2)}, u32[]{:S(2)}) %collective-permute-start.9) | collective-permute-done | bytes 131104 | tf_op jit(solution)/shard_map/ppermute | solution.py:301
  32.1 0.1 collective-permute-done.10.refs_3_
  32.2 0.1 column_sum.1
  32.3 1.1 %collective-permute-start.11 = (bf16[16,1024]{1,0:T(8,128)(2,1)S(1)}, bf16[16,1024]{1,0:T(8,128)(2,1)S(1)}, u32[]{:S(2)}, u32[]{:S(2)}) collective-permute-start(bf16[16,1024]{1,0:T(8,128)(2,1)S(1)} %get-tuple-element.20), channel_id=1, source_target_pairs={{0,24},{1,7},{2,26},{3,5},{4,28},{5,3},{6,30},{7,1},{8,16},{9,15},... | collective-permute-start | bytes 98312 | tf_op jit(solution)/shard_map/ppermute | solution.py:301
  33.5 1.0 %collective-permute-start.12 = (bf16[16,1024]{1,0:T(8,128)(2,1)S(1)}, bf16[16,1024]{1,0:T(8,128)(2,1)S(1)}, u32[]{:S(2)}, u32[]{:S(2)}) collective-permute-start(bf16[16,1024]{1,0:T(8,128)(2,1)S(1)} %get-tuple-element.21), channel_id=1, source_target_pairs={{0,16},{1,5},{2,18},{3,7},{4,20},{5,1},{6,22},{7,3},{8,24},{9,13},... | collective-permute-start | bytes 98312 | tf_op jit(solution)/shard_map/ppermute | solution.py:301
  34.4 2.3 %collective-permute-start.13 = (bf16[16,1024]{1,0:T(8,128)(2,1)S(1)}, bf16[16,1024]{1,0:T(8,128)(2,1)S(1)}, u32[]{:S(2)}, u32[]{:S(2)}) collective-permute-start(bf16[16,1024]{1,0:T(8,128)(2,1)S(1)} %get-tuple-element.22), channel_id=1, source_target_pairs={{0,8},{1,3},{2,10},{3,1},{4,12},{5,7},{6,14},{7,5},{8,0},{9,11},{1... | collective-permute-start | bytes 98312 | tf_op jit(solution)/shard_map/ppermute | solution.py:301
  36.8 1.3 %collective-permute-done.11.refs_2_ = bf16[16,1024]{1,0:T(8,128)(2,1)S(1)} collective-permute-done((bf16[16,1024]{1,0:T(8,128)(2,1)S(1)}, bf16[16,1024]{1,0:T(8,128)(2,1)S(1)}, u32[]{:S(2)}, u32[]{:S(2)}) %collective-permute-start.11) | collective-permute-done | bytes 32800 | tf_op jit(solution)/shard_map/ppermute | solution.py:301
  38.1 0.3 collective-permute-done.12.refs_3_
  38.5 0.3 collective-permute-done.13.refs_4_
  38.8 0.7 %final.1 = bf16[8,2,1024]{2,1,0:T(2,128)(2,1)} custom-call(bf16[16,1024]{1,0:T(8,128)(2,1)S(1)} %get-tuple-element.14.refs_0_, f32[16,1024]{1,0:T(8,128)S(1)} %get-tuple-element.19.refs_1_, bf16[16,1024]{1,0:T(8,128)(2,1)S(1)} %collective-permute-done.11.refs_2_, bf16[16,1024]{1,0:T(8,128)(2,1)S(1)} %collective-permute-done.12.refs_3_, ...), custom_call_target="tpu_custom_call" | custom-call | tf_op jit(solution)/shard_map/final/pallas_call | solution.py:379
Async XLA Ops:
  0.0 23.5 %copy-start = (bf16[1,1024,512]{2,1,0:T(8,128)(2,1)S(1)}, bf16[1,1024,512]{2,1,0:T(8,128)(2,1)}, u32[]{:S(2)}) copy-start(bf16[1,1024,512]{2,1,0:T(8,128)(2,1)} %refs_4_.1) | copy-start | bytes 3145732
  0.0 23.5 %copy-start.1 = (bf16[1,256,1024]{2,1,0:T(8,128)(2,1)S(1)}, bf16[1,256,1024]{2,1,0:T(8,128)(2,1)}, u32[]{:S(2)}) copy-start(bf16[1,256,1024]{2,1,0:T(8,128)(2,1)} %refs_5_.1) | copy-start | bytes 1572868
  0.0 23.5 %copy-start.2 = (bf16[1024,32]{0,1:T(8,128)(2,1)S(1)}, bf16[1024,32]{0,1:T(8,128)(2,1)}, u32[]{:S(2)}) copy-start(bf16[1024,32]{0,1:T(8,128)(2,1)} %param.30) | copy-start | bytes 196612
  0.0 23.5 %collective-permute-start.3 = (bf16[1,1024,512]{2,1,0:T(8,128)(2,1)}, bf16[1,1024,512]{2,1,0:T(8,128)(2,1)S(1)}, u32[]{:S(2)}, u32[]{:S(2)}) collective-permute-start(bf16[1,1024,512]{2,1,0:T(8,128)(2,1)} %refs_4_.1), channel_id=1, source_target_pairs={{0,1},{1,0},{2,3},{3,2},{4,5},{5,4},{6,7},{7,6},{8,9},{9,8},{10,11... | collective-permute-start | bytes 3145736 | tf_op jit(solution)/shard_map/ppermute | solution.py:301
  0.5 22.9 %collective-permute-start.4 = (bf16[1,256,1024]{2,1,0:T(8,128)(2,1)}, bf16[1,256,1024]{2,1,0:T(8,128)(2,1)S(1)}, u32[]{:S(2)}, u32[]{:S(2)}) collective-permute-start(bf16[1,256,1024]{2,1,0:T(8,128)(2,1)} %refs_5_.1), channel_id=1, source_target_pairs={{0,1},{1,0},{2,3},{3,2},{4,5},{5,4},{6,7},{7,6},{8,9},{9,8},{10,11... | collective-permute-start | bytes 1572872 | tf_op jit(solution)/shard_map/ppermute | solution.py:301
  5.0 7.0 %collective-permute-start.2 = (bf16[16,1152]{1,0:T(8,128)(2,1)S(1)}, bf16[16,1152]{1,0:T(8,128)(2,1)S(1)}, u32[]{:S(2)}, u32[]{:S(2)}) collective-permute-start(bf16[16,1152]{1,0:T(8,128)(2,1)S(1)} %get-tuple-element.15.refs_0_), channel_id=1, source_target_pairs={{0,24},{1,7},{2,26},{3,5},{4,28},{5,3},{6,30},{7,1},{8,16},{9,15},... | collective-permute-start | bytes 110600 | tf_op jit(solution)/shard_map/ppermute | solution.py:301
  10.1 4.9 %collective-permute-start.1 = (bf16[16,1152]{1,0:T(8,128)(2,1)S(1)}, bf16[16,1152]{1,0:T(8,128)(2,1)S(1)}, u32[]{:S(2)}, u32[]{:S(2)}) collective-permute-start(bf16[16,1152]{1,0:T(8,128)(2,1)S(1)} %get-tuple-element.15.refs_0_), channel_id=1, source_target_pairs={{0,16},{1,5},{2,18},{3,7},{4,20},{5,1},{6,22},{7,3},{8,24},{9,13},... | collective-permute-start | bytes 110600 | tf_op jit(solution)/shard_map/ppermute | solution.py:301
  10.1 4.9 %collective-permute-start = (bf16[16,1152]{1,0:T(8,128)(2,1)S(1)}, bf16[16,1152]{1,0:T(8,128)(2,1)S(1)}, u32[]{:S(2)}, u32[]{:S(2)}) collective-permute-start(bf16[16,1152]{1,0:T(8,128)(2,1)S(1)} %get-tuple-element.15.refs_0_), channel_id=1, source_target_pairs={{0,8},{1,3},{2,10},{3,1},{4,12},{5,7},{6,14},{7,5},{8,0},{9,11},{1... | collective-permute-start | bytes 110600 | tf_op jit(solution)/shard_map/ppermute | solution.py:301
  15.1 5.9 %collective-permute-start.7 = (bf16[528,128]{1,0:T(8,128)(2,1)S(1)}, bf16[528,128]{1,0:T(8,128)(2,1)S(1)}, u32[]{:S(2)}, u32[]{:S(2)}) collective-permute-start(bf16[528,128]{1,0:T(8,128)(2,1)S(1)} %column.1.refs_0_), channel_id=1, source_target_pairs={{0,6},{1,25},{2,4},{3,27},{4,2},{5,29},{6,0},{7,31},{8,14},{9,17},... | collective-permute-start | bytes 405512 | tf_op jit(solution)/shard_map/ppermute | solution.py:301
  17.9 5.0 %collective-permute-start.6 = (bf16[528,128]{1,0:T(8,128)(2,1)S(1)}, bf16[528,128]{1,0:T(8,128)(2,1)S(1)}, u32[]{:S(2)}, u32[]{:S(2)}) collective-permute-start(bf16[528,128]{1,0:T(8,128)(2,1)S(1)} %column.1.refs_0_), channel_id=1, source_target_pairs={{0,4},{1,17},{2,6},{3,19},{4,0},{5,21},{6,2},{7,23},{8,12},{9,25},... | collective-permute-start | bytes 405512 | tf_op jit(solution)/shard_map/ppermute | solution.py:301
  18.4 5.0 %collective-permute-start.5 = (bf16[528,128]{1,0:T(8,128)(2,1)S(1)}, bf16[528,128]{1,0:T(8,128)(2,1)S(1)}, u32[]{:S(2)}, u32[]{:S(2)}) collective-permute-start(bf16[528,128]{1,0:T(8,128)(2,1)S(1)} %column.1.refs_0_), channel_id=1, source_target_pairs={{0,2},{1,9},{2,0},{3,11},{4,6},{5,13},{6,4},{7,15},{8,10},{9,1},{1... | collective-permute-start | bytes 405512 | tf_op jit(solution)/shard_map/ppermute | solution.py:301
  24.8 6.0 %collective-permute-start.8 = (bf16[64,1024]{1,0:T(8,128)(2,1)S(1)}, bf16[64,1024]{1,0:T(8,128)(2,1)S(1)}, u32[]{:S(2)}, u32[]{:S(2)}) collective-permute-start(bf16[64,1024]{1,0:T(8,128)(2,1)S(1)} %get-tuple-element.16), channel_id=1, source_target_pairs={{0,6},{1,25},{2,4},{3,27},{4,2},{5,29},{6,0},{7,31},{8,14},{9,17},... | collective-permute-start | bytes 393224 | tf_op jit(solution)/shard_map/ppermute | solution.py:301
  25.9 6.2 %collective-permute-start.9 = (bf16[64,1024]{1,0:T(8,128)(2,1)S(1)}, bf16[64,1024]{1,0:T(8,128)(2,1)S(1)}, u32[]{:S(2)}, u32[]{:S(2)}) collective-permute-start(bf16[64,1024]{1,0:T(8,128)(2,1)S(1)} %get-tuple-element.17), channel_id=1, source_target_pairs={{0,4},{1,17},{2,6},{3,19},{4,0},{5,21},{6,2},{7,23},{8,12},{9,25},... | collective-permute-start | bytes 393224 | tf_op jit(solution)/shard_map/ppermute | solution.py:301
  27.3 5.0 %collective-permute-start.10 = (bf16[64,1024]{1,0:T(8,128)(2,1)S(1)}, bf16[64,1024]{1,0:T(8,128)(2,1)S(1)}, u32[]{:S(2)}, u32[]{:S(2)}) collective-permute-start(bf16[64,1024]{1,0:T(8,128)(2,1)S(1)} %get-tuple-element.18), channel_id=1, source_target_pairs={{0,2},{1,9},{2,0},{3,11},{4,6},{5,13},{6,4},{7,15},{8,10},{9,1},{1... | collective-permute-start | bytes 393224 | tf_op jit(solution)/shard_map/ppermute | solution.py:301
  32.3 5.8 %collective-permute-start.11 = (bf16[16,1024]{1,0:T(8,128)(2,1)S(1)}, bf16[16,1024]{1,0:T(8,128)(2,1)S(1)}, u32[]{:S(2)}, u32[]{:S(2)}) collective-permute-start(bf16[16,1024]{1,0:T(8,128)(2,1)S(1)} %get-tuple-element.20), channel_id=1, source_target_pairs={{0,24},{1,7},{2,26},{3,5},{4,28},{5,3},{6,30},{7,1},{8,16},{9,15},... | collective-permute-start | bytes 98312 | tf_op jit(solution)/shard_map/ppermute | solution.py:301
  33.5 5.0 %collective-permute-start.12 = (bf16[16,1024]{1,0:T(8,128)(2,1)S(1)}, bf16[16,1024]{1,0:T(8,128)(2,1)S(1)}, u32[]{:S(2)}, u32[]{:S(2)}) collective-permute-start(bf16[16,1024]{1,0:T(8,128)(2,1)S(1)} %get-tuple-element.21), channel_id=1, source_target_pairs={{0,16},{1,5},{2,18},{3,7},{4,20},{5,1},{6,22},{7,3},{8,24},{9,13},... | collective-permute-start | bytes 98312 | tf_op jit(solution)/shard_map/ppermute | solution.py:301
  34.4 4.4 %collective-permute-start.13 = (bf16[16,1024]{1,0:T(8,128)(2,1)S(1)}, bf16[16,1024]{1,0:T(8,128)(2,1)S(1)}, u32[]{:S(2)}, u32[]{:S(2)}) collective-permute-start(bf16[16,1024]{1,0:T(8,128)(2,1)S(1)} %get-tuple-element.22), channel_id=1, source_target_pairs={{0,8},{1,3},{2,10},{3,1},{4,12},{5,7},{6,14},{7,5},{8,0},{9,11},{1... | collective-permute-start | bytes 98312 | tf_op jit(solution)/shard_map/ppermute | solution.py:301

commit v8 on v7

--- a/solution.py
+++ b/solution.py
@@ -293,7 +293,8 @@
     far = [m << (1 + low) for m in range(1, 1 << (bits - low))]
     if len(near) != len(far):
         return list(zip(far, far)), list(zip(near, near))
-    return list(zip(far, near)), list(zip(near, far))
+    turned = [near[1], near[0], *near[2:]]
+    return list(zip(far, near)), list(zip(turned, far))
 
 
 def hop(x, masks):

time: 39.6 us -> 39.3 us (level)
  no operation moved by 1% of the time
where the time goes in v8:
time: 39.3 us; the launch traced here: 39.2 us
  starting transfers between devices  17.8 us (45%)
  waiting for transfers between devices  13.9 us (35%)
  Pallas kernels  7.4 us (19%)
    ppermute x14, starting transfers between devices, hop(): return lax.ppermute(x, 'dp', [(i, i ^ masks[i % 2]) for i in range(count)])  17.8 us
    ppermute x14, waiting for transfers between devices, hop(): return lax.ppermute(x, 'dp', [(i, i ^ masks[i % 2]) for i in range(count)])  13.9 us
    pallas_call x1, Pallas kernels, shards(): pl.pallas_call(mixer_kernel, out_shape=(jax.ShapeDtypeStruct((token_count...  4.43 us
    pallas_call x5, Pallas kernels, local(): pl.pallas_call(body, out_shape=tuple((jax.ShapeDtypeStruct(*o) for o in o...  2.97 us
  transfers between devices with their start and end apart: 14, of which 11 were waited for; matrix products, arithmetic and copies ran while one was open for 0% of the time, Pallas kernels for 14%

profile of v8, /device:TPU:0, one launch (start us, length us, event | category | flops | bytes accessed | tf_op | source)
XLA Modules:
  0.0 39.2 jit_solution(1193946956440524562)
XLA Ops:
  0.0 0.0 copy-start
  0.0 0.0 copy-start.1
  0.0 0.0 copy-start.2
  0.0 0.5 %collective-permute-start.3 = (bf16[1,1024,512]{2,1,0:T(8,128)(2,1)}, bf16[1,1024,512]{2,1,0:T(8,128)(2,1)S(1)}, u32[]{:S(2)}, u32[]{:S(2)}) collective-permute-start(bf16[1,1024,512]{2,1,0:T(8,128)(2,1)} %refs_4_.1), channel_id=1, source_target_pairs={{0,1},{1,0},{2,3},{3,2},{4,5},{5,4},{6,7},{7,6},{8,9},{9,8},{10,11... | collective-permute-start | bytes 3145736 | tf_op jit(solution)/shard_map/ppermute | solution.py:302
  0.5 0.1 collective-permute-start.4
  0.6 4.4 %mixer.1 = (bf16[16,1152]{1,0:T(8,128)(2,1)S(1)}, bf16[16,1024]{1,0:T(8,128)(2,1)S(1)}) custom-call(bf16[8,2,1024]{2,1,0:T(2,128)(2,1)} %hidden_hbm.1, bf16[8,2,1024]{2,1,0:T(2,128)(2,1)} %query_hbm.1, bf16[8,2,1024]{2,1,0:T(2,128)(2,1)} %key_hbm.1, bf16[8,2,2048]{2,1,0:T(2,128)(2,1)} %value_hbm.1, bf16[8,2,2048]{2,1,0:T(2,128)(2,1)} %gate_hbm.1, ...), custom_call_target="tpu_custom_call" | custom-call | tf_op jit(solution)/shard_map/mixer/pallas_call | solution.py:357
  5.0 5.1 %collective-permute-start.2 = (bf16[16,1152]{1,0:T(8,128)(2,1)S(1)}, bf16[16,1152]{1,0:T(8,128)(2,1)S(1)}, u32[]{:S(2)}, u32[]{:S(2)}) collective-permute-start(bf16[16,1152]{1,0:T(8,128)(2,1)S(1)} %get-tuple-element.15.refs_0_), channel_id=1, source_target_pairs={{0,24},{1,7},{2,26},{3,5},{4,28},{5,3},{6,30},{7,1},{8,16},{9,15},... | collective-permute-start | bytes 110600 | tf_op jit(solution)/shard_map/ppermute | solution.py:302
  10.1 0.0 collective-permute-start.1
  10.1 0.6 %collective-permute-start = (bf16[16,1152]{1,0:T(8,128)(2,1)S(1)}, bf16[16,1152]{1,0:T(8,128)(2,1)S(1)}, u32[]{:S(2)}, u32[]{:S(2)}) collective-permute-start(bf16[16,1152]{1,0:T(8,128)(2,1)S(1)} %get-tuple-element.15.refs_0_), channel_id=1, source_target_pairs={{0,8},{1,3},{2,10},{3,1},{4,12},{5,7},{6,14},{7,5},{8,0},{9,11},{1... | collective-permute-start | bytes 110600 | tf_op jit(solution)/shard_map/ppermute | solution.py:302
  10.8 1.3 %collective-permute-done.2.refs_3_ = bf16[16,1152]{1,0:T(8,128)(2,1)S(1)} collective-permute-done((bf16[16,1152]{1,0:T(8,128)(2,1)S(1)}, bf16[16,1152]{1,0:T(8,128)(2,1)S(1)}, u32[]{:S(2)}, u32[]{:S(2)}) %collective-permute-start.2) | collective-permute-done | bytes 36896 | tf_op jit(solution)/shard_map/ppermute | solution.py:302
  12.1 2.9 %collective-permute-done.1.refs_2_ = bf16[16,1152]{1,0:T(8,128)(2,1)S(1)} collective-permute-done((bf16[16,1152]{1,0:T(8,128)(2,1)S(1)}, bf16[16,1152]{1,0:T(8,128)(2,1)S(1)}, u32[]{:S(2)}, u32[]{:S(2)}) %collective-permute-start.1) | collective-permute-done | bytes 36896 | tf_op jit(solution)/shard_map/ppermute | solution.py:302
  15.0 0.0 collective-permute-done.refs_1_
  15.0 0.1 column.1.refs_0_
  15.1 2.9 %collective-permute-start.7 = (bf16[528,128]{1,0:T(8,128)(2,1)S(1)}, bf16[528,128]{1,0:T(8,128)(2,1)S(1)}, u32[]{:S(2)}, u32[]{:S(2)}) collective-permute-start(bf16[528,128]{1,0:T(8,128)(2,1)S(1)} %column.1.refs_0_), channel_id=1, source_target_pairs={{0,6},{1,25},{2,4},{3,27},{4,2},{5,29},{6,0},{7,31},{8,14},{9,17},... | collective-permute-start | bytes 405512 | tf_op jit(solution)/shard_map/ppermute | solution.py:302
  17.9 0.1 collective-permute-start.6
  18.1 0.5 %collective-permute-start.5 = (bf16[528,128]{1,0:T(8,128)(2,1)S(1)}, bf16[528,128]{1,0:T(8,128)(2,1)S(1)}, u32[]{:S(2)}, u32[]{:S(2)}) collective-permute-start(bf16[528,128]{1,0:T(8,128)(2,1)S(1)} %column.1.refs_0_), channel_id=1, source_target_pairs={{0,4},{1,9},{2,6},{3,11},{4,0},{5,13},{6,2},{7,15},{8,12},{9,1},{1... | collective-permute-start | bytes 405512 | tf_op jit(solution)/shard_map/ppermute | solution.py:302
  18.6 2.4 %collective-permute-done.7.refs_2_ = bf16[528,128]{1,0:T(8,128)(2,1)S(1)} collective-permute-done((bf16[528,128]{1,0:T(8,128)(2,1)S(1)}, bf16[528,128]{1,0:T(8,128)(2,1)S(1)}, u32[]{:S(2)}, u32[]{:S(2)}) %collective-permute-start.7) | collective-permute-done | bytes 135200 | tf_op jit(solution)/shard_map/ppermute | solution.py:302
  21.0 1.9 %collective-permute-done.6.refs_1_ = bf16[528,128]{1,0:T(8,128)(2,1)S(1)} collective-permute-done((bf16[528,128]{1,0:T(8,128)(2,1)S(1)}, bf16[528,128]{1,0:T(8,128)(2,1)S(1)}, u32[]{:S(2)}, u32[]{:S(2)}) %collective-permute-start.6) | collective-permute-done | bytes 135200 | tf_op jit(solution)/shard_map/ppermute | solution.py:302
  23.0 0.1 collective-permute-done.5.refs_0_
  23.1 0.0 collective-permute-done.4.refs_5_.refs_7_
  23.1 0.0 collective-permute-done.3.refs_4_.refs_6_
  23.1 0.0 copy-done
  23.1 0.0 copy-done.1
  23.1 0.0 copy-done.2
  23.1 1.3 %experts.1 = (bf16[64,1024]{1,0:T(8,128)(2,1)S(1)}, bf16[64,1024]{1,0:T(8,128)(2,1)S(1)}, bf16[64,1024]{1,0:T(8,128)(2,1)S(1)}) custom-call(bf16[528,128]{1,0:T(8,128)(2,1)S(1)} %collective-permute-done.5.refs_0_, bf16[528,128]{1,0:T(8,128)(2,1)S(1)} %collective-permute-done.6.refs_1_, bf16[528,128]{1,0:T(8,128)(2,1)S(1)} %collective-permute-done.7.refs_2_, ...), custom_call_target="tpu_custom_call" | custom-call | tf_op jit(solution)/shard_map/experts/pallas_call | solution.py:380
  24.4 2.3 %collective-permute-start.8 = (bf16[64,1024]{1,0:T(8,128)(2,1)S(1)}, bf16[64,1024]{1,0:T(8,128)(2,1)S(1)}, u32[]{:S(2)}, u32[]{:S(2)}) collective-permute-start(bf16[64,1024]{1,0:T(8,128)(2,1)S(1)} %get-tuple-element.16), channel_id=1, source_target_pairs={{0,6},{1,25},{2,4},{3,27},{4,2},{5,29},{6,0},{7,31},{8,14},{9,17},... | collective-permute-start | bytes 393224 | tf_op jit(solution)/shard_map/ppermute | solution.py:302
  26.7 0.1 collective-permute-start.9
  26.8 1.1 %collective-permute-start.10 = (bf16[64,1024]{1,0:T(8,128)(2,1)S(1)}, bf16[64,1024]{1,0:T(8,128)(2,1)S(1)}, u32[]{:S(2)}, u32[]{:S(2)}) collective-permute-start(bf16[64,1024]{1,0:T(8,128)(2,1)S(1)} %get-tuple-element.18), channel_id=1, source_target_pairs={{0,4},{1,9},{2,6},{3,11},{4,0},{5,13},{6,2},{7,15},{8,12},{9,1},{1... | collective-permute-start | bytes 393224 | tf_op jit(solution)/shard_map/ppermute | solution.py:302
  27.9 0.9 %own_experts.1.refs_0_ = f32[64,1024]{1,0:T(8,128)S(1)} custom-call(bf16[528,128]{1,0:T(8,128)(2,1)S(1)} %column.1.refs_0_, bf16[32,1024]{1,0:T(8,128)(2,1)S(1)} %bitcast.2, bf16[1,1024,512]{2,1,0:T(8,128)(2,1)S(1)} %copy-done, bf16[1,256,1024]{2,1,0:T(8,128)(2,1)S(1)} %copy-done.1, bf16[1,1024,512]{2,1,0:T(8,128)(2,1)S(1)} %collective-permute-done.3.refs_4_.refs_6_, ...), custom_call_target="tpu_custom_call" | custom-call | tf_op jit(solution)/shard_map/own_experts/pallas_call | solution.py:380
  28.9 1.5 %collective-permute-done.8.refs_1_ = bf16[64,1024]{1,0:T(8,128)(2,1)S(1)} collective-permute-done((bf16[64,1024]{1,0:T(8,128)(2,1)S(1)}, bf16[64,1024]{1,0:T(8,128)(2,1)S(1)}, u32[]{:S(2)}, u32[]{:S(2)}) %collective-permute-start.8) | collective-permute-done | bytes 131104 | tf_op jit(solution)/shard_map/ppermute | solution.py:302
  30.3 1.3 %collective-permute-done.9.refs_2_ = bf16[64,1024]{1,0:T(8,128)(2,1)S(1)} collective-permute-done((bf16[64,1024]{1,0:T(8,128)(2,1)S(1)}, bf16[64,1024]{1,0:T(8,128)(2,1)S(1)}, u32[]{:S(2)}, u32[]{:S(2)}) %collective-permute-start.9) | collective-permute-done | bytes 131104 | tf_op jit(solution)/shard_map/ppermute | solution.py:302
  31.6 0.1 collective-permute-done.10.refs_3_
  31.8 0.1 column_sum.1
  31.8 1.5 %collective-permute-start.11 = (bf16[16,1024]{1,0:T(8,128)(2,1)S(1)}, bf16[16,1024]{1,0:T(8,128)(2,1)S(1)}, u32[]{:S(2)}, u32[]{:S(2)}) collective-permute-start(bf16[16,1024]{1,0:T(8,128)(2,1)S(1)} %get-tuple-element.20), channel_id=1, source_target_pairs={{0,24},{1,7},{2,26},{3,5},{4,28},{5,3},{6,30},{7,1},{8,16},{9,15},... | collective-permute-start | bytes 98312 | tf_op jit(solution)/shard_map/ppermute | solution.py:302
  33.4 0.6 %collective-permute-start.12 = (bf16[16,1024]{1,0:T(8,128)(2,1)S(1)}, bf16[16,1024]{1,0:T(8,128)(2,1)S(1)}, u32[]{:S(2)}, u32[]{:S(2)}) collective-permute-start(bf16[16,1024]{1,0:T(8,128)(2,1)S(1)} %get-tuple-element.21), channel_id=1, source_target_pairs={{0,16},{1,5},{2,18},{3,7},{4,20},{5,1},{6,22},{7,3},{8,24},{9,13},... | collective-permute-start | bytes 98312 | tf_op jit(solution)/shard_map/ppermute | solution.py:302
  34.0 2.3 %collective-permute-start.13 = (bf16[16,1024]{1,0:T(8,128)(2,1)S(1)}, bf16[16,1024]{1,0:T(8,128)(2,1)S(1)}, u32[]{:S(2)}, u32[]{:S(2)}) collective-permute-start(bf16[16,1024]{1,0:T(8,128)(2,1)S(1)} %get-tuple-element.22), channel_id=1, source_target_pairs={{0,8},{1,3},{2,10},{3,1},{4,12},{5,7},{6,14},{7,5},{8,0},{9,11},{1... | collective-permute-start | bytes 98312 | tf_op jit(solution)/shard_map/ppermute | solution.py:302
  36.3 1.3 %collective-permute-done.11.refs_2_ = bf16[16,1024]{1,0:T(8,128)(2,1)S(1)} collective-permute-done((bf16[16,1024]{1,0:T(8,128)(2,1)S(1)}, bf16[16,1024]{1,0:T(8,128)(2,1)S(1)}, u32[]{:S(2)}, u32[]{:S(2)}) %collective-permute-start.11) | collective-permute-done | bytes 32800 | tf_op jit(solution)/shard_map/ppermute | solution.py:302
  37.6 0.7 %collective-permute-done.12.refs_3_ = bf16[16,1024]{1,0:T(8,128)(2,1)S(1)} collective-permute-done((bf16[16,1024]{1,0:T(8,128)(2,1)S(1)}, bf16[16,1024]{1,0:T(8,128)(2,1)S(1)}, u32[]{:S(2)}, u32[]{:S(2)}) %collective-permute-start.12) | collective-permute-done | bytes 32800 | tf_op jit(solution)/shard_map/ppermute | solution.py:302
  38.3 0.2 collective-permute-done.13.refs_4_
  38.5 0.7 %final.1 = bf16[8,2,1024]{2,1,0:T(2,128)(2,1)} custom-call(bf16[16,1024]{1,0:T(8,128)(2,1)S(1)} %get-tuple-element.14.refs_0_, f32[16,1024]{1,0:T(8,128)S(1)} %get-tuple-element.19.refs_1_, bf16[16,1024]{1,0:T(8,128)(2,1)S(1)} %collective-permute-done.11.refs_2_, bf16[16,1024]{1,0:T(8,128)(2,1)S(1)} %collective-permute-done.12.refs_3_, ...), custom_call_target="tpu_custom_call" | custom-call | tf_op jit(solution)/shard_map/final/pallas_call | solution.py:380
Async XLA Ops:
  0.0 23.1 %copy-start = (bf16[1,1024,512]{2,1,0:T(8,128)(2,1)S(1)}, bf16[1,1024,512]{2,1,0:T(8,128)(2,1)}, u32[]{:S(2)}) copy-start(bf16[1,1024,512]{2,1,0:T(8,128)(2,1)} %refs_4_.1) | copy-start | bytes 3145732
  0.0 23.1 %copy-start.1 = (bf16[1,256,1024]{2,1,0:T(8,128)(2,1)S(1)}, bf16[1,256,1024]{2,1,0:T(8,128)(2,1)}, u32[]{:S(2)}) copy-start(bf16[1,256,1024]{2,1,0:T(8,128)(2,1)} %refs_5_.1) | copy-start | bytes 1572868
  0.0 23.1 %copy-start.2 = (bf16[1024,32]{0,1:T(8,128)(2,1)S(1)}, bf16[1024,32]{0,1:T(8,128)(2,1)}, u32[]{:S(2)}) copy-start(bf16[1024,32]{0,1:T(8,128)(2,1)} %param.30) | copy-start | bytes 196612
  0.0 23.1 %collective-permute-start.3 = (bf16[1,1024,512]{2,1,0:T(8,128)(2,1)}, bf16[1,1024,512]{2,1,0:T(8,128)(2,1)S(1)}, u32[]{:S(2)}, u32[]{:S(2)}) collective-permute-start(bf16[1,1024,512]{2,1,0:T(8,128)(2,1)} %refs_4_.1), channel_id=1, source_target_pairs={{0,1},{1,0},{2,3},{3,2},{4,5},{5,4},{6,7},{7,6},{8,9},{9,8},{10,11... | collective-permute-start | bytes 3145736 | tf_op jit(solution)/shard_map/ppermute | solution.py:302
  0.5 22.6 %collective-permute-start.4 = (bf16[1,256,1024]{2,1,0:T(8,128)(2,1)}, bf16[1,256,1024]{2,1,0:T(8,128)(2,1)S(1)}, u32[]{:S(2)}, u32[]{:S(2)}) collective-permute-start(bf16[1,256,1024]{2,1,0:T(8,128)(2,1)} %refs_5_.1), channel_id=1, source_target_pairs={{0,1},{1,0},{2,3},{3,2},{4,5},{5,4},{6,7},{7,6},{8,9},{9,8},{10,11... | collective-permute-start | bytes 1572872 | tf_op jit(solution)/shard_map/ppermute | solution.py:302
  5.0 7.0 %collective-permute-start.2 = (bf16[16,1152]{1,0:T(8,128)(2,1)S(1)}, bf16[16,1152]{1,0:T(8,128)(2,1)S(1)}, u32[]{:S(2)}, u32[]{:S(2)}) collective-permute-start(bf16[16,1152]{1,0:T(8,128)(2,1)S(1)} %get-tuple-element.15.refs_0_), channel_id=1, source_target_pairs={{0,24},{1,7},{2,26},{3,5},{4,28},{5,3},{6,30},{7,1},{8,16},{9,15},... | collective-permute-start | bytes 110600 | tf_op jit(solution)/shard_map/ppermute | solution.py:302
  10.1 4.9 %collective-permute-start.1 = (bf16[16,1152]{1,0:T(8,128)(2,1)S(1)}, bf16[16,1152]{1,0:T(8,128)(2,1)S(1)}, u32[]{:S(2)}, u32[]{:S(2)}) collective-permute-start(bf16[16,1152]{1,0:T(8,128)(2,1)S(1)} %get-tuple-element.15.refs_0_), channel_id=1, source_target_pairs={{0,16},{1,5},{2,18},{3,7},{4,20},{5,1},{6,22},{7,3},{8,24},{9,13},... | collective-permute-start | bytes 110600 | tf_op jit(solution)/shard_map/ppermute | solution.py:302
  10.1 4.9 %collective-permute-start = (bf16[16,1152]{1,0:T(8,128)(2,1)S(1)}, bf16[16,1152]{1,0:T(8,128)(2,1)S(1)}, u32[]{:S(2)}, u32[]{:S(2)}) collective-permute-start(bf16[16,1152]{1,0:T(8,128)(2,1)S(1)} %get-tuple-element.15.refs_0_), channel_id=1, source_target_pairs={{0,8},{1,3},{2,10},{3,1},{4,12},{5,7},{6,14},{7,5},{8,0},{9,11},{1... | collective-permute-start | bytes 110600 | tf_op jit(solution)/shard_map/ppermute | solution.py:302
  15.1 5.9 %collective-permute-start.7 = (bf16[528,128]{1,0:T(8,128)(2,1)S(1)}, bf16[528,128]{1,0:T(8,128)(2,1)S(1)}, u32[]{:S(2)}, u32[]{:S(2)}) collective-permute-start(bf16[528,128]{1,0:T(8,128)(2,1)S(1)} %column.1.refs_0_), channel_id=1, source_target_pairs={{0,6},{1,25},{2,4},{3,27},{4,2},{5,29},{6,0},{7,31},{8,14},{9,17},... | collective-permute-start | bytes 405512 | tf_op jit(solution)/shard_map/ppermute | solution.py:302
  17.9 5.0 %collective-permute-start.6 = (bf16[528,128]{1,0:T(8,128)(2,1)S(1)}, bf16[528,128]{1,0:T(8,128)(2,1)S(1)}, u32[]{:S(2)}, u32[]{:S(2)}) collective-permute-start(bf16[528,128]{1,0:T(8,128)(2,1)S(1)} %column.1.refs_0_), channel_id=1, source_target_pairs={{0,2},{1,17},{2,0},{3,19},{4,6},{5,21},{6,4},{7,23},{8,10},{9,25},... | collective-permute-start | bytes 405512 | tf_op jit(solution)/shard_map/ppermute | solution.py:302
  18.1 5.0 %collective-permute-start.5 = (bf16[528,128]{1,0:T(8,128)(2,1)S(1)}, bf16[528,128]{1,0:T(8,128)(2,1)S(1)}, u32[]{:S(2)}, u32[]{:S(2)}) collective-permute-start(bf16[528,128]{1,0:T(8,128)(2,1)S(1)} %column.1.refs_0_), channel_id=1, source_target_pairs={{0,4},{1,9},{2,6},{3,11},{4,0},{5,13},{6,2},{7,15},{8,12},{9,1},{1... | collective-permute-start | bytes 405512 | tf_op jit(solution)/shard_map/ppermute | solution.py:302
  24.4 5.9 %collective-permute-start.8 = (bf16[64,1024]{1,0:T(8,128)(2,1)S(1)}, bf16[64,1024]{1,0:T(8,128)(2,1)S(1)}, u32[]{:S(2)}, u32[]{:S(2)}) collective-permute-start(bf16[64,1024]{1,0:T(8,128)(2,1)S(1)} %get-tuple-element.16), channel_id=1, source_target_pairs={{0,6},{1,25},{2,4},{3,27},{4,2},{5,29},{6,0},{7,31},{8,14},{9,17},... | collective-permute-start | bytes 393224 | tf_op jit(solution)/shard_map/ppermute | solution.py:302
  26.7 5.0 %collective-permute-start.9 = (bf16[64,1024]{1,0:T(8,128)(2,1)S(1)}, bf16[64,1024]{1,0:T(8,128)(2,1)S(1)}, u32[]{:S(2)}, u32[]{:S(2)}) collective-permute-start(bf16[64,1024]{1,0:T(8,128)(2,1)S(1)} %get-tuple-element.17), channel_id=1, source_target_pairs={{0,2},{1,17},{2,0},{3,19},{4,6},{5,21},{6,4},{7,23},{8,10},{9,25},... | collective-permute-start | bytes 393224 | tf_op jit(solution)/shard_map/ppermute | solution.py:302
  26.8 5.0 %collective-permute-start.10 = (bf16[64,1024]{1,0:T(8,128)(2,1)S(1)}, bf16[64,1024]{1,0:T(8,128)(2,1)S(1)}, u32[]{:S(2)}, u32[]{:S(2)}) collective-permute-start(bf16[64,1024]{1,0:T(8,128)(2,1)S(1)} %get-tuple-element.18), channel_id=1, source_target_pairs={{0,4},{1,9},{2,6},{3,11},{4,0},{5,13},{6,2},{7,15},{8,12},{9,1},{1... | collective-permute-start | bytes 393224 | tf_op jit(solution)/shard_map/ppermute | solution.py:302
  31.8 5.8 %collective-permute-start.11 = (bf16[16,1024]{1,0:T(8,128)(2,1)S(1)}, bf16[16,1024]{1,0:T(8,128)(2,1)S(1)}, u32[]{:S(2)}, u32[]{:S(2)}) collective-permute-start(bf16[16,1024]{1,0:T(8,128)(2,1)S(1)} %get-tuple-element.20), channel_id=1, source_target_pairs={{0,24},{1,7},{2,26},{3,5},{4,28},{5,3},{6,30},{7,1},{8,16},{9,15},... | collective-permute-start | bytes 98312 | tf_op jit(solution)/shard_map/ppermute | solution.py:302
  33.4 4.9 %collective-permute-start.12 = (bf16[16,1024]{1,0:T(8,128)(2,1)S(1)}, bf16[16,1024]{1,0:T(8,128)(2,1)S(1)}, u32[]{:S(2)}, u32[]{:S(2)}) collective-permute-start(bf16[16,1024]{1,0:T(8,128)(2,1)S(1)} %get-tuple-element.21), channel_id=1, source_target_pairs={{0,16},{1,5},{2,18},{3,7},{4,20},{5,1},{6,22},{7,3},{8,24},{9,13},... | collective-permute-start | bytes 98312 | tf_op jit(solution)/shard_map/ppermute | solution.py:302
  34.0 4.5 %collective-permute-start.13 = (bf16[16,1024]{1,0:T(8,128)(2,1)S(1)}, bf16[16,1024]{1,0:T(8,128)(2,1)S(1)}, u32[]{:S(2)}, u32[]{:S(2)}) collective-permute-start(bf16[16,1024]{1,0:T(8,128)(2,1)S(1)} %get-tuple-element.22), channel_id=1, source_target_pairs={{0,8},{1,3},{2,10},{3,1},{4,12},{5,7},{6,14},{7,5},{8,0},{9,11},{1... | collective-permute-start | bytes 98312 | tf_op jit(solution)/shard_map/ppermute | solution.py:302

commit v9 on v8

--- a/solution.py
+++ b/solution.py
@@ -59,7 +59,7 @@
     share = value_heads // key_heads
     span = share * value_size
     chunks = proj_sem.shape[0]
-    depth = proj_hbm.shape[0] // chunks
+    cut = proj_hbm.shape[0] // 2
 
     groups = state_sem.shape[0]
     group = key_heads // groups
@@ -71,7 +71,7 @@
         )
 
     def proj_copy(c):
-        part = pl.ds(c * depth, depth)
+        part = pl.ds(c * cut, cut)
         return pltpu.make_async_copy(proj_hbm.at[part], proj_buf.at[part], proj_sem.at[c])
 
     pairs = (
@@ -97,10 +97,10 @@
         copy.start()
     for c in range(1, groups):
         state_copy(c).start()
+    for copy in late:
+        copy.start()
     for c in range(chunks):
         proj_copy(c).start()
-    for copy in late:
-        copy.start()
     for copy in early:
         copy.wait()
 
@@ -118,8 +118,23 @@
         betas.append(1.0 / (1.0 + jnp.exp(-beta_in[:, p, :])))
     gain = norm_gain_ref[...].reshape(1, value_size)
 
+    def joined(lists):
+        return jnp.concatenate([jnp.concatenate(m, axis=-1) for m in lists], axis=0).astype(bf16)
+
+    half = value_heads // 2
     mixed = [[], []]
+    total = None
     for h in range(key_heads):
+        if h == key_heads // 2:
+            for copy in late:
+                copy.wait()
+            tokens, extra = 2 * rows, routed_ref.shape[1] - proj_hbm.shape[1]
+            ids = jnp.concatenate([ids_ref[:, p, :] for p in range(2)], axis=0)
+            lane = lax.broadcasted_iota(jnp.int32, (tokens, extra), 1)
+            chosen = jnp.zeros((tokens, extra), f32)
+            for k in range(ids.shape[1]):
+                chosen = chosen + (ids[:, k : k + 1] == lane).astype(f32)
+            routed_ref[:, -extra:] = chosen.astype(bf16)
         lanes = slice(h * key_size, (h + 1) * key_size)
         keys, queries = [], []
         for p in range(2):
@@ -143,6 +158,11 @@
 
         if h % group == 0:
             state_copy(h // group).wait()
+            if h == key_heads - group:
+                proj_copy(0).wait()
+                total = jnp.dot(
+                    joined([m[:half] for m in mixed]), proj_buf[:cut, :], preferred_element_type=f32
+                )
         for r in range(rows):
             left = left_buf[h, r * 8 : (r + 1) * 8, :].astype(bf16)
             right = jnp.concatenate([state_buf[r, h * share + i] for i in range(share)], axis=-1)
@@ -171,24 +191,12 @@
                     o * lax.rsqrt(mean + eps_norm) * gain * (g / (1.0 + jnp.exp(-g)))
                 )
 
-    mixer_out = jnp.concatenate(
-        [jnp.concatenate(mixed[p], axis=-1) for p in range(2)], axis=0
-    ).astype(bf16)
-    for copy in late:
-        copy.wait()
-    tokens, extra = 2 * rows, routed_ref.shape[1] - proj_hbm.shape[1]
-    ids = jnp.concatenate([ids_ref[:, p, :] for p in range(2)], axis=0)
-    lane = lax.broadcasted_iota(jnp.int32, (tokens, extra), 1)
-    chosen = jnp.zeros((tokens, extra), f32)
-    for k in range(ids.shape[1]):
-        chosen = chosen + (ids[:, k : k + 1] == lane).astype(f32)
-    routed_ref[:, -extra:] = chosen.astype(bf16)
     hidden = hidden_ref[...].astype(f32)
-    total = jnp.concatenate([hidden[:, p, :] for p in range(2)], axis=0)
-    for c in range(chunks):
-        proj_copy(c).wait()
-        part = slice(c * depth, (c + 1) * depth)
-        total = total + jnp.dot(mixer_out[:, part], proj_buf[part, :], preferred_element_type=f32)
+    total = total + jnp.concatenate([hidden[:, p, :] for p in range(2)], axis=0)
+    proj_copy(1).wait()
+    total = total + jnp.dot(
+        joined([m[half:] for m in mixed]), proj_buf[cut:, :], preferred_element_type=f32
+    )
     middle = total.astype(bf16)
     middle_ref[...] = middle
     wide = middle.astype(f32)

time: 39.3 us -> 39.4 us (level)
  no operation moved by 1% of the time
where the time goes in v9:
time: 39.4 us; the launch traced here: 39.2 us
  starting transfers between devices  17.8 us (45%)
  waiting for transfers between devices  13.9 us (35%)
  Pallas kernels  7.43 us (19%)
    ppermute x14, starting transfers between devices, hop(): return lax.ppermute(x, 'dp', [(i, i ^ masks[i % 2]) for i in range(count)])  17.8 us
    ppermute x14, waiting for transfers between devices, hop(): return lax.ppermute(x, 'dp', [(i, i ^ masks[i % 2]) for i in range(count)])  13.9 us
    pallas_call x1, Pallas kernels, shards(): pl.pallas_call(mixer_kernel, out_shape=(jax.ShapeDtypeStruct((token_count...  4.46 us
    pallas_call x5, Pallas kernels, local(): pl.pallas_call(body, out_shape=tuple((jax.ShapeDtypeStruct(*o) for o in o...  2.97 us
  transfers between devices with their start and end apart: 14, of which 11 were waited for; matrix products, arithmetic and copies ran while one was open for 0% of the time, Pallas kernels for 14%

profile of v9, /device:TPU:0, one launch (start us, length us, event | category | flops | bytes accessed | tf_op | source)
XLA Modules:
  0.0 39.2 jit_solution(13798140051807712432)
XLA Ops:
  0.0 0.0 copy-start
  0.0 0.0 copy-start.1
  0.0 0.0 copy-start.2
  0.0 0.5 %collective-permute-start.3 = (bf16[1,1024,512]{2,1,0:T(8,128)(2,1)}, bf16[1,1024,512]{2,1,0:T(8,128)(2,1)S(1)}, u32[]{:S(2)}, u32[]{:S(2)}) collective-permute-start(bf16[1,1024,512]{2,1,0:T(8,128)(2,1)} %refs_4_.1), channel_id=1, source_target_pairs={{0,1},{1,0},{2,3},{3,2},{4,5},{5,4},{6,7},{7,6},{8,9},{9,8},{10,11... | collective-permute-start | bytes 3145736 | tf_op jit(solution)/shard_map/ppermute | solution.py:310
  0.5 0.1 collective-permute-start.4
  0.6 4.5 %mixer.1 = (bf16[16,1152]{1,0:T(8,128)(2,1)S(1)}, bf16[16,1024]{1,0:T(8,128)(2,1)S(1)}) custom-call(bf16[8,2,1024]{2,1,0:T(2,128)(2,1)} %hidden_hbm.1, bf16[8,2,1024]{2,1,0:T(2,128)(2,1)} %query_hbm.1, bf16[8,2,1024]{2,1,0:T(2,128)(2,1)} %key_hbm.1, bf16[8,2,2048]{2,1,0:T(2,128)(2,1)} %value_hbm.1, bf16[8,2,2048]{2,1,0:T(2,128)(2,1)} %gate_hbm.1, ...), custom_call_target="tpu_custom_call" | custom-call | tf_op jit(solution)/shard_map/mixer/pallas_call | solution.py:365
  5.1 5.1 %collective-permute-start.2 = (bf16[16,1152]{1,0:T(8,128)(2,1)S(1)}, bf16[16,1152]{1,0:T(8,128)(2,1)S(1)}, u32[]{:S(2)}, u32[]{:S(2)}) collective-permute-start(bf16[16,1152]{1,0:T(8,128)(2,1)S(1)} %get-tuple-element.15.refs_0_), channel_id=1, source_target_pairs={{0,24},{1,7},{2,26},{3,5},{4,28},{5,3},{6,30},{7,1},{8,16},{9,15},... | collective-permute-start | bytes 110600 | tf_op jit(solution)/shard_map/ppermute | solution.py:310
  10.2 0.0 collective-permute-start.1
  10.2 0.6 %collective-permute-start = (bf16[16,1152]{1,0:T(8,128)(2,1)S(1)}, bf16[16,1152]{1,0:T(8,128)(2,1)S(1)}, u32[]{:S(2)}, u32[]{:S(2)}) collective-permute-start(bf16[16,1152]{1,0:T(8,128)(2,1)S(1)} %get-tuple-element.15.refs_0_), channel_id=1, source_target_pairs={{0,8},{1,3},{2,10},{3,1},{4,12},{5,7},{6,14},{7,5},{8,0},{9,11},{1... | collective-permute-start | bytes 110600 | tf_op jit(solution)/shard_map/ppermute | solution.py:310
  10.8 1.3 %collective-permute-done.2.refs_3_ = bf16[16,1152]{1,0:T(8,128)(2,1)S(1)} collective-permute-done((bf16[16,1152]{1,0:T(8,128)(2,1)S(1)}, bf16[16,1152]{1,0:T(8,128)(2,1)S(1)}, u32[]{:S(2)}, u32[]{:S(2)}) %collective-permute-start.2) | collective-permute-done | bytes 36896 | tf_op jit(solution)/shard_map/ppermute | solution.py:310
  12.1 2.9 %collective-permute-done.1.refs_2_ = bf16[16,1152]{1,0:T(8,128)(2,1)S(1)} collective-permute-done((bf16[16,1152]{1,0:T(8,128)(2,1)S(1)}, bf16[16,1152]{1,0:T(8,128)(2,1)S(1)}, u32[]{:S(2)}, u32[]{:S(2)}) %collective-permute-start.1) | collective-permute-done | bytes 36896 | tf_op jit(solution)/shard_map/ppermute | solution.py:310
  15.0 0.0 collective-permute-done.refs_1_
  15.0 0.1 column.1.refs_0_
  15.1 2.9 %collective-permute-start.7 = (bf16[528,128]{1,0:T(8,128)(2,1)S(1)}, bf16[528,128]{1,0:T(8,128)(2,1)S(1)}, u32[]{:S(2)}, u32[]{:S(2)}) collective-permute-start(bf16[528,128]{1,0:T(8,128)(2,1)S(1)} %column.1.refs_0_), channel_id=1, source_target_pairs={{0,6},{1,25},{2,4},{3,27},{4,2},{5,29},{6,0},{7,31},{8,14},{9,17},... | collective-permute-start | bytes 405512 | tf_op jit(solution)/shard_map/ppermute | solution.py:310
  18.0 0.1 collective-permute-start.6
  18.1 0.5 %collective-permute-start.5 = (bf16[528,128]{1,0:T(8,128)(2,1)S(1)}, bf16[528,128]{1,0:T(8,128)(2,1)S(1)}, u32[]{:S(2)}, u32[]{:S(2)}) collective-permute-start(bf16[528,128]{1,0:T(8,128)(2,1)S(1)} %column.1.refs_0_), channel_id=1, source_target_pairs={{0,4},{1,9},{2,6},{3,11},{4,0},{5,13},{6,2},{7,15},{8,12},{9,1},{1... | collective-permute-start | bytes 405512 | tf_op jit(solution)/shard_map/ppermute | solution.py:310
  18.6 2.4 %collective-permute-done.7.refs_2_ = bf16[528,128]{1,0:T(8,128)(2,1)S(1)} collective-permute-done((bf16[528,128]{1,0:T(8,128)(2,1)S(1)}, bf16[528,128]{1,0:T(8,128)(2,1)S(1)}, u32[]{:S(2)}, u32[]{:S(2)}) %collective-permute-start.7) | collective-permute-done | bytes 135200 | tf_op jit(solution)/shard_map/ppermute | solution.py:310
  21.0 1.9 %collective-permute-done.6.refs_1_ = bf16[528,128]{1,0:T(8,128)(2,1)S(1)} collective-permute-done((bf16[528,128]{1,0:T(8,128)(2,1)S(1)}, bf16[528,128]{1,0:T(8,128)(2,1)S(1)}, u32[]{:S(2)}, u32[]{:S(2)}) %collective-permute-start.6) | collective-permute-done | bytes 135200 | tf_op jit(solution)/shard_map/ppermute | solution.py:310
  23.0 0.1 collective-permute-done.5.refs_0_
  23.1 0.0 collective-permute-done.4.refs_5_.refs_7_
  23.1 0.0 collective-permute-done.3.refs_4_.refs_6_
  23.1 0.0 copy-done
  23.1 0.0 copy-done.1
  23.1 0.0 copy-done.2
  23.2 1.3 %experts.1 = (bf16[64,1024]{1,0:T(8,128)(2,1)S(1)}, bf16[64,1024]{1,0:T(8,128)(2,1)S(1)}, bf16[64,1024]{1,0:T(8,128)(2,1)S(1)}) custom-call(bf16[528,128]{1,0:T(8,128)(2,1)S(1)} %collective-permute-done.5.refs_0_, bf16[528,128]{1,0:T(8,128)(2,1)S(1)} %collective-permute-done.6.refs_1_, bf16[528,128]{1,0:T(8,128)(2,1)S(1)} %collective-permute-done.7.refs_2_, ...), custom_call_target="tpu_custom_call" | custom-call | tf_op jit(solution)/shard_map/experts/pallas_call | solution.py:388
  24.4 2.3 %collective-permute-start.8 = (bf16[64,1024]{1,0:T(8,128)(2,1)S(1)}, bf16[64,1024]{1,0:T(8,128)(2,1)S(1)}, u32[]{:S(2)}, u32[]{:S(2)}) collective-permute-start(bf16[64,1024]{1,0:T(8,128)(2,1)S(1)} %get-tuple-element.16), channel_id=1, source_target_pairs={{0,6},{1,25},{2,4},{3,27},{4,2},{5,29},{6,0},{7,31},{8,14},{9,17},... | collective-permute-start | bytes 393224 | tf_op jit(solution)/shard_map/ppermute | solution.py:310
  26.7 0.1 collective-permute-start.9
  26.8 1.1 %collective-permute-start.10 = (bf16[64,1024]{1,0:T(8,128)(2,1)S(1)}, bf16[64,1024]{1,0:T(8,128)(2,1)S(1)}, u32[]{:S(2)}, u32[]{:S(2)}) collective-permute-start(bf16[64,1024]{1,0:T(8,128)(2,1)S(1)} %get-tuple-element.18), channel_id=1, source_target_pairs={{0,4},{1,9},{2,6},{3,11},{4,0},{5,13},{6,2},{7,15},{8,12},{9,1},{1... | collective-permute-start | bytes 393224 | tf_op jit(solution)/shard_map/ppermute | solution.py:310
  28.0 0.9 %own_experts.1.refs_0_ = f32[64,1024]{1,0:T(8,128)S(1)} custom-call(bf16[528,128]{1,0:T(8,128)(2,1)S(1)} %column.1.refs_0_, bf16[32,1024]{1,0:T(8,128)(2,1)S(1)} %bitcast.2, bf16[1,1024,512]{2,1,0:T(8,128)(2,1)S(1)} %copy-done, bf16[1,256,1024]{2,1,0:T(8,128)(2,1)S(1)} %copy-done.1, bf16[1,1024,512]{2,1,0:T(8,128)(2,1)S(1)} %collective-permute-done.3.refs_4_.refs_6_, ...), custom_call_target="tpu_custom_call" | custom-call | tf_op jit(solution)/shard_map/own_experts/pallas_call | solution.py:388
  28.9 1.5 %collective-permute-done.8.refs_1_ = bf16[64,1024]{1,0:T(8,128)(2,1)S(1)} collective-permute-done((bf16[64,1024]{1,0:T(8,128)(2,1)S(1)}, bf16[64,1024]{1,0:T(8,128)(2,1)S(1)}, u32[]{:S(2)}, u32[]{:S(2)}) %collective-permute-start.8) | collective-permute-done | bytes 131104 | tf_op jit(solution)/shard_map/ppermute | solution.py:310
  30.4 1.3 %collective-permute-done.9.refs_2_ = bf16[64,1024]{1,0:T(8,128)(2,1)S(1)} collective-permute-done((bf16[64,1024]{1,0:T(8,128)(2,1)S(1)}, bf16[64,1024]{1,0:T(8,128)(2,1)S(1)}, u32[]{:S(2)}, u32[]{:S(2)}) %collective-permute-start.9) | collective-permute-done | bytes 131104 | tf_op jit(solution)/shard_map/ppermute | solution.py:310
  31.7 0.1 collective-permute-done.10.refs_3_
  31.8 0.1 column_sum.1
  31.9 1.5 %collective-permute-start.11 = (bf16[16,1024]{1,0:T(8,128)(2,1)S(1)}, bf16[16,1024]{1,0:T(8,128)(2,1)S(1)}, u32[]{:S(2)}, u32[]{:S(2)}) collective-permute-start(bf16[16,1024]{1,0:T(8,128)(2,1)S(1)} %get-tuple-element.20), channel_id=1, source_target_pairs={{0,24},{1,7},{2,26},{3,5},{4,28},{5,3},{6,30},{7,1},{8,16},{9,15},... | collective-permute-start | bytes 98312 | tf_op jit(solution)/shard_map/ppermute | solution.py:310
  33.4 0.6 %collective-permute-start.12 = (bf16[16,1024]{1,0:T(8,128)(2,1)S(1)}, bf16[16,1024]{1,0:T(8,128)(2,1)S(1)}, u32[]{:S(2)}, u32[]{:S(2)}) collective-permute-start(bf16[16,1024]{1,0:T(8,128)(2,1)S(1)} %get-tuple-element.21), channel_id=1, source_target_pairs={{0,16},{1,5},{2,18},{3,7},{4,20},{5,1},{6,22},{7,3},{8,24},{9,13},... | collective-permute-start | bytes 98312 | tf_op jit(solution)/shard_map/ppermute | solution.py:310
  34.0 2.3 %collective-permute-start.13 = (bf16[16,1024]{1,0:T(8,128)(2,1)S(1)}, bf16[16,1024]{1,0:T(8,128)(2,1)S(1)}, u32[]{:S(2)}, u32[]{:S(2)}) collective-permute-start(bf16[16,1024]{1,0:T(8,128)(2,1)S(1)} %get-tuple-element.22), channel_id=1, source_target_pairs={{0,8},{1,3},{2,10},{3,1},{4,12},{5,7},{6,14},{7,5},{8,0},{9,11},{1... | collective-permute-start | bytes 98312 | tf_op jit(solution)/shard_map/ppermute | solution.py:310
  36.3 1.3 %collective-permute-done.11.refs_2_ = bf16[16,1024]{1,0:T(8,128)(2,1)S(1)} collective-permute-done((bf16[16,1024]{1,0:T(8,128)(2,1)S(1)}, bf16[16,1024]{1,0:T(8,128)(2,1)S(1)}, u32[]{:S(2)}, u32[]{:S(2)}) %collective-permute-start.11) | collective-permute-done | bytes 32800 | tf_op jit(solution)/shard_map/ppermute | solution.py:310
  37.7 0.6 %collective-permute-done.12.refs_3_ = bf16[16,1024]{1,0:T(8,128)(2,1)S(1)} collective-permute-done((bf16[16,1024]{1,0:T(8,128)(2,1)S(1)}, bf16[16,1024]{1,0:T(8,128)(2,1)S(1)}, u32[]{:S(2)}, u32[]{:S(2)}) %collective-permute-start.12) | collective-permute-done | bytes 32800 | tf_op jit(solution)/shard_map/ppermute | solution.py:310
  38.3 0.3 collective-permute-done.13.refs_4_
  38.6 0.7 %final.1 = bf16[8,2,1024]{2,1,0:T(2,128)(2,1)} custom-call(bf16[16,1024]{1,0:T(8,128)(2,1)S(1)} %get-tuple-element.14.refs_0_, f32[16,1024]{1,0:T(8,128)S(1)} %get-tuple-element.19.refs_1_, bf16[16,1024]{1,0:T(8,128)(2,1)S(1)} %collective-permute-done.11.refs_2_, bf16[16,1024]{1,0:T(8,128)(2,1)S(1)} %collective-permute-done.12.refs_3_, ...), custom_call_target="tpu_custom_call" | custom-call | tf_op jit(solution)/shard_map/final/pallas_call | solution.py:388
Async XLA Ops:
  0.0 23.1 %copy-start = (bf16[1,1024,512]{2,1,0:T(8,128)(2,1)S(1)}, bf16[1,1024,512]{2,1,0:T(8,128)(2,1)}, u32[]{:S(2)}) copy-start(bf16[1,1024,512]{2,1,0:T(8,128)(2,1)} %refs_4_.1) | copy-start | bytes 3145732
  0.0 23.1 %copy-start.1 = (bf16[1,256,1024]{2,1,0:T(8,128)(2,1)S(1)}, bf16[1,256,1024]{2,1,0:T(8,128)(2,1)}, u32[]{:S(2)}) copy-start(bf16[1,256,1024]{2,1,0:T(8,128)(2,1)} %refs_5_.1) | copy-start | bytes 1572868
  0.0 23.1 %copy-start.2 = (bf16[1024,32]{0,1:T(8,128)(2,1)S(1)}, bf16[1024,32]{0,1:T(8,128)(2,1)}, u32[]{:S(2)}) copy-start(bf16[1024,32]{0,1:T(8,128)(2,1)} %param.30) | copy-start | bytes 196612
  0.0 23.1 %collective-permute-start.3 = (bf16[1,1024,512]{2,1,0:T(8,128)(2,1)}, bf16[1,1024,512]{2,1,0:T(8,128)(2,1)S(1)}, u32[]{:S(2)}, u32[]{:S(2)}) collective-permute-start(bf16[1,1024,512]{2,1,0:T(8,128)(2,1)} %refs_4_.1), channel_id=1, source_target_pairs={{0,1},{1,0},{2,3},{3,2},{4,5},{5,4},{6,7},{7,6},{8,9},{9,8},{10,11... | collective-permute-start | bytes 3145736 | tf_op jit(solution)/shard_map/ppermute | solution.py:310
  0.5 22.6 %collective-permute-start.4 = (bf16[1,256,1024]{2,1,0:T(8,128)(2,1)}, bf16[1,256,1024]{2,1,0:T(8,128)(2,1)S(1)}, u32[]{:S(2)}, u32[]{:S(2)}) collective-permute-start(bf16[1,256,1024]{2,1,0:T(8,128)(2,1)} %refs_5_.1), channel_id=1, source_target_pairs={{0,1},{1,0},{2,3},{3,2},{4,5},{5,4},{6,7},{7,6},{8,9},{9,8},{10,11... | collective-permute-start | bytes 1572872 | tf_op jit(solution)/shard_map/ppermute | solution.py:310
  5.1 7.0 %collective-permute-start.2 = (bf16[16,1152]{1,0:T(8,128)(2,1)S(1)}, bf16[16,1152]{1,0:T(8,128)(2,1)S(1)}, u32[]{:S(2)}, u32[]{:S(2)}) collective-permute-start(bf16[16,1152]{1,0:T(8,128)(2,1)S(1)} %get-tuple-element.15.refs_0_), channel_id=1, source_target_pairs={{0,24},{1,7},{2,26},{3,5},{4,28},{5,3},{6,30},{7,1},{8,16},{9,15},... | collective-permute-start | bytes 110600 | tf_op jit(solution)/shard_map/ppermute | solution.py:310
  10.2 4.9 %collective-permute-start.1 = (bf16[16,1152]{1,0:T(8,128)(2,1)S(1)}, bf16[16,1152]{1,0:T(8,128)(2,1)S(1)}, u32[]{:S(2)}, u32[]{:S(2)}) collective-permute-start(bf16[16,1152]{1,0:T(8,128)(2,1)S(1)} %get-tuple-element.15.refs_0_), channel_id=1, source_target_pairs={{0,16},{1,5},{2,18},{3,7},{4,20},{5,1},{6,22},{7,3},{8,24},{9,13},... | collective-permute-start | bytes 110600 | tf_op jit(solution)/shard_map/ppermute | solution.py:310
  10.2 4.9 %collective-permute-start = (bf16[16,1152]{1,0:T(8,128)(2,1)S(1)}, bf16[16,1152]{1,0:T(8,128)(2,1)S(1)}, u32[]{:S(2)}, u32[]{:S(2)}) collective-permute-start(bf16[16,1152]{1,0:T(8,128)(2,1)S(1)} %get-tuple-element.15.refs_0_), channel_id=1, source_target_pairs={{0,8},{1,3},{2,10},{3,1},{4,12},{5,7},{6,14},{7,5},{8,0},{9,11},{1... | collective-permute-start | bytes 110600 | tf_op jit(solution)/shard_map/ppermute | solution.py:310
  15.1 5.9 %collective-permute-start.7 = (bf16[528,128]{1,0:T(8,128)(2,1)S(1)}, bf16[528,128]{1,0:T(8,128)(2,1)S(1)}, u32[]{:S(2)}, u32[]{:S(2)}) collective-permute-start(bf16[528,128]{1,0:T(8,128)(2,1)S(1)} %column.1.refs_0_), channel_id=1, source_target_pairs={{0,6},{1,25},{2,4},{3,27},{4,2},{5,29},{6,0},{7,31},{8,14},{9,17},... | collective-permute-start | bytes 405512 | tf_op jit(solution)/shard_map/ppermute | solution.py:310
  18.0 5.0 %collective-permute-start.6 = (bf16[528,128]{1,0:T(8,128)(2,1)S(1)}, bf16[528,128]{1,0:T(8,128)(2,1)S(1)}, u32[]{:S(2)}, u32[]{:S(2)}) collective-permute-start(bf16[528,128]{1,0:T(8,128)(2,1)S(1)} %column.1.refs_0_), channel_id=1, source_target_pairs={{0,2},{1,17},{2,0},{3,19},{4,6},{5,21},{6,4},{7,23},{8,10},{9,25},... | collective-permute-start | bytes 405512 | tf_op jit(solution)/shard_map/ppermute | solution.py:310
  18.1 5.0 %collective-permute-start.5 = (bf16[528,128]{1,0:T(8,128)(2,1)S(1)}, bf16[528,128]{1,0:T(8,128)(2,1)S(1)}, u32[]{:S(2)}, u32[]{:S(2)}) collective-permute-start(bf16[528,128]{1,0:T(8,128)(2,1)S(1)} %column.1.refs_0_), channel_id=1, source_target_pairs={{0,4},{1,9},{2,6},{3,11},{4,0},{5,13},{6,2},{7,15},{8,12},{9,1},{1... | collective-permute-start | bytes 405512 | tf_op jit(solution)/shard_map/ppermute | solution.py:310
  24.4 5.9 %collective-permute-start.8 = (bf16[64,1024]{1,0:T(8,128)(2,1)S(1)}, bf16[64,1024]{1,0:T(8,128)(2,1)S(1)}, u32[]{:S(2)}, u32[]{:S(2)}) collective-permute-start(bf16[64,1024]{1,0:T(8,128)(2,1)S(1)} %get-tuple-element.16), channel_id=1, source_target_pairs={{0,6},{1,25},{2,4},{3,27},{4,2},{5,29},{6,0},{7,31},{8,14},{9,17},... | collective-permute-start | bytes 393224 | tf_op jit(solution)/shard_map/ppermute | solution.py:310
  26.7 5.0 %collective-permute-start.9 = (bf16[64,1024]{1,0:T(8,128)(2,1)S(1)}, bf16[64,1024]{1,0:T(8,128)(2,1)S(1)}, u32[]{:S(2)}, u32[]{:S(2)}) collective-permute-start(bf16[64,1024]{1,0:T(8,128)(2,1)S(1)} %get-tuple-element.17), channel_id=1, source_target_pairs={{0,2},{1,17},{2,0},{3,19},{4,6},{5,21},{6,4},{7,23},{8,10},{9,25},... | collective-permute-start | bytes 393224 | tf_op jit(solution)/shard_map/ppermute | solution.py:310
  26.8 5.0 %collective-permute-start.10 = (bf16[64,1024]{1,0:T(8,128)(2,1)S(1)}, bf16[64,1024]{1,0:T(8,128)(2,1)S(1)}, u32[]{:S(2)}, u32[]{:S(2)}) collective-permute-start(bf16[64,1024]{1,0:T(8,128)(2,1)S(1)} %get-tuple-element.18), channel_id=1, source_target_pairs={{0,4},{1,9},{2,6},{3,11},{4,0},{5,13},{6,2},{7,15},{8,12},{9,1},{1... | collective-permute-start | bytes 393224 | tf_op jit(solution)/shard_map/ppermute | solution.py:310
  31.9 5.8 %collective-permute-start.11 = (bf16[16,1024]{1,0:T(8,128)(2,1)S(1)}, bf16[16,1024]{1,0:T(8,128)(2,1)S(1)}, u32[]{:S(2)}, u32[]{:S(2)}) collective-permute-start(bf16[16,1024]{1,0:T(8,128)(2,1)S(1)} %get-tuple-element.20), channel_id=1, source_target_pairs={{0,24},{1,7},{2,26},{3,5},{4,28},{5,3},{6,30},{7,1},{8,16},{9,15},... | collective-permute-start | bytes 98312 | tf_op jit(solution)/shard_map/ppermute | solution.py:310
  33.4 4.8 %collective-permute-start.12 = (bf16[16,1024]{1,0:T(8,128)(2,1)S(1)}, bf16[16,1024]{1,0:T(8,128)(2,1)S(1)}, u32[]{:S(2)}, u32[]{:S(2)}) collective-permute-start(bf16[16,1024]{1,0:T(8,128)(2,1)S(1)} %get-tuple-element.21), channel_id=1, source_target_pairs={{0,16},{1,5},{2,18},{3,7},{4,20},{5,1},{6,22},{7,3},{8,24},{9,13},... | collective-permute-start | bytes 98312 | tf_op jit(solution)/shard_map/ppermute | solution.py:310
  34.0 4.5 %collective-permute-start.13 = (bf16[16,1024]{1,0:T(8,128)(2,1)S(1)}, bf16[16,1024]{1,0:T(8,128)(2,1)S(1)}, u32[]{:S(2)}, u32[]{:S(2)}) collective-permute-start(bf16[16,1024]{1,0:T(8,128)(2,1)S(1)} %get-tuple-element.22), channel_id=1, source_target_pairs={{0,8},{1,3},{2,10},{3,1},{4,12},{5,7},{6,14},{7,5},{8,0},{9,11},{1... | collective-permute-start | bytes 98312 | tf_op jit(solution)/shard_map/ppermute | solution.py:310

commit v10 on v9

--- a/solution.py
+++ b/solution.py
@@ -377,7 +377,7 @@
             pltpu.VMEM((key_heads, 8 * row_count, key_size), f32),
             pltpu.VMEM((key_heads, share, 8 * row_count, value_size), f32),
             pltpu.SemaphoreType.DMA((12,)),
-            pltpu.SemaphoreType.DMA((key_heads // 2,)),
+            pltpu.SemaphoreType.DMA((key_heads // 4,)),
             pltpu.SemaphoreType.DMA((chunks,)),
         ],
         compiler_params=params,

time: 39.4 us -> 39.3 us (level)
  no operation moved by 1% of the time
where the time goes in v10:
time: 39.3 us; the launch traced here: 39.1 us
  starting transfers between devices  17.8 us (45%)
  waiting for transfers between devices  13.9 us (35%)
  Pallas kernels  7.33 us (19%)
    ppermute x14, starting transfers between devices, hop(): return lax.ppermute(x, 'dp', [(i, i ^ masks[i % 2]) for i in range(count)])  17.8 us
    ppermute x14, waiting for transfers between devices, hop(): return lax.ppermute(x, 'dp', [(i, i ^ masks[i % 2]) for i in range(count)])  13.9 us
    pallas_call x1, Pallas kernels, shards(): pl.pallas_call(mixer_kernel, out_shape=(jax.ShapeDtypeStruct((token_count...  4.35 us
    pallas_call x5, Pallas kernels, local(): pl.pallas_call(body, out_shape=tuple((jax.ShapeDtypeStruct(*o) for o in o...  2.98 us
  transfers between devices with their start and end apart: 14, of which 11 were waited for; matrix products, arithmetic and copies ran while one was open for 0% of the time, Pallas kernels for 14%

profile of v10, /device:TPU:0, one launch (start us, length us, event | category | flops | bytes accessed | tf_op | source)
XLA Modules:
  0.0 39.1 jit_solution(5179639496844061711)
XLA Ops:
  0.0 0.0 copy-start
  0.0 0.0 copy-start.1
  0.0 0.0 copy-start.2
  0.0 0.5 %collective-permute-start.3 = (bf16[1,1024,512]{2,1,0:T(8,128)(2,1)}, bf16[1,1024,512]{2,1,0:T(8,128)(2,1)S(1)}, u32[]{:S(2)}, u32[]{:S(2)}) collective-permute-start(bf16[1,1024,512]{2,1,0:T(8,128)(2,1)} %refs_4_.1), channel_id=1, source_target_pairs={{0,1},{1,0},{2,3},{3,2},{4,5},{5,4},{6,7},{7,6},{8,9},{9,8},{10,11... | collective-permute-start | bytes 3145736 | tf_op jit(solution)/shard_map/ppermute | solution.py:310
  0.5 0.1 collective-permute-start.4
  0.6 4.4 %mixer.1 = (bf16[16,1152]{1,0:T(8,128)(2,1)S(1)}, bf16[16,1024]{1,0:T(8,128)(2,1)S(1)}) custom-call(bf16[8,2,1024]{2,1,0:T(2,128)(2,1)} %hidden_hbm.1, bf16[8,2,1024]{2,1,0:T(2,128)(2,1)} %query_hbm.1, bf16[8,2,1024]{2,1,0:T(2,128)(2,1)} %key_hbm.1, bf16[8,2,2048]{2,1,0:T(2,128)(2,1)} %value_hbm.1, bf16[8,2,2048]{2,1,0:T(2,128)(2,1)} %gate_hbm.1, ...), custom_call_target="tpu_custom_call" | custom-call | tf_op jit(solution)/shard_map/mixer/pallas_call | solution.py:365
  5.0 5.1 %collective-permute-start.2 = (bf16[16,1152]{1,0:T(8,128)(2,1)S(1)}, bf16[16,1152]{1,0:T(8,128)(2,1)S(1)}, u32[]{:S(2)}, u32[]{:S(2)}) collective-permute-start(bf16[16,1152]{1,0:T(8,128)(2,1)S(1)} %get-tuple-element.15.refs_0_), channel_id=1, source_target_pairs={{0,24},{1,7},{2,26},{3,5},{4,28},{5,3},{6,30},{7,1},{8,16},{9,15},... | collective-permute-start | bytes 110600 | tf_op jit(solution)/shard_map/ppermute | solution.py:310
  10.1 0.0 collective-permute-start.1
  10.1 0.6 %collective-permute-start = (bf16[16,1152]{1,0:T(8,128)(2,1)S(1)}, bf16[16,1152]{1,0:T(8,128)(2,1)S(1)}, u32[]{:S(2)}, u32[]{:S(2)}) collective-permute-start(bf16[16,1152]{1,0:T(8,128)(2,1)S(1)} %get-tuple-element.15.refs_0_), channel_id=1, source_target_pairs={{0,8},{1,3},{2,10},{3,1},{4,12},{5,7},{6,14},{7,5},{8,0},{9,11},{1... | collective-permute-start | bytes 110600 | tf_op jit(solution)/shard_map/ppermute | solution.py:310
  10.7 1.3 %collective-permute-done.2.refs_3_ = bf16[16,1152]{1,0:T(8,128)(2,1)S(1)} collective-permute-done((bf16[16,1152]{1,0:T(8,128)(2,1)S(1)}, bf16[16,1152]{1,0:T(8,128)(2,1)S(1)}, u32[]{:S(2)}, u32[]{:S(2)}) %collective-permute-start.2) | collective-permute-done | bytes 36896 | tf_op jit(solution)/shard_map/ppermute | solution.py:310
  12.0 2.9 %collective-permute-done.1.refs_2_ = bf16[16,1152]{1,0:T(8,128)(2,1)S(1)} collective-permute-done((bf16[16,1152]{1,0:T(8,128)(2,1)S(1)}, bf16[16,1152]{1,0:T(8,128)(2,1)S(1)}, u32[]{:S(2)}, u32[]{:S(2)}) %collective-permute-start.1) | collective-permute-done | bytes 36896 | tf_op jit(solution)/shard_map/ppermute | solution.py:310
  14.9 0.0 collective-permute-done.refs_1_
  14.9 0.1 column.1.refs_0_
  15.0 2.9 %collective-permute-start.7 = (bf16[528,128]{1,0:T(8,128)(2,1)S(1)}, bf16[528,128]{1,0:T(8,128)(2,1)S(1)}, u32[]{:S(2)}, u32[]{:S(2)}) collective-permute-start(bf16[528,128]{1,0:T(8,128)(2,1)S(1)} %column.1.refs_0_), channel_id=1, source_target_pairs={{0,6},{1,25},{2,4},{3,27},{4,2},{5,29},{6,0},{7,31},{8,14},{9,17},... | collective-permute-start | bytes 405512 | tf_op jit(solution)/shard_map/ppermute | solution.py:310
  17.9 0.1 collective-permute-start.6
  18.0 0.5 %collective-permute-start.5 = (bf16[528,128]{1,0:T(8,128)(2,1)S(1)}, bf16[528,128]{1,0:T(8,128)(2,1)S(1)}, u32[]{:S(2)}, u32[]{:S(2)}) collective-permute-start(bf16[528,128]{1,0:T(8,128)(2,1)S(1)} %column.1.refs_0_), channel_id=1, source_target_pairs={{0,4},{1,9},{2,6},{3,11},{4,0},{5,13},{6,2},{7,15},{8,12},{9,1},{1... | collective-permute-start | bytes 405512 | tf_op jit(solution)/shard_map/ppermute | solution.py:310
  18.5 2.4 %collective-permute-done.7.refs_2_ = bf16[528,128]{1,0:T(8,128)(2,1)S(1)} collective-permute-done((bf16[528,128]{1,0:T(8,128)(2,1)S(1)}, bf16[528,128]{1,0:T(8,128)(2,1)S(1)}, u32[]{:S(2)}, u32[]{:S(2)}) %collective-permute-start.7) | collective-permute-done | bytes 135200 | tf_op jit(solution)/shard_map/ppermute | solution.py:310
  20.9 1.9 %collective-permute-done.6.refs_1_ = bf16[528,128]{1,0:T(8,128)(2,1)S(1)} collective-permute-done((bf16[528,128]{1,0:T(8,128)(2,1)S(1)}, bf16[528,128]{1,0:T(8,128)(2,1)S(1)}, u32[]{:S(2)}, u32[]{:S(2)}) %collective-permute-start.6) | collective-permute-done | bytes 135200 | tf_op jit(solution)/shard_map/ppermute | solution.py:310
  22.9 0.1 collective-permute-done.5.refs_0_
  23.0 0.0 collective-permute-done.4.refs_5_.refs_7_
  23.0 0.0 collective-permute-done.3.refs_4_.refs_6_
  23.0 0.0 copy-done
  23.0 0.0 copy-done.1
  23.0 0.0 copy-done.2
  23.0 1.3 %experts.1 = (bf16[64,1024]{1,0:T(8,128)(2,1)S(1)}, bf16[64,1024]{1,0:T(8,128)(2,1)S(1)}, bf16[64,1024]{1,0:T(8,128)(2,1)S(1)}) custom-call(bf16[528,128]{1,0:T(8,128)(2,1)S(1)} %collective-permute-done.5.refs_0_, bf16[528,128]{1,0:T(8,128)(2,1)S(1)} %collective-permute-done.6.refs_1_, bf16[528,128]{1,0:T(8,128)(2,1)S(1)} %collective-permute-done.7.refs_2_, ...), custom_call_target="tpu_custom_call" | custom-call | tf_op jit(solution)/shard_map/experts/pallas_call | solution.py:388
  24.3 2.3 %collective-permute-start.8 = (bf16[64,1024]{1,0:T(8,128)(2,1)S(1)}, bf16[64,1024]{1,0:T(8,128)(2,1)S(1)}, u32[]{:S(2)}, u32[]{:S(2)}) collective-permute-start(bf16[64,1024]{1,0:T(8,128)(2,1)S(1)} %get-tuple-element.16), channel_id=1, source_target_pairs={{0,6},{1,25},{2,4},{3,27},{4,2},{5,29},{6,0},{7,31},{8,14},{9,17},... | collective-permute-start | bytes 393224 | tf_op jit(solution)/shard_map/ppermute | solution.py:310
  26.6 0.1 collective-permute-start.9
  26.7 1.1 %collective-permute-start.10 = (bf16[64,1024]{1,0:T(8,128)(2,1)S(1)}, bf16[64,1024]{1,0:T(8,128)(2,1)S(1)}, u32[]{:S(2)}, u32[]{:S(2)}) collective-permute-start(bf16[64,1024]{1,0:T(8,128)(2,1)S(1)} %get-tuple-element.18), channel_id=1, source_target_pairs={{0,4},{1,9},{2,6},{3,11},{4,0},{5,13},{6,2},{7,15},{8,12},{9,1},{1... | collective-permute-start | bytes 393224 | tf_op jit(solution)/shard_map/ppermute | solution.py:310
  27.9 0.9 %own_experts.1.refs_0_ = f32[64,1024]{1,0:T(8,128)S(1)} custom-call(bf16[528,128]{1,0:T(8,128)(2,1)S(1)} %column.1.refs_0_, bf16[32,1024]{1,0:T(8,128)(2,1)S(1)} %bitcast.2, bf16[1,1024,512]{2,1,0:T(8,128)(2,1)S(1)} %copy-done, bf16[1,256,1024]{2,1,0:T(8,128)(2,1)S(1)} %copy-done.1, bf16[1,1024,512]{2,1,0:T(8,128)(2,1)S(1)} %collective-permute-done.3.refs_4_.refs_6_, ...), custom_call_target="tpu_custom_call" | custom-call | tf_op jit(solution)/shard_map/own_experts/pallas_call | solution.py:388
  28.8 1.5 %collective-permute-done.8.refs_1_ = bf16[64,1024]{1,0:T(8,128)(2,1)S(1)} collective-permute-done((bf16[64,1024]{1,0:T(8,128)(2,1)S(1)}, bf16[64,1024]{1,0:T(8,128)(2,1)S(1)}, u32[]{:S(2)}, u32[]{:S(2)}) %collective-permute-start.8) | collective-permute-done | bytes 131104 | tf_op jit(solution)/shard_map/ppermute | solution.py:310
  30.3 1.3 %collective-permute-done.9.refs_2_ = bf16[64,1024]{1,0:T(8,128)(2,1)S(1)} collective-permute-done((bf16[64,1024]{1,0:T(8,128)(2,1)S(1)}, bf16[64,1024]{1,0:T(8,128)(2,1)S(1)}, u32[]{:S(2)}, u32[]{:S(2)}) %collective-permute-start.9) | collective-permute-done | bytes 131104 | tf_op jit(solution)/shard_map/ppermute | solution.py:310
  31.6 0.1 collective-permute-done.10.refs_3_
  31.7 0.1 column_sum.1
  31.8 1.5 %collective-permute-start.11 = (bf16[16,1024]{1,0:T(8,128)(2,1)S(1)}, bf16[16,1024]{1,0:T(8,128)(2,1)S(1)}, u32[]{:S(2)}, u32[]{:S(2)}) collective-permute-start(bf16[16,1024]{1,0:T(8,128)(2,1)S(1)} %get-tuple-element.20), channel_id=1, source_target_pairs={{0,24},{1,7},{2,26},{3,5},{4,28},{5,3},{6,30},{7,1},{8,16},{9,15},... | collective-permute-start | bytes 98312 | tf_op jit(solution)/shard_map/ppermute | solution.py:310
  33.3 0.6 %collective-permute-start.12 = (bf16[16,1024]{1,0:T(8,128)(2,1)S(1)}, bf16[16,1024]{1,0:T(8,128)(2,1)S(1)}, u32[]{:S(2)}, u32[]{:S(2)}) collective-permute-start(bf16[16,1024]{1,0:T(8,128)(2,1)S(1)} %get-tuple-element.21), channel_id=1, source_target_pairs={{0,16},{1,5},{2,18},{3,7},{4,20},{5,1},{6,22},{7,3},{8,24},{9,13},... | collective-permute-start | bytes 98312 | tf_op jit(solution)/shard_map/ppermute | solution.py:310
  33.9 2.3 %collective-permute-start.13 = (bf16[16,1024]{1,0:T(8,128)(2,1)S(1)}, bf16[16,1024]{1,0:T(8,128)(2,1)S(1)}, u32[]{:S(2)}, u32[]{:S(2)}) collective-permute-start(bf16[16,1024]{1,0:T(8,128)(2,1)S(1)} %get-tuple-element.22), channel_id=1, source_target_pairs={{0,8},{1,3},{2,10},{3,1},{4,12},{5,7},{6,14},{7,5},{8,0},{9,11},{1... | collective-permute-start | bytes 98312 | tf_op jit(solution)/shard_map/ppermute | solution.py:310
  36.2 1.3 %collective-permute-done.11.refs_2_ = bf16[16,1024]{1,0:T(8,128)(2,1)S(1)} collective-permute-done((bf16[16,1024]{1,0:T(8,128)(2,1)S(1)}, bf16[16,1024]{1,0:T(8,128)(2,1)S(1)}, u32[]{:S(2)}, u32[]{:S(2)}) %collective-permute-start.11) | collective-permute-done | bytes 32800 | tf_op jit(solution)/shard_map/ppermute | solution.py:310
  37.6 0.6 %collective-permute-done.12.refs_3_ = bf16[16,1024]{1,0:T(8,128)(2,1)S(1)} collective-permute-done((bf16[16,1024]{1,0:T(8,128)(2,1)S(1)}, bf16[16,1024]{1,0:T(8,128)(2,1)S(1)}, u32[]{:S(2)}, u32[]{:S(2)}) %collective-permute-start.12) | collective-permute-done | bytes 32800 | tf_op jit(solution)/shard_map/ppermute | solution.py:310
  38.1 0.3 collective-permute-done.13.refs_4_
  38.5 0.7 %final.1 = bf16[8,2,1024]{2,1,0:T(2,128)(2,1)} custom-call(bf16[16,1024]{1,0:T(8,128)(2,1)S(1)} %get-tuple-element.14.refs_0_, f32[16,1024]{1,0:T(8,128)S(1)} %get-tuple-element.19.refs_1_, bf16[16,1024]{1,0:T(8,128)(2,1)S(1)} %collective-permute-done.11.refs_2_, bf16[16,1024]{1,0:T(8,128)(2,1)S(1)} %collective-permute-done.12.refs_3_, ...), custom_call_target="tpu_custom_call" | custom-call | tf_op jit(solution)/shard_map/final/pallas_call | solution.py:388
Async XLA Ops:
  0.0 23.0 %copy-start = (bf16[1,1024,512]{2,1,0:T(8,128)(2,1)S(1)}, bf16[1,1024,512]{2,1,0:T(8,128)(2,1)}, u32[]{:S(2)}) copy-start(bf16[1,1024,512]{2,1,0:T(8,128)(2,1)} %refs_4_.1) | copy-start | bytes 3145732
  0.0 23.0 %copy-start.1 = (bf16[1,256,1024]{2,1,0:T(8,128)(2,1)S(1)}, bf16[1,256,1024]{2,1,0:T(8,128)(2,1)}, u32[]{:S(2)}) copy-start(bf16[1,256,1024]{2,1,0:T(8,128)(2,1)} %refs_5_.1) | copy-start | bytes 1572868
  0.0 23.0 %copy-start.2 = (bf16[1024,32]{0,1:T(8,128)(2,1)S(1)}, bf16[1024,32]{0,1:T(8,128)(2,1)}, u32[]{:S(2)}) copy-start(bf16[1024,32]{0,1:T(8,128)(2,1)} %param.30) | copy-start | bytes 196612
  0.0 23.0 %collective-permute-start.3 = (bf16[1,1024,512]{2,1,0:T(8,128)(2,1)}, bf16[1,1024,512]{2,1,0:T(8,128)(2,1)S(1)}, u32[]{:S(2)}, u32[]{:S(2)}) collective-permute-start(bf16[1,1024,512]{2,1,0:T(8,128)(2,1)} %refs_4_.1), channel_id=1, source_target_pairs={{0,1},{1,0},{2,3},{3,2},{4,5},{5,4},{6,7},{7,6},{8,9},{9,8},{10,11... | collective-permute-start | bytes 3145736 | tf_op jit(solution)/shard_map/ppermute | solution.py:310
  0.5 22.5 %collective-permute-start.4 = (bf16[1,256,1024]{2,1,0:T(8,128)(2,1)}, bf16[1,256,1024]{2,1,0:T(8,128)(2,1)S(1)}, u32[]{:S(2)}, u32[]{:S(2)}) collective-permute-start(bf16[1,256,1024]{2,1,0:T(8,128)(2,1)} %refs_5_.1), channel_id=1, source_target_pairs={{0,1},{1,0},{2,3},{3,2},{4,5},{5,4},{6,7},{7,6},{8,9},{9,8},{10,11... | collective-permute-start | bytes 1572872 | tf_op jit(solution)/shard_map/ppermute | solution.py:310
  5.0 7.0 %collective-permute-start.2 = (bf16[16,1152]{1,0:T(8,128)(2,1)S(1)}, bf16[16,1152]{1,0:T(8,128)(2,1)S(1)}, u32[]{:S(2)}, u32[]{:S(2)}) collective-permute-start(bf16[16,1152]{1,0:T(8,128)(2,1)S(1)} %get-tuple-element.15.refs_0_), channel_id=1, source_target_pairs={{0,24},{1,7},{2,26},{3,5},{4,28},{5,3},{6,30},{7,1},{8,16},{9,15},... | collective-permute-start | bytes 110600 | tf_op jit(solution)/shard_map/ppermute | solution.py:310
  10.1 4.9 %collective-permute-start.1 = (bf16[16,1152]{1,0:T(8,128)(2,1)S(1)}, bf16[16,1152]{1,0:T(8,128)(2,1)S(1)}, u32[]{:S(2)}, u32[]{:S(2)}) collective-permute-start(bf16[16,1152]{1,0:T(8,128)(2,1)S(1)} %get-tuple-element.15.refs_0_), channel_id=1, source_target_pairs={{0,16},{1,5},{2,18},{3,7},{4,20},{5,1},{6,22},{7,3},{8,24},{9,13},... | collective-permute-start | bytes 110600 | tf_op jit(solution)/shard_map/ppermute | solution.py:310
  10.1 4.9 %collective-permute-start = (bf16[16,1152]{1,0:T(8,128)(2,1)S(1)}, bf16[16,1152]{1,0:T(8,128)(2,1)S(1)}, u32[]{:S(2)}, u32[]{:S(2)}) collective-permute-start(bf16[16,1152]{1,0:T(8,128)(2,1)S(1)} %get-tuple-element.15.refs_0_), channel_id=1, source_target_pairs={{0,8},{1,3},{2,10},{3,1},{4,12},{5,7},{6,14},{7,5},{8,0},{9,11},{1... | collective-permute-start | bytes 110600 | tf_op jit(solution)/shard_map/ppermute | solution.py:310
  15.0 5.9 %collective-permute-start.7 = (bf16[528,128]{1,0:T(8,128)(2,1)S(1)}, bf16[528,128]{1,0:T(8,128)(2,1)S(1)}, u32[]{:S(2)}, u32[]{:S(2)}) collective-permute-start(bf16[528,128]{1,0:T(8,128)(2,1)S(1)} %column.1.refs_0_), channel_id=1, source_target_pairs={{0,6},{1,25},{2,4},{3,27},{4,2},{5,29},{6,0},{7,31},{8,14},{9,17},... | collective-permute-start | bytes 405512 | tf_op jit(solution)/shard_map/ppermute | solution.py:310
  17.9 5.0 %collective-permute-start.6 = (bf16[528,128]{1,0:T(8,128)(2,1)S(1)}, bf16[528,128]{1,0:T(8,128)(2,1)S(1)}, u32[]{:S(2)}, u32[]{:S(2)}) collective-permute-start(bf16[528,128]{1,0:T(8,128)(2,1)S(1)} %column.1.refs_0_), channel_id=1, source_target_pairs={{0,2},{1,17},{2,0},{3,19},{4,6},{5,21},{6,4},{7,23},{8,10},{9,25},... | collective-permute-start | bytes 405512 | tf_op jit(solution)/shard_map/ppermute | solution.py:310
  18.0 5.0 %collective-permute-start.5 = (bf16[528,128]{1,0:T(8,128)(2,1)S(1)}, bf16[528,128]{1,0:T(8,128)(2,1)S(1)}, u32[]{:S(2)}, u32[]{:S(2)}) collective-permute-start(bf16[528,128]{1,0:T(8,128)(2,1)S(1)} %column.1.refs_0_), channel_id=1, source_target_pairs={{0,4},{1,9},{2,6},{3,11},{4,0},{5,13},{6,2},{7,15},{8,12},{9,1},{1... | collective-permute-start | bytes 405512 | tf_op jit(solution)/shard_map/ppermute | solution.py:310
  24.3 5.9 %collective-permute-start.8 = (bf16[64,1024]{1,0:T(8,128)(2,1)S(1)}, bf16[64,1024]{1,0:T(8,128)(2,1)S(1)}, u32[]{:S(2)}, u32[]{:S(2)}) collective-permute-start(bf16[64,1024]{1,0:T(8,128)(2,1)S(1)} %get-tuple-element.16), channel_id=1, source_target_pairs={{0,6},{1,25},{2,4},{3,27},{4,2},{5,29},{6,0},{7,31},{8,14},{9,17},... | collective-permute-start | bytes 393224 | tf_op jit(solution)/shard_map/ppermute | solution.py:310
  26.6 5.0 %collective-permute-start.9 = (bf16[64,1024]{1,0:T(8,128)(2,1)S(1)}, bf16[64,1024]{1,0:T(8,128)(2,1)S(1)}, u32[]{:S(2)}, u32[]{:S(2)}) collective-permute-start(bf16[64,1024]{1,0:T(8,128)(2,1)S(1)} %get-tuple-element.17), channel_id=1, source_target_pairs={{0,2},{1,17},{2,0},{3,19},{4,6},{5,21},{6,4},{7,23},{8,10},{9,25},... | collective-permute-start | bytes 393224 | tf_op jit(solution)/shard_map/ppermute | solution.py:310
  26.7 5.0 %collective-permute-start.10 = (bf16[64,1024]{1,0:T(8,128)(2,1)S(1)}, bf16[64,1024]{1,0:T(8,128)(2,1)S(1)}, u32[]{:S(2)}, u32[]{:S(2)}) collective-permute-start(bf16[64,1024]{1,0:T(8,128)(2,1)S(1)} %get-tuple-element.18), channel_id=1, source_target_pairs={{0,4},{1,9},{2,6},{3,11},{4,0},{5,13},{6,2},{7,15},{8,12},{9,1},{1... | collective-permute-start | bytes 393224 | tf_op jit(solution)/shard_map/ppermute | solution.py:310
  31.8 5.8 %collective-permute-start.11 = (bf16[16,1024]{1,0:T(8,128)(2,1)S(1)}, bf16[16,1024]{1,0:T(8,128)(2,1)S(1)}, u32[]{:S(2)}, u32[]{:S(2)}) collective-permute-start(bf16[16,1024]{1,0:T(8,128)(2,1)S(1)} %get-tuple-element.20), channel_id=1, source_target_pairs={{0,24},{1,7},{2,26},{3,5},{4,28},{5,3},{6,30},{7,1},{8,16},{9,15},... | collective-permute-start | bytes 98312 | tf_op jit(solution)/shard_map/ppermute | solution.py:310
  33.3 4.8 %collective-permute-start.12 = (bf16[16,1024]{1,0:T(8,128)(2,1)S(1)}, bf16[16,1024]{1,0:T(8,128)(2,1)S(1)}, u32[]{:S(2)}, u32[]{:S(2)}) collective-permute-start(bf16[16,1024]{1,0:T(8,128)(2,1)S(1)} %get-tuple-element.21), channel_id=1, source_target_pairs={{0,16},{1,5},{2,18},{3,7},{4,20},{5,1},{6,22},{7,3},{8,24},{9,13},... | collective-permute-start | bytes 98312 | tf_op jit(solution)/shard_map/ppermute | solution.py:310
  33.9 4.5 %collective-permute-start.13 = (bf16[16,1024]{1,0:T(8,128)(2,1)S(1)}, bf16[16,1024]{1,0:T(8,128)(2,1)S(1)}, u32[]{:S(2)}, u32[]{:S(2)}) collective-permute-start(bf16[16,1024]{1,0:T(8,128)(2,1)S(1)} %get-tuple-element.22), channel_id=1, source_target_pairs={{0,8},{1,3},{2,10},{3,1},{4,12},{5,7},{6,14},{7,5},{8,0},{9,11},{1... | collective-permute-start | bytes 98312 | tf_op jit(solution)/shard_map/ppermute | solution.py:310
